TPU v7x, 256 devices: a whole 4x4x8 slice. The times are simulated.
256 devices in a mesh: tm: 4 (over z_lo, core), cam: 64 (over y, x, z_hi).
Axes of the slice: x: 4, y: 4, z: 8 (z_hi: 4, z_lo: 2; z = z_hi * 2 + z_lo), core: 2. Of those that a mesh axis runs over, the one named last changes fastest.
Arguments:
- queries: bfloat16 [8, 64, 128, 1024], P('tm', 'cam'), may hold values from -170 to 170
- key_vectors: bfloat16 [8, 64, 128, 1024], P('tm', 'cam'), may hold values from -6 to 6
- value_vectors: bfloat16 [8, 64, 128, 1024], P('tm', 'cam'), may hold values from -6 to 6
- w_out: bfloat16 [1024, 1024], replicated, may hold values from -0.1875 to 0.1875
- rig_tiles: int32 [64, 7], replicated, may hold values from 0 to 63, as said below
- rig_count: int32 [64], replicated, may hold values from 1 to 7, as said below
- strip_rows: int32 [64, 16], replicated, may hold values from 0 to 127, as said below
- cotangent: bfloat16 [8, 64, 128, 1024], P('tm', 'cam'), may hold values from -6 to 6
Outputs:
- mixed: bfloat16 [8, 64, 128, 1024], P('tm', 'cam')
- grad_queries: bfloat16 [8, 64, 128, 1024], P('tm', 'cam')
- grad_keys: bfloat16 [8, 64, 128, 1024], P('tm', 'cam')
- grad_values: bfloat16 [8, 64, 128, 1024], P('tm', 'cam')
- grad_w_out: float32 [1024, 1024], P(('tm', 'cam'))
Inputs may be any that keep to these rules, and one draw needn't show every extreme that they name: `rig_tiles`: row c names 7 different camera-tiles, none of them c. `rig_count`: some camera-tile uses all 7 slots. `strip_rows`: each row holds 16 different token indices.
All inputs are finite; a program needn't handle non-finite values.
Results may differ from a plain program's by a relative error of at most 0.03.
Values may be sent and summed in bfloat16 or wider, within the bound.
No kernel may reach another device: no remote copies, remote signals or barrier semaphores. Data moves between devices by JAX's collectives and lax.ppermute only.
A program may use at most 192 MiB of HBM per device.

v0:
```python
import jax
import jax.numpy as jnp
from jax import lax
from jax.sharding import PartitionSpec as P

HEADS = 16


def shifted(block, axis, distance):
    devices = range(lax.axis_size(axis))
    route = [(i - distance, i) for i in devices if i - distance in devices]
    return lax.ppermute(block, axis, route)


def split_heads(tensor):
    return tensor.reshape(tensor.shape[:-1] + (HEADS, tensor.shape[-1] // HEADS))


def masked_scores(query_rows, ctx_keys, visible):
    score_scale = (query_rows.shape[-1] // HEADS) ** (-0.5)
    scores = (
        jnp.einsum(
            "bqhd,bkhd->bhqk",
            split_heads(query_rows),
            split_heads(ctx_keys),
            preferred_element_type=jnp.float32,
        )
        * score_scale
    )
    return jnp.where(visible[:, None, None, :], scores, -1e30)


def attend(query_rows, ctx_keys, ctx_vals, visible):
    scores = masked_scores(query_rows, ctx_keys, visible)
    row_max = jnp.max(scores, -1)
    expo = jnp.exp(scores - row_max[..., None])
    row_sum = jnp.sum(expo, -1)
    softmax_prob = expo / row_sum[..., None]
    weights = softmax_prob.astype(jnp.bfloat16)
    attended = jnp.einsum(
        "bhqk,bkhd->bqhd", weights, split_heads(ctx_vals), preferred_element_type=jnp.float32
    )
    return (attended.reshape(query_rows.shape).astype(jnp.bfloat16), row_max, row_sum)


def delta_of(attended, grad_attended):
    product = split_heads(attended).astype(jnp.float32) * split_heads(grad_attended).astype(
        jnp.float32
    )
    return jnp.swapaxes(jnp.sum(product, -1), 1, 2)


def attend_back(
    query_rows, ctx_keys, ctx_vals, visible, grad_attended, row_max, row_sum, row_delta
):
    score_scale = (query_rows.shape[-1] // HEADS) ** (-0.5)
    scores = masked_scores(query_rows, ctx_keys, visible)
    softmax_prob = jnp.exp(scores - row_max[..., None]) / row_sum[..., None]
    weights = softmax_prob.astype(jnp.bfloat16)
    grad_heads = split_heads(grad_attended)
    grad_prob = jnp.einsum(
        "bqhd,bkhd->bhqk", grad_heads, split_heads(ctx_vals), preferred_element_type=jnp.float32
    )
    grad_score = (softmax_prob * (grad_prob - row_delta[..., None]) * score_scale).astype(
        jnp.bfloat16
    )
    grad_q = jnp.einsum(
        "bhqk,bkhd->bqhd", grad_score, split_heads(ctx_keys), preferred_element_type=jnp.float32
    ).reshape(query_rows.shape)
    grad_k = jnp.einsum(
        "bhqk,bqhd->bkhd", grad_score, split_heads(query_rows), preferred_element_type=jnp.float32
    ).reshape(ctx_keys.shape)
    grad_v = jnp.einsum(
        "bhqk,bqhd->bkhd", weights, grad_heads, preferred_element_type=jnp.float32
    ).reshape(ctx_keys.shape)
    return (grad_q, grad_k, grad_v)


def on_device(
    queries, key_vectors, value_vectors, w_out, rig_tiles, rig_count, strip_rows, cotangent
):
    frames = queries.shape[0]
    tile_len = queries.shape[2]
    model_width = queries.shape[3]
    slot_count = rig_tiles.shape[1]
    strip_len = strip_rows.shape[1]
    cam_count = lax.axis_size("cam")
    device_cam = lax.axis_index("cam")
    time_index = lax.axis_index("tm")
    query_rows = queries[:, 0]
    key_value = jnp.concatenate([key_vectors[:, 0], value_vectors[:, 0]], -1)
    last_frame = shifted(key_value[-1], "tm", 1)
    before = jnp.concatenate([last_frame[None], key_value[:-1]], 0)
    own_rows = lax.dynamic_index_in_dim(strip_rows, device_cam, 0, keepdims=False)
    own_strip = jnp.take(key_value, own_rows, axis=1)
    everyone = lax.all_gather(own_strip[:, None], "cam", axis=1, tiled=True)
    my_rig = lax.dynamic_index_in_dim(rig_tiles, device_cam, 0, keepdims=False)
    my_count = lax.dynamic_index_in_dim(rig_count, device_cam, 0, keepdims=False)
    chosen = jnp.take(everyone, my_rig, axis=1).reshape(
        frames, slot_count * strip_len, 2 * model_width
    )
    context = jnp.concatenate([key_value, before, chosen], 1)
    global_frame = time_index * frames + jnp.arange(frames, dtype=jnp.int32)
    slot_visible = jnp.repeat(jnp.arange(slot_count, dtype=jnp.int32) < my_count, strip_len)
    visible = jnp.concatenate(
        [
            jnp.ones((frames, tile_len), bool),
            jnp.broadcast_to((global_frame > 0)[:, None], (frames, tile_len)),
            jnp.broadcast_to(slot_visible[None, :], (frames, slot_count * strip_len)),
        ],
        1,
    )
    ctx_keys = context[..., :model_width]
    ctx_vals = context[..., model_width:]
    attended, row_max, row_sum = attend(query_rows, ctx_keys, ctx_vals, visible)
    flat = attended.reshape(-1, model_width)
    mixed = jnp.dot(flat, w_out, preferred_element_type=jnp.float32).astype(jnp.bfloat16)
    mixed = mixed.reshape(frames, 1, tile_len, model_width)
    grad_flat = cotangent[:, 0].reshape(-1, model_width)
    grad_attended = lax.dot_general(
        grad_flat, w_out, (((1,), (1,)), ((), ())), preferred_element_type=jnp.float32
    )
    grad_attended = grad_attended.astype(jnp.bfloat16).reshape(frames, tile_len, model_width)
    weight_term = lax.dot_general(
        flat, grad_flat, (((0,), (0,)), ((), ())), preferred_element_type=jnp.float32
    )
    row_delta = delta_of(attended, grad_attended)
    grad_q, grad_k, grad_v = attend_back(
        query_rows, ctx_keys, ctx_vals, visible, grad_attended, row_max, row_sum, row_delta
    )
    grad_ctx = jnp.concatenate([grad_k, grad_v], -1)
    own_grad = grad_ctx[:, :tile_len]
    prev_grad = grad_ctx[:, tile_len : 2 * tile_len]
    strip_grad = grad_ctx[:, 2 * tile_len :].reshape(frames, slot_count, strip_len, 2 * model_width)
    own_grad = own_grad + jnp.concatenate([prev_grad[1:], jnp.zeros_like(prev_grad[:1])], 0)
    returned = shifted(prev_grad[0].astype(jnp.bfloat16), "tm", -1).astype(jnp.float32)
    own_grad = own_grad.at[-1].add(returned)
    pick_table = (my_rig[:, None] == jnp.arange(cam_count, dtype=jnp.int32)[None, :]).astype(
        jnp.float32
    )
    spread_grads = jnp.einsum(
        "jc,fjsx->fcsx", pick_table, strip_grad, precision=lax.Precision.HIGHEST
    )
    own_strip_grads = lax.psum_scatter(spread_grads, "cam", scatter_dimension=1, tiled=True)[:, 0]
    placement_table = (own_rows[:, None] == jnp.arange(tile_len, dtype=jnp.int32)[None, :]).astype(
        jnp.float32
    )
    own_grad = own_grad + jnp.einsum(
        "st,fsx->ftx", placement_table, own_strip_grads, precision=lax.Precision.HIGHEST
    )
    grad_queries = grad_q.astype(jnp.bfloat16)[:, None]
    grad_keys = own_grad[..., :model_width].astype(jnp.bfloat16)[:, None]
    grad_values = own_grad[..., model_width:].astype(jnp.bfloat16)[:, None]
    grad_w_out = lax.psum_scatter(weight_term, ("tm", "cam"), scatter_dimension=0, tiled=True)
    return (mixed, grad_queries, grad_keys, grad_values, grad_w_out)


def solution(mesh):
    return jax.shard_map(
        on_device,
        mesh=mesh,
        in_specs=(
            P("tm", "cam", None, None),
            P("tm", "cam", None, None),
            P("tm", "cam", None, None),
            P(),
            P(),
            P(),
            P(),
            P("tm", "cam", None, None),
        ),
        out_specs=(
            P("tm", "cam", None, None),
            P("tm", "cam", None, None),
            P("tm", "cam", None, None),
            P("tm", "cam", None, None),
            P(("tm", "cam"), None),
        ),
        check_vma=False,
    )
```

profile of v0, /device:TPU:32, one launch (start us, length us, event | category | flops | bytes accessed | tf_op | source)
XLA Modules:
  0.0 972.2 jit_solution(2724043239157752588)
XLA Ops:
  7.2 1.0 dynamic-slice_reduce_fusion
  8.3 2.3 copy_bitcast_fusion.1
  10.6 1.9 pad_maximum_fusion.2
  12.5 2.1 gather_fusion
  14.8 0.7 copy.76
  15.5 2.7 slice_maximum_fusion.1
  18.3 1.1 copy.111
  19.4 2.2 collective-permute-start
  23.4 2.0 copy.80
  25.4 2.6 convolution_convert_fusion.1
  28.0 2.5 reshape.201
  30.5 2.8 copy.83
  33.4 2.8 copy.75
  36.2 96.3 %all-gather.2.cloned.1.call-done = bf16[2,64,16,2048]{3,2,0,1:T(8,128)(2,1)} async-done(((bf16[2,1,16,2048]{3,2,0,1:T(8,128)(2,1)}), bf16[2,64,16,2048]{3,2,0,1:T(8,128)(2,1)}) %all-gather.2.cloned.1.call-update) | async-done | bytes 8388624 | tf_op jit(solution)/shard_map/all_gather | solution.py:96
  132.5 4.9 gather_fusion.1
  137.4 2.3 copy.77
  139.7 0.9 broadcast_select_fusion
  140.7 28.5 %pad_maximum_fusion = bf16[2,368,2048]{2,0,1:T(2,128)(2,1)S(1)} fusion(bf16[2,112,2048]{2,0,1:T(2,128)(2,1)S(1)} %broadcast_select_fusion, bf16[1,128,2048]{2,0,1:T(2,128)(2,1)S(1)} %copy-done.8, bf16[1,128,2048]{2,0,1:T(2,128)(2,1)S(1)} %copy-done.9, bf16[2,128,1024]{2,0,1:T(2,128)(2,1)S(1)} %get-tuple-element.52, ...), kind=kLoop, calls=%fused_computation.16 | loop fusion | flops 15073280 | bytes 6029312 | tf_op jit(solution)/shard_map/concatenate | solution.py:102
  169.2 3.4 fusion.38
  172.6 5.0 copy.79
  177.6 5.6 copy.78
  183.2 6.3 fusion.39
  189.5 3.2 fusion.10
  192.8 3.1 fusion.41
  195.9 0.8 multiply_reduce_fusion
  197.2 2.7 fusion.19
  200.0 4.8 multiply_convert_fusion
  204.8 1.3 fusion.40
  206.4 1.7 copy-done.3
  208.1 0.8 copy-done.1
  208.9 1.5 pad_maximum_fusion.1
  210.3 3.0 copy.86
  213.3 12.4 %convolution_bitcast_fusion = f32[2,64,16,2048]{3,1,2,0:T(8,128)S(1)} fusion(f32[2,7,16,2048]{3,2,1,0:T(8,128)} %bitcast.118, s32[7]{0:T(128)S(1)} %dynamic-slice_reduce_fusion.1), kind=kOutput, calls=%fused_computation.9 | convolution fusion | flops 352321984 | bytes 18612252 | tf_op jit(solution)/shard_map/jc,fjsx->fcsx/dot_general | solution.py:141
  225.8 19.2 %copy.88 = f32[2,64,16,2048]{3,2,0,1:T(8,128)} copy(f32[2,64,16,2048]{3,1,2,0:T(8,128)S(1)} %convolution_bitcast_fusion) | data formatting | bytes 33554432 | tf_op jit(solution)/shard_map/jc,fjsx->fcsx/transpose | solution.py:141
  245.0 3.1 convolution_convert_fusion
  248.1 1.0 copy.90
  249.1 1.4 fusion.22
  250.5 2.2 collective-permute-start.1
  252.8 1.5 fusion.12
  254.4 1.5 convolution_convert_fusion.2
  255.9 4.2 collective-permute-done.1
  260.1 2.3 fusion.18
  262.4 202.9 %all-reduce.4.cloned.1.call-done = f32[1024,1024]{1,0:T(8,128)} async-done(((f32[1024,1024]{1,0:T(8,128)}), f32[1024,1024]{1,0:T(8,128)}) %all-reduce.4.cloned.1.call-update) | async-done | bytes 4194320
  465.2 1.4 constant_dynamic-slice_fusion
  466.6 493.2 %reduce-scatter.2.cloned.1.call-done = f32[2,1,16,2048]{3,2,0,1:T(8,128)} async-done(((f32[2,64,16,2048]{3,2,0,1:T(8,128)}), f32[2,1,16,2048]{3,2,0,1:T(8,128)}) %reduce-scatter.2.cloned.1.call-update) | async-done | bytes 262160 | tf_op jit(solution)/shard_map/reduce_scatter | solution.py:144
  959.8 3.5 fusion.9
  963.4 1.0 copy.92
  964.4 1.0 copy.91
  (58 shorter events, 3.3 us)
Async XLA Ops:
  7.2 18.3 %copy-start = (bf16[1024,1024]{1,0:T(8,128)(2,1)S(1)}, bf16[1024,1024]{1,0:T(8,128)(2,1)}, u32[]{:S(2)}) copy-start(bf16[1024,1024]{1,0:T(8,128)(2,1)} %param.13) | copy-start | bytes 6291460
  7.2 125.3 %all-gather.2.cloned.1.call-start = ((), (), s32[]{:S(2)}) async-start(), calls=%async_computation.1 | async-start | bytes 8519680 | tf_op jit(solution)/shard_map/all_gather | solution.py:96
  12.5 9.1 copy-start.14
  12.5 9.7 copy-start.13
  15.5 449.8 %all-reduce.4.cloned.1.call-start = ((), (), s32[]{:S(2)}) async-start(), calls=%async_computation.3 | async-start | bytes 8388608
  19.4 14.0 %collective-permute-start = (bf16[128,2048]{1,0:T(8,128)(2,1)}, bf16[128,2048]{1,0:T(8,128)(2,1)}, u32[]{:S(2)}, u32[]{:S(2)}) collective-permute-start(bf16[128,2048]{1,0:T(8,128)(2,1)} %bitcast.109), channel_id=1, source_target_pairs={{0,64},{64,128},{128,192},{1,65},{65,129},{129,193},{2,66},{66,130... | collective-permute-start | bytes 1572872 | tf_op jit(solution)/shard_map/ppermute | solution.py:12
  137.4 3.2 copy-start.8
  137.4 3.2 copy-start.9
  172.6 10.6 %copy-start.10 = (bf16[2,1,128,1024]{2,3,0,1:T(8,128)(2,1)S(1)}, bf16[2,1,128,1024]{2,3,0,1:T(8,128)(2,1)}, u32[]{:S(2)}) copy-start(bf16[2,1,128,1024]{2,3,0,1:T(8,128)(2,1)} %copy.80) | copy-start | bytes 1572868
  189.5 3.3 copy-start.7
  192.8 3.1 copy-start.6
  195.9 1.4 copy-start.12
  199.9 759.9 %reduce-scatter.2.cloned.1.call-start = ((), (), s32[]{:S(2)}) async-start(), calls=%async_computation.2 | async-start | bytes 17039360 | tf_op jit(solution)/shard_map/reduce_scatter | solution.py:144
  200.0 4.8 copy-start.11
  204.8 1.6 copy-start.5
  204.8 4.1 copy-start.1
  206.4 1.7 copy-start.3
  249.1 3.6 copy-start.2
  249.1 3.6 copy-start.4
  250.5 9.6 collective-permute-start.1
Sparse Core Ops, SparseCore 0:
  15.6 116.8 all-gather.1
  200.0 265.1 all-reduce.3
  468.0 491.8 reduce-scatter.1
where the time goes:
time: 977 us; the launch traced here: 972 us
  waiting for transfers between devices  797 us (82%)
  local copies, waits for them, and re-layouts  69.6 us (7%)
  other arithmetic  45.1 us (5%)
  matrix products  42.1 us (4%)
  between operations  14.3 us (1%)
    reduce_scatter x1, waiting for transfers between devices, on_device(): lax.psum_scatter(spread_grads, 'cam', scatter_dimension=1, tiled=True)[:, 0]  493 us
    unnamed x4, waiting for transfers between devices  203 us
    all_gather x1, waiting for transfers between devices, on_device(): everyone = lax.all_gather(own_strip[:, None], 'cam', axis=1, tiled=True)  96.3 us
    concatenate x1, other arithmetic, on_device(): context = jnp.concatenate([key_value, before, chosen], 1)  28.5 us
  transfers between devices with their start and end apart: 5, of which 4 were waited for; matrix products, arithmetic and copies ran while one was open for 8% of the time, Pallas kernels for 0%

commit v1 on v0

v1 whole, which is shorter than its diff:
```python
import functools

import jax
import jax.numpy as jnp
from jax import lax
from jax.experimental import pallas as pl
from jax.experimental.pallas import tpu as pltpu
from jax.sharding import PartitionSpec as P

TILE = 128
D = 1024
PAIRS = 8
RING = 4
GRID = 16
SLOTS = 8
NEG = -1e30
BF = jnp.bfloat16
F32 = jnp.float32
MIB = 1 << 20

CORE, ZLO, TM, Q, CAM, COUNT = range(6)
ORDER = 8


def nt(a, b):
    return lax.dot_general(a, b, (((1,), (1,)), ((), ())), preferred_element_type=F32)


def tn(a, b):
    return lax.dot_general(a, b, (((0,), (0,)), ((), ())), preferred_element_type=F32)


def nn(a, b):
    return jnp.dot(a, b, preferred_element_type=F32)


def iota(shape, dim):
    return lax.broadcasted_iota(jnp.int32, shape, dim)


def call(body, grid, inputs, outputs, limit_mib, flops, nbytes, scalars=1):
    def spec(entry):
        shape, block, index = entry
        if block is None:
            zeros = (0,) * len(shape.shape)
            return pl.BlockSpec(shape.shape, lambda *_: zeros)
        return pl.BlockSpec(block, index)

    return pl.pallas_call(
        body,
        grid_spec=pltpu.PrefetchScalarGridSpec(
            num_scalar_prefetch=scalars,
            grid=grid,
            in_specs=[spec(e) for e in inputs[scalars:]],
            out_specs=[spec(e) for e in outputs],
        ),
        out_shape=[e[0] for e in outputs],
        compiler_params=pltpu.CompilerParams(vmem_limit_bytes=limit_mib * MIB),
        cost_estimate=pl.CostEstimate(flops=flops, bytes_accessed=nbytes, transcendentals=0),
    )(*[e[0] if isinstance(e, tuple) else e for e in inputs])


def like(shape, dtype=BF):
    return jax.ShapeDtypeStruct(shape, dtype)


def strip_target(info, strip_rows, shape, group):
    s = iota(shape, 0) // group
    target = jnp.zeros(shape, jnp.int32)
    for i in range(GRID):
        target = jnp.where(s == i, strip_rows[info[CAM], i], target)
    return target


def extract_body(info, strip_rows, k, v, out, last):
    shape = (GRID * 8, 2 * TILE)
    r, c = iota(shape, 0), iota(shape, 1)
    hit = (strip_target(info, strip_rows, shape, 8) == c % TILE) & ((r // 2) % 2 == c // TILE)
    total = jnp.zeros((GRID * 8, D // 2), F32)
    for part, ref in enumerate((k, v)):
        whole = ref[...].reshape(2 * TILE, D)
        for half in range(2):
            pick = hit & (r % 2 == part) & ((r // 4) % 2 == half)
            total += nn(pick.astype(F32).astype(BF), whole[:, half * 512 : half * 512 + 512])
        last[part] = ref[1]
    out[...] = total.astype(BF)


def stacked(block):
    first = iota(block.shape, 1) < 64
    zero = jnp.zeros_like(block)
    return jnp.concatenate([jnp.where(first, block, zero), jnp.where(first, zero, block)], 0)


def own_half(wide):
    return jnp.concatenate([wide[:64, :TILE], wide[64:, TILE:]], 0)


def spread(row):
    return jnp.concatenate(
        [jnp.broadcast_to(row[:, :TILE], (64, TILE)), jnp.broadcast_to(row[:, TILE:], (64, TILE))],
        0,
    )


def local_body(info, q, k, v, prev, cot, w, g_out, gt_out, m_out, l_out, o_out):
    cots = cot[...].reshape(2 * TILE, D)
    g_out[...] = nt(cots, w[...]).astype(BF).reshape(2, TILE, TILE)
    gt_out[...] = nt(w[...], cots).astype(BF)
    for f in range(2):
        qs = stacked(q[f] * jnp.asarray(0.125, BF))
        before_k, before_v = (prev[0], prev[1]) if f == 0 else (k[0], v[0])
        s1 = nt(k[f], qs)
        s2 = nt(before_k, qs)
        if f == 0:
            s2 = jnp.where(info[TM] > 0, s2, NEG)
        m = jnp.maximum(jnp.max(s1, 0, keepdims=True), jnp.max(s2, 0, keepdims=True))
        p1 = jnp.exp(s1 - m)
        p2 = jnp.exp(s2 - m)
        m_out[0, f] = m[0]
        l_out[0, f] = jnp.sum(p1, 0) + jnp.sum(p2, 0)
        o_out[0, f] = own_half(tn(v[f], p1.astype(BF)) + tn(before_v, p2.astype(BF)))


def strip_body(
    info, q, g, gt, strips, m1, l1, o1, cot,
    att, back, m_out, rl_out, delta_out, dq_out, w_send, w_keep,
):
    weight = jnp.zeros((TILE, D), F32)
    seen = iota((TILE, 2 * TILE), 0) % SLOTS < info[COUNT]
    for f in range(2):
        qs = stacked(q[f] * jnp.asarray(0.125, BF))
        gs = stacked(g[f])
        ks = strips[:, 2 * f].astype(F32).reshape(TILE, TILE).astype(BF)
        vs = strips[:, 2 * f + 1].astype(F32).reshape(TILE, TILE).astype(BF)
        s = jnp.where(seen, nt(ks, qs), NEG)
        m_old = m1[0, f : f + 1]
        m = jnp.maximum(m_old, jnp.max(s, 0, keepdims=True))
        p = jnp.exp(s - m)
        shrink = jnp.exp(m_old - m)
        rl = 1.0 / (l1[0, f : f + 1] * shrink + jnp.sum(p, 0, keepdims=True))
        p = p * rl
        pb = p.astype(BF)
        ot = (o1[0, f] * spread(shrink * rl) + own_half(tn(vs, pb))).astype(BF)
        prod = gt[:, f * TILE : f * TILE + TILE].astype(F32) * ot.astype(F32)
        delta = jnp.concatenate(
            [jnp.sum(prod[:64], 0, keepdims=True), jnp.sum(prod[64:], 0, keepdims=True)], 1
        )
        ds = (p * (nt(vs, gs) - delta)).astype(BF)
        back[:, 2 * f] = nn(ds, qs).reshape(GRID, SLOTS, TILE).astype(BF)
        back[:, 2 * f + 1] = nn(pb, gs).reshape(GRID, SLOTS, TILE).astype(BF)
        dq_out[0, f] = own_half(tn(ks, ds))
        att[f] = ot.astype(F32).T.astype(BF)
        m_out[0, f] = m[0]
        rl_out[0, f] = rl[0]
        delta_out[0, f] = delta[0]
        weight += nn(ot, cot[f])
    step = pl.program_id(0)

    @pl.when(step < 4)
    def _():
        w_send[0] = weight.astype(BF)

    @pl.when(step >= 4)
    def _():
        w_keep[0] = weight.astype(BF)


def back_body(
    info, q, k, v, prev, g, m, rl, delta, dq, att, w,
    gq_out, gk_out, gv_out, ret_out, mixed_out,
):
    mixed_out[...] = nn(att[...].reshape(2 * TILE, D), w[...]).astype(BF).reshape(2, TILE, TILE)
    for f in range(2):
        qs = stacked(q[f] * jnp.asarray(0.125, BF))
        gs = stacked(g[f])
        total = dq[0, f]
        for own in (True, False):
            if own:
                kb, vb = k[f], v[f]
            elif f == 0:
                kb, vb = prev[0], prev[1]
            else:
                kb, vb = k[0], v[0]
            s = nt(kb, qs)
            if not own and f == 0:
                s = jnp.where(info[TM] > 0, s, NEG)
            p = jnp.exp(s - m[0, f : f + 1]) * rl[0, f : f + 1]
            ds = (p * (nt(vb, gs) - delta[0, f : f + 1])).astype(BF)
            dk = nn(ds, qs)
            dv = nn(p.astype(BF), gs)
            total += own_half(tn(kb, ds))
            if own:
                gk_out[f] = dk
                gv_out[f] = dv
            elif f == 0:
                ret_out[0] = dk.astype(BF)
                ret_out[1] = dv.astype(BF)
            else:
                gk_out[0] += dk
                gv_out[0] += dv
        gq_out[f] = (total * 0.125).T.astype(BF)


def select_body(info, rowid, t0, t1, t2, t3, out):
    table = jnp.concatenate([t0[...], t1[...], t2[...], t3[...]], 0)
    shape = (GRID * 4 * SLOTS, RING * GRID * 8)
    r, c = iota(shape, 0), iota(shape, 1)
    tile = ((c // 8) % GRID) * RING + (info[Q] + RING - c // 128) % RING
    hit = (rowid[...] == tile) & ((r // SLOTS) % 4 == c % 4)
    for half in range(2):
        pick = hit & ((c // 4) % 2 == half)
        out[:, half * 512 : half * 512 + 512] = nn(pick.astype(F32).astype(BF), table).astype(BF)


def sum_body(info, rowid, b, keep, came, across, z0, z1, z2, z3):
    rows = RING * GRID * 8
    shape = (rows, GRID * 4 * SLOTS)
    r, c = iota(shape, 0), iota(shape, 1)
    target = ((r // 8) % GRID) * RING + (info[Q] + RING - r // 128) % RING
    pick = (rowid[...] == target) & (r % 8 == (c // SLOTS) % 4)
    strips = nn(pick.astype(F32).astype(BF), b[...])
    grads = keep[...].astype(F32) + came[...].astype(F32)
    grads = (grads.reshape(256, D) + across[...].astype(F32)).astype(BF)
    shape = (rows, 256)
    r, c = iota(shape, 0), iota(shape, 1)
    source = ((r // 8) % GRID) * 16 + ((info[Q] + RING - r // 128) % RING) * 4 + r % 8 - 4
    pick = (r % 8 >= 4) & (c == source)
    total = (strips + nn(pick.astype(F32).astype(BF), grads)).astype(BF)
    for i, z in enumerate((z0, z1, z2, z3)):
        z[...] = total[i * 128 : i * 128 + 128]


def final_body(info, strip_rows, gk, gv, ret, r_in, gk_out, gv_out, w_out):
    shape = (GRID * 8, TILE)
    r, t = iota(shape, 0), iota(shape, 1)
    hit = strip_target(info, strip_rows, shape, 8) == t
    arrived = r_in[...]
    for part, (grad, out) in enumerate(((gk, gk_out), (gv, gv_out))):
        for f in range(2):
            pick = hit & (r % 8 == 2 * f + part)
            total = grad[f] + tn(pick.astype(F32).astype(BF), arrived)
            if f == 1:
                total = total + ret[part].astype(F32)
            out[f] = total.astype(BF)
    shape = (8, GRID * 8)
    pick = iota(shape, 0) + 4 == iota(shape, 1) % 8
    w_out[...] = nn(pick.astype(F32).astype(BF), arrived)[:4]


def on_device(
    queries, key_vectors, value_vectors, w_out, rig_tiles, rig_count, strip_rows, cotangent
):
    cam = lax.axis_index("cam")
    tm = lax.axis_index("tm")
    core, zlo = tm % 2, tm // 2
    ring = cam % RING
    steps = jnp.arange(8, dtype=jnp.int32)
    order = (((zlo ^ (1 - (steps >> 1) % 2)) * 2 + (core ^ (1 - (steps >> 2)))) * 2 + steps % 2)
    count = lax.dynamic_index_in_dim(rig_count, cam, 0, keepdims=False)
    zero = jnp.zeros((), jnp.int32)
    info = jnp.concatenate([jnp.stack([core, zlo, tm, ring, cam, count, zero, zero]), order])
    info = info.astype(jnp.int32)

    q = queries.reshape(2, TILE, D)
    k = key_vectors.reshape(2, TILE, D)
    v = value_vectors.reshape(2, TILE, D)
    cot = cotangent.reshape(2, TILE, D)

    plane = [[p * RING + z for p in range(GRID)] for z in range(RING)]

    def exchange(block):
        return lax.all_to_all(block, "cam", 0, 0, axis_index_groups=plane, tiled=True)

    def along_ring(block, shift):
        route = [
            (p * RING + z, p * RING + (z + shift) % RING)
            for p in range(GRID)
            for z in range(RING)
        ]
        return lax.ppermute(block, "cam", route)

    rigs = lax.dynamic_index_in_dim(rig_tiles.reshape(GRID, RING, 7), ring, 1, keepdims=False)
    counts = lax.dynamic_index_in_dim(rig_count.reshape(GRID, RING), ring, 1, keepdims=False)
    rigs = jnp.where(jnp.arange(7, dtype=jnp.int32) < counts[:, None], rigs, -1)
    rigs = jnp.pad(rigs, ((0, 0), (0, 1)), constant_values=-1)
    rowid = jnp.broadcast_to(rigs[:, None], (GRID, 4, SLOTS)).reshape(-1)

    pair = lambda i, *_: (0, 0, i)
    row = lambda i, *_: (i, 0)
    head = lambda i, *_: (i, 0, 0)
    head4 = lambda i, *_: (i, 0, 0, 0)
    blk = (2, TILE, TILE)

    mine, last = call(
        extract_body,
        (1,),
        [info, strip_rows, (k, None, None), (v, None, None)],
        [(like((GRID * 8, 512)), None, None), (like((2, TILE, D)), None, None)],
        16,
        1 << 27,
        2 << 20,
        scalars=2,
    )
    prev = lax.ppermute(last, "tm", [(i, i + 1) for i in range(3)])
    t0 = exchange(mine.reshape(GRID, 8, 512)).reshape(GRID * 8, 512)
    t1, t2, t3 = [along_ring(t0, s) for s in (1, 2, 3)]

    g, gt, m1, l1, o1 = call(
        local_body,
        (PAIRS,),
        [
            info,
            (q, blk, pair),
            (k, blk, pair),
            (v, blk, pair),
            (prev, blk, pair),
            (cot, None, None),
            (w_out, (TILE, D), row),
        ],
        [
            (like((2, TILE, D)), blk, pair),
            (like((D, 2 * TILE)), (TILE, 2 * TILE), row),
            (like((PAIRS, 2, 256), F32), (1, 2, 256), head),
            (like((PAIRS, 2, 256), F32), (1, 2, 256), head),
            (like((PAIRS, 2, TILE, TILE), F32), (1, 2, TILE, TILE), head4),
        ],
        24,
        3 << 30,
        8 << 20,
    )

    (sends,) = call(
        select_body,
        (1,),
        [info, (rowid.reshape(-1, 1), None, None)] + [(t, None, None) for t in (t0, t1, t2, t3)],
        [(like((GRID * 4 * SLOTS, D)), None, None)],
        24,
        1 << 29,
        2 << 20,
    )
    strips = exchange(sends.reshape(GRID, 4 * SLOTS, D)).reshape(GRID, 4, SLOTS, D)

    opair = lambda i, info: (0, 0, info[ORDER + i])
    orow = lambda i, info: (info[ORDER + i], 0)
    ohead = lambda i, info: (info[ORDER + i], 0, 0)
    ohead4 = lambda i, info: (info[ORDER + i], 0, 0, 0)
    sblk = (GRID, 4, SLOTS, TILE)
    spair = lambda i, info: (0, 0, 0, info[ORDER + i])
    stat = (like((PAIRS, 2, 256), F32), (1, 2, 256), ohead)
    att, back, m, rl, delta, dq, w_send, w_keep = call(
        strip_body,
        (PAIRS,),
        [
            info,
            (q, blk, opair),
            (g, blk, opair),
            (gt, (TILE, 2 * TILE), orow),
            (strips, sblk, spair),
            (m1, (1, 2, 256), ohead),
            (l1, (1, 2, 256), ohead),
            (o1, (1, 2, TILE, TILE), ohead4),
            (cot, None, None),
        ],
        [
            (like((2, TILE, D)), blk, opair),
            (like((GRID, 4, SLOTS, D)), sblk, spair),
            stat,
            stat,
            stat,
            (like((PAIRS, 2, TILE, TILE), F32), (1, 2, TILE, TILE), ohead4),
            (like((4, TILE, D)), (1, TILE, D), lambda i, info: (jnp.minimum(i, 3), 0, 0)),
            (like((4, TILE, D)), (1, TILE, D), lambda i, info: (jnp.maximum(i - 4, 0), 0, 0)),
        ],
        24,
        2 << 30,
        10 << 20,
    )
    came = lax.ppermute(w_send, "tm", [(i, i ^ 1) for i in range(4)])
    half = (w_keep[:2].astype(F32) + came[:2].astype(F32)).astype(BF).reshape(2 * TILE, D)
    across = lax.ppermute(half, "tm", [(i, i ^ 2) for i in range(4)])
    b = exchange(back.reshape(GRID, 4 * SLOTS, D)).reshape(GRID * 4 * SLOTS, D)

    upper = ((2, TILE, D), lambda *_: (1, 0, 0))
    zs = call(
        sum_body,
        (1,),
        [
            info,
            (rowid.reshape(1, -1), None, None),
            (b, None, None),
            (w_keep,) + upper,
            (came,) + upper,
            (across, None, None),
        ],
        [(like((GRID * 8, D)), None, None)] * 4,
        32,
        1 << 30,
        4 << 20,
    )
    pieces = [zs[0]] + [along_ring(zs[s], -s) for s in (1, 2, 3)]

    gq, gk, gv, ret, mixed = call(
        back_body,
        (PAIRS,),
        [
            info,
            (q, blk, pair),
            (k, blk, pair),
            (v, blk, pair),
            (prev, blk, pair),
            (g, blk, pair),
            (m, (1, 2, 256), head),
            (rl, (1, 2, 256), head),
            (delta, (1, 2, 256), head),
            (dq, (1, 2, TILE, TILE), head4),
            (att, None, None),
            (w_out, (D, TILE), lambda i, *_: (0, i)),
        ],
        [
            (like((2, TILE, D)), blk, pair),
            (like((2, TILE, D), F32), blk, pair),
            (like((2, TILE, D), F32), blk, pair),
            (like((2, TILE, D)), blk, pair),
            (like((2, TILE, D)), blk, pair),
        ],
        24,
        4 << 30,
        12 << 20,
    )
    returned = lax.ppermute(ret, "tm", [(i + 1, i) for i in range(3)])
    summed = functools.reduce(jnp.add, [z.astype(F32) for z in pieces]).astype(BF)
    arrived = exchange(summed.reshape(GRID, 8, D)).reshape(GRID * 8, D)

    quarter = (2, TILE, 256)
    grad_k, grad_v, grad_w = call(
        final_body,
        (4,),
        [
            info,
            strip_rows,
            (gk, quarter, pair),
            (gv, quarter, pair),
            (returned, quarter, pair),
            (arrived, (GRID * 8, 256), lambda i, *_: (0, i)),
        ],
        [
            (like((2, TILE, D)), quarter, pair),
            (like((2, TILE, D)), quarter, pair),
            (like((4, D), F32), (4, 256), lambda i, *_: (0, i)),
        ],
        24,
        1 << 27,
        4 << 20,
        scalars=2,
    )
    whole = (2, 1, TILE, D)
    return (
        mixed.reshape(whole),
        gq.reshape(whole),
        grad_k.reshape(whole),
        grad_v.reshape(whole),
        grad_w,
    )


def solution(mesh):
    block = P("tm", "cam", None, None)
    return jax.shard_map(
        on_device,
        mesh=mesh,
        in_specs=(block, block, block, P(), P(), P(), P(), block),
        out_specs=(block, block, block, block, P(("tm", "cam"), None)),
        check_vma=False,
    )
```

time: 977 us -> 167 us (0.17)
  waiting for transfers between devices: 797 us -> 48.7 us
  local copies, waits for them, and re-layouts: 69.6 us -> 22.4 us
  Pallas kernels: 0 us -> 44.3 us
  other arithmetic: 45.1 us -> 2.93 us
  matrix products: 42.1 us -> 0 us
  starting transfers between devices: 4.51 us -> 46.5 us
  between operations: 14.3 us -> 0.91 us
    reduce_scatter x1 -> x0, waiting for transfers between devices: 493 us -> none  [on_device(): lax.psum_scatter(spread_grads, 'cam', scatter_dimension=1, tiled=True)[:, 0]]
    unnamed x4 -> x0, waiting for transfers between devices: 203 us -> none
    all_gather x1 -> x0, waiting for transfers between devices: 96.3 us -> none  [on_device(): everyone = lax.all_gather(own_strip[:, None], 'cam', axis=1, tiled=True)]
    pallas_call x0 -> x7, Pallas kernels: none -> 44.3 us  [call(): pl.pallas_call(body, grid_spec=pltpu.PrefetchScalarGridSpec(num_scalar_pr...]
    dot_general x10 -> x0, matrix products: 35.8 us -> none  [the longest x1 12.4 us: on_device(): jnp.einsum('jc,fjsx->fcsx', pick_table, strip_grad, precision=lax.Precisi...]
    concatenate x6 -> x0, other arithmetic: 34.7 us -> none  [the longest x1 28.5 us: on_device(): context = jnp.concatenate([key_value, before, chosen], 1)]
    all_to_all x0 -> x4, waiting for transfers between devices: none -> 31.4 us  [exchange(): lax.all_to_all(block, 'cam', 0, 0, axis_index_groups=plane, tiled=True)]
    all_to_all x0 -> x4, starting transfers between devices: none -> 24.5 us  [exchange(): lax.all_to_all(block, 'cam', 0, 0, axis_index_groups=plane, tiled=True)]
  transfers between devices with their start and end apart: 5 -> 14, of which waited for: 4 -> 8; matrix products, arithmetic and copies ran while one was open for 8% -> 3% of each run, Pallas kernels for 0% -> 13%
where the time goes in v1:
time: 167 us; the launch traced here: 166 us
  waiting for transfers between devices  48.7 us (29%)
  starting transfers between devices  46.5 us (28%)
  Pallas kernels  44.3 us (27%)
  local copies, waits for them, and re-layouts  22.4 us (13%)
  other arithmetic  2.93 us (2%)
    pallas_call x7, Pallas kernels, call(): pl.pallas_call(body, grid_spec=pltpu.PrefetchScalarGridSpec(num_scalar_pr...  44.3 us
    all_to_all x4, waiting for transfers between devices, exchange(): lax.all_to_all(block, 'cam', 0, 0, axis_index_groups=plane, tiled=True)  31.4 us
    all_to_all x4, starting transfers between devices, exchange(): lax.all_to_all(block, 'cam', 0, 0, axis_index_groups=plane, tiled=True)  24.5 us
    ppermute x6, starting transfers between devices, along_ring(): return lax.ppermute(block, 'cam', route)  18.2 us
    unnamed x52, local copies, waits for them, and re-layouts  18.1 us
    ppermute x1, waiting for transfers between devices, on_device(): prev = lax.ppermute(last, 'tm', [(i, i + 1) for i in range(3)])  8.78 us
    ppermute x6, waiting for transfers between devices, along_ring(): return lax.ppermute(block, 'cam', route)  8.51 us
  transfers between devices with their start and end apart: 14, of which 8 were waited for; matrix products, arithmetic and copies ran while one was open for 3% of the time, Pallas kernels for 13%

profile of v1, /device:TPU:32, one launch (start us, length us, event | category | flops | bytes accessed | tf_op | source)
XLA Modules:
  0.0 165.7 jit_solution(9661677041724501634)
XLA Ops:
  0.7 0.8 copy.28.strip_rows
  1.5 1.3 dynamic_slice.12
  3.5 1.0 copy-done
  4.5 1.0 copy-done.2
  5.5 2.1 %shard_map.119 = (bf16[128,512]{1,0:T(8,128)(2,1)}, bf16[2,128,1024]{2,1,0:T(8,128)(2,1)S(1)}) custom-call(s32[16]{0:T(128)S(1)} %concatenate.3.info, s32[64,16]{1,0:T(8,128)S(1)} %copy.28.strip_rows, bf16[2,128,1024]{2,1,0:T(8,128)(2,1)S(1)} %bitcast.36, bf16[2,128,1024]{2,1,0:T(8,128)(2,1)S(1)} %bitcast.39), custom_call_target="tpu_custom_call" | custom-call | flops 134217728 | bytes 2097152 | tf_op jit(solution)/shard_map/pallas_call | solution.py:49
  7.6 0.8 copy-done.13
  8.4 7.0 %all-to-all-start = ((bf16[16,8,512]{2,1,0:T(8,128)(2,1)}), bf16[16,8,512]{2,1,0:T(8,128)(2,1)S(1)}, u32[]{:S(2)}, u32[]{:S(2)}) async-start(bf16[16,8,512]{2,1,0:T(8,128)(2,1)} %bitcast.9), calls=%async_computation | async-start | bytes 262144 | tf_op jit(solution)/shard_map/all_to_all | solution.py:273
  17.4 6.0 %all-to-all-done = bf16[16,8,512]{2,1,0:T(8,128)(2,1)S(1)} async-done(((bf16[16,8,512]{2,1,0:T(8,128)(2,1)}), bf16[16,8,512]{2,1,0:T(8,128)(2,1)S(1)}, u32[]{:S(2)}, u32[]{:S(2)}) %all-to-all-start) | async-done | bytes 131104 | tf_op jit(solution)/shard_map/all_to_all | solution.py:273
  23.4 3.3 %collective-permute-start.1 = (bf16[128,512]{1,0:T(8,128)(2,1)S(1)}, bf16[128,512]{1,0:T(8,128)(2,1)S(1)}, u32[]{:S(2)}, u32[]{:S(2)}) collective-permute-start(bf16[128,512]{1,0:T(8,128)(2,1)S(1)} %bitcast.42), channel_id=1, source_target_pairs={{0,1},{1,2},{2,3},{3,0},{4,5},{5,6},{6,7},{7,4},{8,9},{9,10},{10,1... | collective-permute-start | bytes 393224 | tf_op jit(solution)/shard_map/ppermute | solution.py:281
  26.7 4.5 %collective-permute-start.2 = (bf16[128,512]{1,0:T(8,128)(2,1)S(1)}, bf16[128,512]{1,0:T(8,128)(2,1)S(1)}, u32[]{:S(2)}, u32[]{:S(2)}) collective-permute-start(bf16[128,512]{1,0:T(8,128)(2,1)S(1)} %bitcast.43), channel_id=1, source_target_pairs={{0,2},{1,3},{2,0},{3,1},{4,6},{5,7},{6,4},{7,5},{8,10},{9,11},{10,... | collective-permute-start | bytes 393224 | tf_op jit(solution)/shard_map/ppermute | solution.py:281
  31.2 2.7 %collective-permute-start.3 = (bf16[128,512]{1,0:T(8,128)(2,1)S(1)}, bf16[128,512]{1,0:T(8,128)(2,1)S(1)}, u32[]{:S(2)}, u32[]{:S(2)}) collective-permute-start(bf16[128,512]{1,0:T(8,128)(2,1)S(1)} %bitcast.44), channel_id=1, source_target_pairs={{0,3},{1,0},{2,1},{3,2},{4,7},{5,4},{6,5},{7,6},{8,11},{9,8},{10,9... | collective-permute-start | bytes 393224 | tf_op jit(solution)/shard_map/ppermute | solution.py:281
  34.2 1.2 collective-permute-done.1.t1
  35.4 4.3 %collective-permute-done.2.t2 = bf16[128,512]{1,0:T(8,128)(2,1)S(1)} collective-permute-done((bf16[128,512]{1,0:T(8,128)(2,1)S(1)}, bf16[128,512]{1,0:T(8,128)(2,1)S(1)}, u32[]{:S(2)}, u32[]{:S(2)}) %collective-permute-start.2) | collective-permute-done | bytes 131104 | tf_op jit(solution)/shard_map/ppermute | solution.py:281
  39.7 1.1 collective-permute-done.3.t3
  40.7 2.3 %shard_map.121 = bf16[512,1024]{1,0:T(8,128)(2,1)} custom-call(s32[16]{0:T(128)S(1)} %concatenate.3.info, s32[512,1]{1,0:T(8,128)S(1)} %reshape_reshape.8.rowid, bf16[128,512]{1,0:T(8,128)(2,1)S(1)} %bitcast.45, bf16[128,512]{1,0:T(8,128)(2,1)S(1)} %collective-permute-done.1.t1, bf16[128,512]{1,0:T(8,128)(2,1)S(1)} %collective-permute-done.2.t2, ...), custom_call_target="tpu_custom_call" | custom-call | flops 536870912 | bytes 2097152 | tf_op jit(solution)/shard_map/pallas_call | solution.py:49
  43.0 3.7 %all-to-all-start.1 = ((bf16[16,32,1024]{2,1,0:T(8,128)(2,1)}), bf16[16,32,1024]{2,1,0:T(8,128)(2,1)S(1)}, u32[]{:S(2)}, u32[]{:S(2)}) async-start(bf16[16,32,1024]{2,1,0:T(8,128)(2,1)} %bitcast.11), calls=%async_computation.1 | async-start | bytes 2097152 | tf_op jit(solution)/shard_map/all_to_all | solution.py:273
  46.7 1.9 %collective-permute-start = (bf16[2,128,1024]{2,1,0:T(8,128)(2,1)}, bf16[2,128,1024]{2,1,0:T(8,128)(2,1)S(1)}, u32[]{:S(2)}, u32[]{:S(2)}) collective-permute-start(bf16[2,128,1024]{2,1,0:T(8,128)(2,1)} %copy-done.13), channel_id=1, source_target_pairs={{0,64},{64,128},{128,192},{1,65},{65,129},{129,193},{2,66},{66,130... | collective-permute-start | bytes 1572872 | tf_op jit(solution)/shard_map/ppermute | solution.py:305
  48.6 8.8 %collective-permute-done.prev = bf16[2,128,1024]{2,1,0:T(8,128)(2,1)S(1)} collective-permute-done((bf16[2,128,1024]{2,1,0:T(8,128)(2,1)}, bf16[2,128,1024]{2,1,0:T(8,128)(2,1)S(1)}, u32[]{:S(2)}, u32[]{:S(2)}) %collective-permute-start) | collective-permute-done | bytes 524320 | tf_op jit(solution)/shard_map/ppermute | solution.py:305
  57.4 1.6 copy-done.4
  59.0 9.5 %shard_map.120 = (bf16[2,128,1024]{2,1,0:T(8,128)(2,1)S(1)}, bf16[1024,256]{1,0:T(8,128)(2,1)S(1)}, f32[8,2,256]{2,1,0:T(2,128)S(1)}, f32[8,2,256]{2,1,0:T(2,128)S(1)}, f32[8,2,128,128]{3,2,1,0:T(8,128)S(1)}) custom-call(s32[16]{0:T(128)S(1)} %concatenate.3.info, bf16[2,128,1024]{2,1,0:T(8,128)(2,1)S(1)} %bitcast.48, bf16[2,128,1024]{2,1,0:T(8,128)(2,1)S(1)} %bitcast.37, ...), custom_call_target="tpu_custom_call" | custom-call | flops 3221225472 | bytes 8388608 | tf_op jit(solution)/shard_map/pallas_call | solution.py:49
  68.5 0.8 copy-done.11
  69.3 1.0 copy-done.16
  70.3 0.8 copy-done.18
  71.1 0.8 copy-done.23
  71.9 1.0 copy-done.7
  72.9 1.0 copy-done.9
  74.0 1.2 copy-done.17
  75.2 1.0 copy-done.19
  76.2 1.0 copy-done.24
  77.3 11.4 %shard_map.122 = (bf16[2,128,1024]{2,1,0:T(8,128)(2,1)S(1)}, bf16[16,4,8,1024]{3,2,1,0:T(8,128)(2,1)}, f32[8,2,256]{2,1,0:T(2,128)S(1)}, f32[8,2,256]{2,1,0:T(2,...) custom-call(s32[16]{0:T(128)S(1)} %concatenate.3.info, ...), custom_call_target="tpu_custom_call" | custom-call | flops 2147483648 | bytes 10485760 | tf_op jit(solution)/shard_map/pallas_call | solution.py:49
  88.7 1.0 copy-done.14
  89.7 0.8 copy-done.21
  90.5 7.2 %all-to-all-start.2 = ((bf16[16,32,1024]{2,1,0:T(8,128)(2,1)}), bf16[16,32,1024]{2,1,0:T(8,128)(2,1)S(1)}, u32[]{:S(2)}, u32[]{:S(2)}) async-start(bf16[16,32,1024]{2,1,0:T(8,128)(2,1)} %bitcast.17), calls=%async_computation.2 | async-start | bytes 2097152 | tf_op jit(solution)/shard_map/all_to_all | solution.py:273
  97.7 2.0 %add_convert_fusion = bf16[2,128,1024]{2,1,0:T(8,128)(2,1)} fusion(bf16[4,128,1024]{2,1,0:T(8,128)(2,1)} %collective-permute-done.5.came, bf16[4,128,1024]{2,1,0:T(8,128)(2,1)S(1)} %get-tuple-element.50.keep), kind=kLoop, calls=%fused_computation | loop fusion | flops 1048576 | bytes 1572864 | tf_op jit(solution)/shard_map/convert_element_type | solution.py:380
  99.8 16.5 %all-to-all-done.2 = bf16[16,32,1024]{2,1,0:T(8,128)(2,1)S(1)} async-done(((bf16[16,32,1024]{2,1,0:T(8,128)(2,1)}), bf16[16,32,1024]{2,1,0:T(8,128)(2,1)S(1)}, u32[]{:S(2)}, u32[]{:S(2)}) %all-to-all-start.2) | async-done | bytes 1048608 | tf_op jit(solution)/shard_map/all_to_all | solution.py:273
  116.4 3.3 %shard_map.124 = (bf16[128,1024]{1,0:T(8,128)(2,1)S(1)}, bf16[128,1024]{1,0:T(8,128)(2,1)S(1)}, bf16[128,1024]{1,0:T(8,128)(2,1)S(1)}, bf16[128,1024]{1,0:T(8,128)(2,1)S(1)}) custom-call(s32[16]{0:T(128)S(1)} %concatenate.3.info, s32[1,512]{1,0:T(1,128)S(1)} %reshape_reshape.7.rowid, bf16[512,1024]{1,0:T(8,128)(2,1)S(1)} %bitcast.35, ...), custom_call_target="tpu_custom_call" | custom-call | flops 1073741824 | bytes 4194304 | tf_op jit(solution)/shard_map/pallas_call | solution.py:49
  119.6 3.6 %collective-permute-start.7 = (bf16[128,1024]{1,0:T(8,128)(2,1)S(1)}, bf16[128,1024]{1,0:T(8,128)(2,1)S(1)}, u32[]{:S(2)}, u32[]{:S(2)}) collective-permute-start(bf16[128,1024]{1,0:T(8,128)(2,1)S(1)} %get-tuple-element.53), channel_id=1, source_target_pairs={{0,3},{1,0},{2,1},{3,2},{4,7},{5,4},{6,5},{7,6},{8,11},{9,8},{10,9... | collective-permute-start | bytes 786440 | tf_op jit(solution)/shard_map/ppermute | solution.py:281
  123.3 1.9 %collective-permute-start.8 = (bf16[128,1024]{1,0:T(8,128)(2,1)S(1)}, bf16[128,1024]{1,0:T(8,128)(2,1)S(1)}, u32[]{:S(2)}, u32[]{:S(2)}) collective-permute-start(bf16[128,1024]{1,0:T(8,128)(2,1)S(1)} %get-tuple-element.54), channel_id=1, source_target_pairs={{0,2},{1,3},{2,0},{3,1},{4,6},{5,7},{6,4},{7,5},{8,10},{9,11},{10,... | collective-permute-start | bytes 786440 | tf_op jit(solution)/shard_map/ppermute | solution.py:281
  125.2 2.2 %collective-permute-start.9 = (bf16[128,1024]{1,0:T(8,128)(2,1)S(1)}, bf16[128,1024]{1,0:T(8,128)(2,1)S(1)}, u32[]{:S(2)}, u32[]{:S(2)}) collective-permute-start(bf16[128,1024]{1,0:T(8,128)(2,1)S(1)} %get-tuple-element.55), channel_id=1, source_target_pairs={{0,1},{1,2},{2,3},{3,0},{4,5},{5,6},{6,7},{7,4},{8,9},{9,10},{10,1... | collective-permute-start | bytes 786440 | tf_op jit(solution)/shard_map/ppermute | solution.py:281
  127.5 1.2 copy-done.15
  128.7 1.0 copy-done.22
  129.7 12.3 %shard_map.123 = (bf16[2,128,1024]{2,1,0:T(8,128)(2,1)}, f32[2,128,1024]{2,1,0:T(8,128)S(1)}, f32[2,128,1024]{2,1,0:T(8,128)S(1)}, bf16[2,128,1024]{2,1,0:T(8,128)(2,1)}, bf16[2,128,1024]{2,1,0:T(8,128)(2,1)}) custom-call(s32[16]{0:T(128)S(1)} %concatenate.3.info, bf16[2,128,1024]{2,1,0:T(8,128)(2,1)S(1)} %bitcast.50, bf16[2,128,1024]{2,1,0:T(8,128)(2,1)S(1)} %bitcast.38, ...), custom_call_target="tpu_custom_call" | custom-call | flops 4294967296 | bytes 12582912 | tf_op jit(solution)/shard_map/pallas_call | solution.py:49
  142.0 1.9 %collective-permute-start.4 = (bf16[2,128,1024]{2,1,0:T(8,128)(2,1)}, bf16[2,128,1024]{2,1,0:T(8,128)(2,1)S(1)}, u32[]{:S(2)}, u32[]{:S(2)}) collective-permute-start(bf16[2,128,1024]{2,1,0:T(8,128)(2,1)} %get-tuple-element.48), channel_id=1, source_target_pairs={{64,0},{128,64},{192,128},{65,1},{129,65},{193,129},{66,2},{130,66... | collective-permute-start | bytes 1572872 | tf_op jit(solution)/shard_map/ppermute | solution.py:431
  144.0 2.0 %collective-permute-done.9 = bf16[128,1024]{1,0:T(8,128)(2,1)S(1)} collective-permute-done((bf16[128,1024]{1,0:T(8,128)(2,1)S(1)}, bf16[128,1024]{1,0:T(8,128)(2,1)S(1)}, u32[]{:S(2)}, u32[]{:S(2)}) %collective-permute-start.9) | collective-permute-done | bytes 262176 | tf_op jit(solution)/shard_map/ppermute | solution.py:281
  145.9 0.9 fusion
  146.8 6.6 %all-to-all-start.3 = ((bf16[16,8,1024]{2,1,0:T(8,128)(2,1)}), bf16[16,8,1024]{2,1,0:T(8,128)(2,1)S(1)}, u32[]{:S(2)}, u32[]{:S(2)}) async-start(bf16[16,8,1024]{2,1,0:T(8,128)(2,1)} %fusion), calls=%async_computation.3 | async-start | bytes 524288 | tf_op jit(solution)/shard_map/all_to_all | solution.py:273
  153.4 8.9 %all-to-all-done.3 = bf16[16,8,1024]{2,1,0:T(8,128)(2,1)S(1)} async-done(((bf16[16,8,1024]{2,1,0:T(8,128)(2,1)}), bf16[16,8,1024]{2,1,0:T(8,128)(2,1)S(1)}, u32[]{:S(2)}, u32[]{:S(2)}) %all-to-all-start.3) | async-done | bytes 262176 | tf_op jit(solution)/shard_map/all_to_all | solution.py:273
  162.3 3.5 %shard_map.125 = (bf16[2,128,1024]{2,1,0:T(8,128)(2,1)}, bf16[2,128,1024]{2,1,0:T(8,128)(2,1)}, f32[4,1024]{1,0:T(4,128)}) custom-call(s32[16]{0:T(128)S(1)} %concatenate.3.info, s32[64,16]{1,0:T(8,128)S(1)} %copy.28.strip_rows, f32[2,128,1024]{2,1,0:T(8,128)S(1)} %get-tuple-element.46.gk, f32[2,128,1024]{2,1,0:T(8,128)S(1)} %get-tuple-element.47.gv, ...), custom_call_target="tpu_custom_call" | custom-call | flops 134217728 | bytes 4194304 | tf_op jit(solution)/shard_map/pallas_call | solution.py:49
  (54 shorter events, 3.1 us)
Async XLA Ops:
  3.4 1.0 copy-start
  4.5 1.0 copy-start.2
  7.6 0.8 copy-start.13
  8.4 15.0 %all-to-all-start = ((bf16[16,8,512]{2,1,0:T(8,128)(2,1)}), bf16[16,8,512]{2,1,0:T(8,128)(2,1)S(1)}, u32[]{:S(2)}, u32[]{:S(2)}) async-start(bf16[16,8,512]{2,1,0:T(8,128)(2,1)} %bitcast.9), calls=%async_computation | async-start | bytes 262144 | tf_op jit(solution)/shard_map/all_to_all | solution.py:273
  23.4 12.0 %collective-permute-start.1 = (bf16[128,512]{1,0:T(8,128)(2,1)S(1)}, bf16[128,512]{1,0:T(8,128)(2,1)S(1)}, u32[]{:S(2)}, u32[]{:S(2)}) collective-permute-start(bf16[128,512]{1,0:T(8,128)(2,1)S(1)} %bitcast.42), channel_id=1, source_target_pairs={{0,1},{1,2},{2,3},{3,0},{4,5},{5,6},{6,7},{7,4},{8,9},{9,10},{10,1... | collective-permute-start | bytes 393224 | tf_op jit(solution)/shard_map/ppermute | solution.py:281
  26.7 13.0 %collective-permute-start.2 = (bf16[128,512]{1,0:T(8,128)(2,1)S(1)}, bf16[128,512]{1,0:T(8,128)(2,1)S(1)}, u32[]{:S(2)}, u32[]{:S(2)}) collective-permute-start(bf16[128,512]{1,0:T(8,128)(2,1)S(1)} %bitcast.43), channel_id=1, source_target_pairs={{0,2},{1,3},{2,0},{3,1},{4,6},{5,7},{6,4},{7,5},{8,10},{9,11},{10,... | collective-permute-start | bytes 393224 | tf_op jit(solution)/shard_map/ppermute | solution.py:281
  31.2 9.5 %collective-permute-start.3 = (bf16[128,512]{1,0:T(8,128)(2,1)S(1)}, bf16[128,512]{1,0:T(8,128)(2,1)S(1)}, u32[]{:S(2)}, u32[]{:S(2)}) collective-permute-start(bf16[128,512]{1,0:T(8,128)(2,1)S(1)} %bitcast.44), channel_id=1, source_target_pairs={{0,3},{1,0},{2,1},{3,2},{4,7},{5,4},{6,5},{7,6},{8,11},{9,8},{10,9... | collective-permute-start | bytes 393224 | tf_op jit(solution)/shard_map/ppermute | solution.py:281
  34.1 23.3 %copy-start.1 = (bf16[2,1,128,1024]{3,2,1,0:T(8,128)(2,1)S(1)}, bf16[2,1,128,1024]{3,2,1,0:T(8,128)(2,1)}, u32[]{:S(2)}) copy-start(bf16[2,1,128,1024]{3,2,1,0:T(8,128)(2,1)} %param.9) | copy-start | bytes 1572868
  34.1 23.3 %copy-start.3 = (bf16[2,1,128,1024]{3,2,1,0:T(8,128)(2,1)S(1)}, bf16[2,1,128,1024]{3,2,1,0:T(8,128)(2,1)}, u32[]{:S(2)}) copy-start(bf16[2,1,128,1024]{3,2,1,0:T(8,128)(2,1)} %param.10) | copy-start | bytes 1572868
  34.1 23.3 %copy-start.6 = (bf16[2,1,128,1024]{3,2,1,0:T(8,128)(2,1)S(1)}, bf16[2,1,128,1024]{3,2,1,0:T(8,128)(2,1)}, u32[]{:S(2)}) copy-start(bf16[2,1,128,1024]{3,2,1,0:T(8,128)(2,1)} %param.15) | copy-start | bytes 1572868
  34.1 23.2 %copy-start.8 = (bf16[2,1,128,1024]{3,2,1,0:T(8,128)(2,1)S(1)}, bf16[2,1,128,1024]{3,2,1,0:T(8,128)(2,1)}, u32[]{:S(2)}) copy-start(bf16[2,1,128,1024]{3,2,1,0:T(8,128)(2,1)} %param.8) | copy-start | bytes 1572868
  43.0 28.9 %all-to-all-start.1 = ((bf16[16,32,1024]{2,1,0:T(8,128)(2,1)}), bf16[16,32,1024]{2,1,0:T(8,128)(2,1)S(1)}, u32[]{:S(2)}, u32[]{:S(2)}) async-start(bf16[16,32,1024]{2,1,0:T(8,128)(2,1)} %bitcast.11), calls=%async_computation.1 | async-start | bytes 2097152 | tf_op jit(solution)/shard_map/all_to_all | solution.py:273
  46.7 10.7 %collective-permute-start = (bf16[2,128,1024]{2,1,0:T(8,128)(2,1)}, bf16[2,128,1024]{2,1,0:T(8,128)(2,1)S(1)}, u32[]{:S(2)}, u32[]{:S(2)}) collective-permute-start(bf16[2,128,1024]{2,1,0:T(8,128)(2,1)} %copy-done.13), channel_id=1, source_target_pairs={{0,64},{64,128},{128,192},{1,65},{65,129},{129,193},{2,66},{66,130... | collective-permute-start | bytes 1572872 | tf_op jit(solution)/shard_map/ppermute | solution.py:305
  57.4 1.6 copy-start.4
  68.5 0.8 copy-start.11
  69.3 1.0 copy-start.16
  70.3 0.8 copy-start.18
  71.1 0.8 copy-start.23
  71.9 1.0 copy-start.7
  72.9 1.0 copy-start.9
  74.0 1.2 copy-start.17
  75.2 1.0 copy-start.19
  76.2 1.0 copy-start.24
  88.7 1.0 copy-start.14
  89.7 0.8 copy-start.21
  90.5 7.2 %collective-permute-start.5 = (bf16[4,128,1024]{2,1,0:T(8,128)(2,1)}, bf16[4,128,1024]{2,1,0:T(8,128)(2,1)}, u32[]{:S(2)}, u32[]{:S(2)}) collective-permute-start(bf16[4,128,1024]{2,1,0:T(8,128)(2,1)} %get-tuple-element.51), channel_id=1, source_target_pairs={{0,64},{64,0},{128,192},{192,128},{1,65},{65,1},{129,193},{193,129... | collective-permute-start | bytes 3145736 | tf_op jit(solution)/shard_map/ppermute | solution.py:379
  90.5 25.8 %all-to-all-start.2 = ((bf16[16,32,1024]{2,1,0:T(8,128)(2,1)}), bf16[16,32,1024]{2,1,0:T(8,128)(2,1)S(1)}, u32[]{:S(2)}, u32[]{:S(2)}) async-start(bf16[16,32,1024]{2,1,0:T(8,128)(2,1)} %bitcast.17), calls=%async_computation.2 | async-start | bytes 2097152 | tf_op jit(solution)/shard_map/all_to_all | solution.py:273
  99.7 16.7 %collective-permute-start.6 = (bf16[256,1024]{1,0:T(8,128)(2,1)}, bf16[256,1024]{1,0:T(8,128)(2,1)}, u32[]{:S(2)}, u32[]{:S(2)}) collective-permute-start(bf16[256,1024]{1,0:T(8,128)(2,1)} %bitcast.19), channel_id=1, source_target_pairs={{0,128},{64,192},{128,0},{192,64},{1,129},{65,193},{129,1},{193,65... | collective-permute-start | bytes 1572872 | tf_op jit(solution)/shard_map/ppermute | solution.py:381
  116.3 11.1 %copy-start.5 = (bf16[1024,1024]{1,0:T(8,128)(2,1)S(1)}, bf16[1024,1024]{1,0:T(8,128)(2,1)}, u32[]{:S(2)}) copy-start(bf16[1024,1024]{1,0:T(8,128)(2,1)} %w.3) | copy-start | bytes 6291460
  116.3 11.1 %copy-start.10 = (bf16[2,1,128,1024]{3,2,1,0:T(8,128)(2,1)S(1)}, bf16[2,1,128,1024]{3,2,1,0:T(8,128)(2,1)}, u32[]{:S(2)}) copy-start(bf16[2,1,128,1024]{3,2,1,0:T(8,128)(2,1)} %param.8) | copy-start | bytes 1572868
  116.3 11.1 %copy-start.12 = (bf16[2,128,1024]{2,1,0:T(8,128)(2,1)S(1)}, bf16[2,128,1024]{2,1,0:T(8,128)(2,1)}, u32[]{:S(2)}) copy-start(bf16[2,128,1024]{2,1,0:T(8,128)(2,1)} %copy-done.11) | copy-start | bytes 1572868
  116.3 11.1 %copy-start.20 = (bf16[2,128,1024]{2,1,0:T(8,128)(2,1)S(1)}, bf16[2,128,1024]{2,1,0:T(8,128)(2,1)}, u32[]{:S(2)}) copy-start(bf16[2,128,1024]{2,1,0:T(8,128)(2,1)} %copy-done.18) | copy-start | bytes 1572868
  119.6 24.3 %collective-permute-start.7 = (bf16[128,1024]{1,0:T(8,128)(2,1)S(1)}, bf16[128,1024]{1,0:T(8,128)(2,1)S(1)}, u32[]{:S(2)}, u32[]{:S(2)}) collective-permute-start(bf16[128,1024]{1,0:T(8,128)(2,1)S(1)} %get-tuple-element.53), channel_id=1, source_target_pairs={{0,3},{1,0},{2,1},{3,2},{4,7},{5,4},{6,5},{7,6},{8,11},{9,8},{10,9... | collective-permute-start | bytes 786440 | tf_op jit(solution)/shard_map/ppermute | solution.py:281
  123.3 20.7 %collective-permute-start.8 = (bf16[128,1024]{1,0:T(8,128)(2,1)S(1)}, bf16[128,1024]{1,0:T(8,128)(2,1)S(1)}, u32[]{:S(2)}, u32[]{:S(2)}) collective-permute-start(bf16[128,1024]{1,0:T(8,128)(2,1)S(1)} %get-tuple-element.54), channel_id=1, source_target_pairs={{0,2},{1,3},{2,0},{3,1},{4,6},{5,7},{6,4},{7,5},{8,10},{9,11},{10,... | collective-permute-start | bytes 786440 | tf_op jit(solution)/shard_map/ppermute | solution.py:281
  125.2 20.7 %collective-permute-start.9 = (bf16[128,1024]{1,0:T(8,128)(2,1)S(1)}, bf16[128,1024]{1,0:T(8,128)(2,1)S(1)}, u32[]{:S(2)}, u32[]{:S(2)}) collective-permute-start(bf16[128,1024]{1,0:T(8,128)(2,1)S(1)} %get-tuple-element.55), channel_id=1, source_target_pairs={{0,1},{1,2},{2,3},{3,0},{4,5},{5,6},{6,7},{7,4},{8,9},{9,10},{10,1... | collective-permute-start | bytes 786440 | tf_op jit(solution)/shard_map/ppermute | solution.py:281
  127.4 1.2 copy-start.15
  128.7 1.0 copy-start.22
  142.0 11.4 %collective-permute-start.4 = (bf16[2,128,1024]{2,1,0:T(8,128)(2,1)}, bf16[2,128,1024]{2,1,0:T(8,128)(2,1)S(1)}, u32[]{:S(2)}, u32[]{:S(2)}) collective-permute-start(bf16[2,128,1024]{2,1,0:T(8,128)(2,1)} %get-tuple-element.48), channel_id=1, source_target_pairs={{64,0},{128,64},{192,128},{65,1},{129,65},{193,129},{66,2},{130,66... | collective-permute-start | bytes 1572872 | tf_op jit(solution)/shard_map/ppermute | solution.py:431
  146.8 15.5 %all-to-all-start.3 = ((bf16[16,8,1024]{2,1,0:T(8,128)(2,1)}), bf16[16,8,1024]{2,1,0:T(8,128)(2,1)S(1)}, u32[]{:S(2)}, u32[]{:S(2)}) async-start(bf16[16,8,1024]{2,1,0:T(8,128)(2,1)} %fusion), calls=%async_computation.3 | async-start | bytes 524288 | tf_op jit(solution)/shard_map/all_to_all | solution.py:273

commit v2 on v1

v2 whole, which is shorter than its diff:
```python
import functools

import jax
import jax.numpy as jnp
from jax import lax
from jax.experimental import pallas as pl
from jax.experimental.pallas import tpu as pltpu
from jax.sharding import PartitionSpec as P

TILE = 128
D = 1024
PAIRS = 8
RING = 4
GRID = 16
SLOTS = 8
NEG = -1e30
BF = jnp.bfloat16
F32 = jnp.float32
MIB = 1 << 20

TM, CAM = range(2)
BLOCKS = 4
WIDE = 2 * TILE
AFTER = "after"


def nt(a, b):
    return lax.dot_general(a, b, (((1,), (1,)), ((), ())), preferred_element_type=F32)


def tn(a, b):
    return lax.dot_general(a, b, (((0,), (0,)), ((), ())), preferred_element_type=F32)


def nn(a, b):
    return jnp.dot(a, b, preferred_element_type=F32)


def iota(shape, dim):
    return lax.broadcasted_iota(jnp.int32, shape, dim)


def call(body, grid, inputs, outputs, limit_mib, flops, nbytes, scalars=1):
    def spec(entry):
        shape, block, index = entry
        if block == AFTER:
            return pl.BlockSpec(memory_space=pl.ANY)
        if block is None:
            zeros = (0,) * len(shape.shape)
            return pl.BlockSpec(shape.shape, lambda *_: zeros)
        return pl.BlockSpec(block, index)

    return pl.pallas_call(
        body,
        grid_spec=pltpu.PrefetchScalarGridSpec(
            num_scalar_prefetch=scalars,
            grid=grid,
            in_specs=[spec(e) for e in inputs[scalars:]],
            out_specs=[spec(e) for e in outputs],
        ),
        out_shape=[e[0] for e in outputs],
        compiler_params=pltpu.CompilerParams(vmem_limit_bytes=limit_mib * MIB),
        cost_estimate=pl.CostEstimate(flops=flops, bytes_accessed=nbytes, transcendentals=0),
    )(*[e[0] if isinstance(e, tuple) else e for e in inputs])


def like(shape, dtype=BF):
    return jax.ShapeDtypeStruct(shape, dtype)


def strip_target(info, strip_rows, shape, group):
    s = iota(shape, 0) // group
    target = jnp.zeros(shape, jnp.int32)
    for i in range(GRID):
        target = jnp.where(s == i, strip_rows[i, info[CAM]], target)
    return target


def ring_place(info, back):
    return (info[CAM] + RING - back) % RING


def extract_body(info, strip_rows, k, v, out, last):
    shape = (GRID * 8, 2 * TILE)
    r, c = iota(shape, 0), iota(shape, 1)
    hit = (strip_target(info, strip_rows, shape, 8) == c % TILE) & ((r // 2) % 2 == c // TILE)
    total = jnp.zeros((GRID * 8, D // 2), F32)
    for part, ref in enumerate((k, v)):
        whole = ref[...].reshape(2 * TILE, D)
        for half in range(2):
            pick = hit & (r % 2 == part) & ((r // 4) % 2 == half)
            total += nn(pick.astype(F32).astype(BF), whole[:, half * 512 : half * 512 + 512])
        last[part] = ref[1]
    out[...] = total.astype(BF)


def stacked(block):
    first = iota(block.shape, 1) < 64
    zero = jnp.zeros_like(block)
    return jnp.concatenate([jnp.where(first, block, zero), jnp.where(first, zero, block)], 0)


def own_half(wide):
    return jnp.concatenate([wide[:64, :TILE], wide[64:, TILE:]], 0)


def spread(row):
    return jnp.concatenate(
        [jnp.broadcast_to(row[:, :TILE], (64, TILE)), jnp.broadcast_to(row[:, TILE:], (64, TILE))],
        0,
    )


def units():
    return [(n, slice(n * TILE, n * TILE + TILE), f) for n in range(2) for f in range(2)]


def grad_body(cot, w, g_out, gt_out):
    cots = cot[...].reshape(2 * TILE, D)
    g_out[...] = nt(cots, w[...]).astype(BF).reshape(2, TILE, WIDE)
    gt_out[...] = nt(w[...], cots).astype(BF)


def copy_body(block, _, out):
    out[...] = block[...]


def local_body(info, q, k, v, prev, _, m_out, l_out, o_out):
    for n, at, f in units():
        qs = stacked(q[f, :, at] * jnp.asarray(0.125, BF))
        before_k, before_v = (prev[0, :, at], prev[1, :, at]) if f == 0 else (k[0, :, at], v[0, :, at])
        s1 = nt(k[f, :, at], qs)
        s2 = nt(before_k, qs)
        if f == 0:
            s2 = jnp.where(info[TM] > 0, s2, NEG)
        m = jnp.maximum(jnp.max(s1, 0, keepdims=True), jnp.max(s2, 0, keepdims=True))
        p1 = jnp.exp(s1 - m)
        p2 = jnp.exp(s2 - m)
        m_out[n, f] = m[0]
        l_out[n, f] = jnp.sum(p1, 0) + jnp.sum(p2, 0)
        o_out[n, f] = own_half(tn(v[f, :, at], p1.astype(BF)) + tn(before_v, p2.astype(BF)))


def strip_body(
    info, rig_count, q, g, gt, strips, m1, l1, o1, _,
    back, m_out, rl_out, delta_out, dq_out, *ot_out,
):
    seen = iota((TILE, WIDE), 0) % SLOTS < rig_count[info[CAM]]
    ots = {}
    for n, at, f in units():
        qs = stacked(q[f, :, at] * jnp.asarray(0.125, BF))
        gs = stacked(g[f, :, at])
        ks = strips[:, 2 * f, :, at].astype(F32).reshape(TILE, TILE).astype(BF)
        vs = strips[:, 2 * f + 1, :, at].astype(F32).reshape(TILE, TILE).astype(BF)
        s = jnp.where(seen, nt(ks, qs), NEG)
        m_old = m1[n, f : f + 1]
        m = jnp.maximum(m_old, jnp.max(s, 0, keepdims=True))
        p = jnp.exp(s - m)
        shrink = jnp.exp(m_old - m)
        rl = 1.0 / (l1[n, f : f + 1] * shrink + jnp.sum(p, 0, keepdims=True))
        p = p * rl
        pb = p.astype(BF)
        ot = (o1[n, f] * spread(shrink * rl) + own_half(tn(vs, pb))).astype(BF)
        prod = gt[at, f * TILE : f * TILE + TILE].astype(F32) * ot.astype(F32)
        delta = jnp.concatenate(
            [jnp.sum(prod[:64], 0, keepdims=True), jnp.sum(prod[64:], 0, keepdims=True)], 1
        )
        ds = (p * (nt(vs, gs) - delta)).astype(BF)
        back[:, 2 * f, :, at] = nn(ds, qs).reshape(GRID, SLOTS, TILE).astype(BF)
        back[:, 2 * f + 1, :, at] = nn(pb, gs).reshape(GRID, SLOTS, TILE).astype(BF)
        dq_out[n, f] = own_half(tn(ks, ds))
        m_out[n, f] = m[0]
        rl_out[n, f] = rl[0]
        delta_out[n, f] = delta[0]
        ots[n, f] = ot
    whole = jnp.concatenate([jnp.concatenate([ots[n, 0], ots[n, 1]], 1) for n in range(2)], 0)
    for i, out in enumerate(ot_out):

        @pl.when(pl.program_id(0) == i)
        def _():
            out[...] = whole


def weight_body(info, c0, c1, c2, c3, ot0, ot1, ot2, ot3, _, e0, e1, e2, e3):
    total = jnp.zeros((WIDE, D), F32)
    for ot, c in ((ot0, c0), (ot1, c1), (ot2, c2), (ot3, c3)):
        total += nn(ot[...], c[...].reshape(WIDE, D))
    total = total.astype(BF)
    shape = (RING * GRID * 8, WIDE)
    r, c = iota(shape, 0), iota(shape, 1)
    hit = c == ((r // 8) % GRID) * 16 + ring_place(info, r // 128) * 4 + r % 4
    out = jnp.zeros((RING * GRID * 8, D // 2), F32)
    for half in range(2):
        pick = hit & ((r // 4) % 2 == half)
        out += nn(pick.astype(F32).astype(BF), total[:, half * 512 : half * 512 + 512])
    out = out.astype(BF)
    for i, e in enumerate((e0, e1, e2, e3)):
        e[...] = out[i * 128 : i * 128 + 128]


def mixed_body(info, ot0, ot1, ot2, ot3, w, _, out):
    total = jnp.zeros((WIDE, 512), F32)
    for i, ot in enumerate((ot0, ot1, ot2, ot3)):
        total += tn(ot[...], w[pl.ds((info[TM] ^ i) * WIDE, WIDE)])
    out[...] = total.astype(BF).reshape(2, TILE, 512)


def block_back(kb, vb, qs, gs, m, rl, delta, hidden=None):
    s = nt(kb, qs)
    if hidden is not None:
        s = jnp.where(hidden, NEG, s)
    p = jnp.exp(s - m) * rl
    ds = (p * (nt(vb, gs) - delta)).astype(BF)
    return nn(ds, qs), nn(p.astype(BF), gs), own_half(tn(kb, ds))


def before_body(info, q, prev, g, m, rl, delta, dq, ret_out, dq_out):
    for n in range(4):
        at = slice(n * TILE, n * TILE + TILE)
        qs = stacked(q[0, :, at] * jnp.asarray(0.125, BF))
        gs = stacked(g[0, :, at])
        dk, dv, part = block_back(
            prev[0, :, at], prev[1, :, at], qs, gs, m[n, :1], rl[n, :1], delta[n, :1],
            info[TM] == 0,
        )
        ret_out[0, :, at] = dk.astype(BF)
        ret_out[1, :, at] = dv.astype(BF)
        dq_out[n] = dq[n, 0] + part


def back_body(
    info, q, k, v, g, m, rl, delta, dq0, dq, _, __, ___, ____, gq_out, gk_out, gv_out
):
    for n in range(2):
        at = slice(n * TILE, n * TILE + TILE)
        for f in range(2):
            qs = stacked(q[f, :, at] * jnp.asarray(0.125, BF))
            gs = stacked(g[f, :, at])
            stats = m[n, f : f + 1], rl[n, f : f + 1], delta[n, f : f + 1]
            dk, dv, part = block_back(k[f, :, at], v[f, :, at], qs, gs, *stats)
            if f == 0:
                total, dk0, dv0 = dq0[n] + part, dk, dv
            else:
                gk_out[1, :, at] = dk
                gv_out[1, :, at] = dv
                dk, dv, before = block_back(k[0, :, at], v[0, :, at], qs, gs, *stats)
                gk_out[0, :, at] = dk0 + dk
                gv_out[0, :, at] = dv0 + dv
                total = dq[n, 0] + part + before
            gq_out[f, :, at] = (total * 0.125).T.astype(BF)


def select_body(info, rowid, t0, t1, t2, t3, _, out):
    table = jnp.concatenate([t0[...], t1[...], t2[...], t3[...]], 0)
    shape = (GRID * 4 * SLOTS, RING * GRID * 8)
    r, c = iota(shape, 0), iota(shape, 1)
    tile = ((c // 8) % GRID) * RING + ring_place(info, c // 128)
    hit = (rowid[...] == tile) & ((r // SLOTS) % 4 == c % 4)
    for half in range(2):
        pick = hit & ((c // 4) % 2 == half)
        out[:, half * 512 : half * 512 + 512] = nn(pick.astype(F32).astype(BF), table).astype(BF)


def sum_body(info, rowid, b, z0, z1, z2, z3):
    rows = RING * GRID * 8
    shape = (rows, GRID * 4 * SLOTS)
    r, c = iota(shape, 0), iota(shape, 1)
    target = ((r // 8) % GRID) * RING + ring_place(info, r // 128)
    hit = (rowid[...] == target) & (r % 4 == (c // SLOTS) % 4)
    total = jnp.zeros((rows, D // 2), F32)
    for half in range(2):
        pick = hit & ((r // 4) % 2 == half)
        total += nn(pick.astype(F32).astype(BF), b[:, half * 512 : half * 512 + 512])
    total = total.astype(BF)
    for i, z in enumerate((z0, z1, z2, z3)):
        z[...] = total[i * 128 : i * 128 + 128]


def merge_body(z0, z1, z2, z3, e0, e1, e2, e3, _, out):
    def total(parts):
        return functools.reduce(jnp.add, [part[...].astype(F32) for part in parts])

    out[...] = jnp.concatenate([total((z0, z1, z2, z3)), total((e0, e1, e2, e3))], 1).astype(BF)


def final_body(info, strip_rows, gk, gv, ret, r_in, gk_out, gv_out, w_out):
    half = pl.program_id(0) // 2
    shape = (GRID * 16, TILE)
    r, t = iota(shape, 0), iota(shape, 1)
    hit = strip_target(info, strip_rows, shape, 16) == t
    arrived = r_in[...]
    for part, (grad, out) in enumerate(((gk, gk_out), (gv, gv_out))):
        for f in range(2):
            pick = hit & (r % 16 == half * 4 + 2 * f + part)
            total = grad[f] + tn(pick.astype(F32).astype(BF), arrived)
            if f == 1:
                total = total + ret[part].astype(F32)
            out[f] = total.astype(BF)
    shape = (8, GRID * 16)
    pick = iota(shape, 1) % 16 == 8 + half * 4 + iota(shape, 0)
    w_out[...] = nn(pick.astype(F32).astype(BF), arrived)[:4]


def on_device(
    queries, key_vectors, value_vectors, w_out, rig_tiles, rig_count, strip_rows, cotangent
):
    cam = lax.axis_index("cam")
    tm = lax.axis_index("tm")
    ring = cam % RING
    info = jnp.stack([tm, cam]).astype(jnp.int32)
    strip_rows = strip_rows.T

    q = queries.reshape(2, TILE, D)
    k = key_vectors.reshape(2, TILE, D)
    v = value_vectors.reshape(2, TILE, D)
    cot = cotangent.reshape(2, TILE, D)

    plane = [[p * RING + z for p in range(GRID)] for z in range(RING)]

    def exchange(block):
        return lax.all_to_all(block, "cam", 0, 0, axis_index_groups=plane, tiled=True)

    def along_ring(block, shift):
        route = [
            (p * RING + z, p * RING + (z + shift) % RING)
            for p in range(GRID)
            for z in range(RING)
        ]
        return lax.ppermute(block, "cam", route)

    rigs = lax.dynamic_index_in_dim(rig_tiles.reshape(GRID, RING, 7), ring, 1, keepdims=False)
    counts = lax.dynamic_index_in_dim(rig_count.reshape(GRID, RING), ring, 1, keepdims=False)
    rigs = jnp.where(jnp.arange(7, dtype=jnp.int32) < counts[:, None], rigs, -1)
    rigs = jnp.pad(rigs, ((0, 0), (0, 1)), constant_values=-1)
    rowid = jnp.broadcast_to(rigs[:, None], (GRID, 4, SLOTS)).reshape(-1)

    pair = lambda i, *_: (0, 0, i)
    row = lambda i, *_: (i, 0)
    head = lambda i, *_: (i, 0, 0)
    head4 = lambda i, *_: (i, 0, 0, 0)
    blk = (2, TILE, WIDE)
    stats, sblk = like((PAIRS, 2, WIDE), F32), (2, 2, WIDE)
    heads, hblk = like((PAIRS, 2, TILE, TILE), F32), (2, 2, TILE, TILE)
    act = like((2, TILE, D))

    mine, last = call(
        extract_body,
        (1,),
        [info, strip_rows, (k, None, None), (v, None, None)],
        [(like((GRID * 8, 512)), None, None), (act, None, None)],
        60,
        1 << 27,
        2 << 20,
        scalars=2,
    )
    prev = lax.ppermute(last, "tm", [(i, i + 1) for i in range(3)])
    t0 = exchange(mine.reshape(GRID, 8, 512)).reshape(GRID * 8, 512)
    t1, t2, t3 = [along_ring(t0, s) for s in (1, 2, 3)]

    g, gt = call(
        grad_body,
        (BLOCKS,),
        [(cot, None, None), (w_out, (WIDE, D), row)],
        [(act, blk, pair), (like((D, WIDE)), (WIDE, WIDE), row)],
        60,
        1 << 30,
        4 << 20,
        scalars=0,
    )
    m1, l1, o1 = call(
        local_body,
        (BLOCKS,),
        [
            info,
            (q, blk, pair),
            (k, blk, pair),
            (v, blk, pair),
            (prev, blk, pair),
            (t0, AFTER, None),
        ],
        [
            (stats, sblk, head),
            (stats, sblk, head),
            (heads, hblk, head4),
        ],
        60,
        1 << 30,
        4 << 20,
    )

    (sends,) = call(
        select_body,
        (1,),
        [info, (rowid.reshape(-1, 1), None, None)]
        + [(t, None, None) for t in (t0, t1, t2, t3)]
        + [(m1, AFTER, None)],
        [(like((GRID * 4 * SLOTS, D)), None, None)],
        60,
        1 << 29,
        2 << 20,
    )
    (cot0,) = call(
        copy_body,
        (1,),
        [(cot, None, None), (sends, AFTER, None)],
        [(act, None, None)],
        60,
        1 << 20,
        1 << 20,
        scalars=0,
    )
    cot1 = lax.ppermute(cot0, "tm", [(t, t ^ 1) for t in range(4)])
    cot2 = lax.ppermute(cot0, "tm", [(t, t ^ 2) for t in range(4)])
    cot3 = lax.ppermute(cot2, "tm", [(t, t ^ 1) for t in range(4)])
    strips = exchange(sends.reshape(GRID, 4 * SLOTS, D)).reshape(GRID, 4, SLOTS, D)

    def block_of(i, info):
        return info[TM] ^ i

    opair = lambda i, info, _: (0, 0, block_of(i, info))
    orow = lambda i, info, _: (block_of(i, info), 0)
    ohead = lambda i, info, _: (block_of(i, info), 0, 0)
    ohead4 = lambda i, info, _: (block_of(i, info), 0, 0, 0)
    gblk = (GRID, 4, SLOTS, WIDE)
    gpair = lambda i, info, _: (0, 0, 0, block_of(i, info))
    back, m, rl, delta, dq, *ots = call(
        strip_body,
        (BLOCKS,),
        [
            info,
            rig_count,
            (q, blk, opair),
            (g, blk, opair),
            (gt, (WIDE, WIDE), orow),
            (strips, gblk, gpair),
            (m1, sblk, ohead),
            (l1, sblk, ohead),
            (o1, hblk, ohead4),
            (cot2, AFTER, None),
        ],
        [
            (like((GRID, 4, SLOTS, D)), gblk, gpair),
            (stats, sblk, ohead),
            (stats, sblk, ohead),
            (stats, sblk, ohead),
            (heads, hblk, ohead4),
        ]
        + [(like((WIDE, WIDE)), None, None)] * 4,
        60,
        2 << 30,
        10 << 20,
        scalars=2,
    )
    own_ots = ots
    ots = [ots[0]] + [
        lax.ppermute(ots[i], "tm", [(t, t ^ i) for t in range(4)]) for i in (1, 2, 3)
    ]
    front, wide = (1, TILE, 4 * TILE), (2, TILE, 4 * TILE)
    wstat = (4, 2, WIDE)
    ret, dq0 = call(
        before_body,
        (2,),
        [
            info,
            (q, front, pair),
            (prev, wide, pair),
            (g, front, pair),
            (m, wstat, head),
            (rl, wstat, head),
            (delta, wstat, head),
            (dq, (4, 1, TILE, TILE), head4),
        ],
        [(act, wide, pair), (like((PAIRS, TILE, TILE), F32), (4, TILE, TILE), head)],
        60,
        1 << 29,
        4 << 20,
    )
    returned = lax.ppermute(ret, "tm", [(i + 1, i) for i in range(3)])
    b = exchange(back.reshape(GRID, 4 * SLOTS, D)).reshape(GRID * 4 * SLOTS, D)

    piece = (like((GRID * 8, 512)), None, None)
    es = call(
        weight_body,
        (1,),
        [info] + [(o, None, None) for o in (cot, cot1, cot2, cot3, *ots)] + [(ret, AFTER, None)],
        [piece] * 4,
        60,
        1 << 30,
        6 << 20,
    )
    es = [es[0]] + [along_ring(es[s], -s) for s in (1, 2, 3)]

    zs = call(
        sum_body,
        (1,),
        [info, (rowid.reshape(1, -1), None, None), (b, None, None)],
        [piece] * 4,
        10,
        1 << 29,
        2 << 20,
    )
    pieces = [zs[0]] + [along_ring(zs[s], -s) for s in (1, 2, 3)]

    gq, gk, gv = call(
        back_body,
        (BLOCKS,),
        [
            info,
            (q, blk, pair),
            (k, blk, pair),
            (v, blk, pair),
            (g, blk, pair),
            (m, sblk, head),
            (rl, sblk, head),
            (delta, sblk, head),
            (dq0, (2, TILE, TILE), head),
            (dq, (2, 1, TILE, TILE), lambda i, *_: (i, 1, 0, 0)),
            (pieces[1], AFTER, None),
        ]
        + [(e, AFTER, None) for e in es[1:]],
        [
            (act, blk, pair),
            (like((2, TILE, D), F32), blk, pair),
            (like((2, TILE, D), F32), blk, pair),
        ],
        60,
        2 << 30,
        8 << 20,
    )

    (summed,) = call(
        merge_body,
        (1,),
        [(x.reshape(GRID, 8, 512), None, None) for x in pieces + es] + [(gq, AFTER, None)],
        [(like((GRID, 16, 512)), None, None)],
        60,
        1 << 20,
        1 << 20,
        scalars=0,
    )
    arrived = exchange(summed).reshape(GRID * 16, 512)
    (mixed,) = call(
        mixed_body,
        (2,),
        [info]
        + [(o, None, None) for o in own_ots]
        + [(w_out, (D, 512), lambda i, *_: (0, i)), (summed, AFTER, None)],
        [(act, (2, TILE, 512), pair)],
        60,
        1 << 29,
        4 << 20,
    )

    quarter = (2, TILE, 256)
    grad_k, grad_v, grad_w = call(
        final_body,
        (4,),
        [
            info,
            strip_rows,
            (gk, quarter, pair),
            (gv, quarter, pair),
            (returned, quarter, pair),
            (arrived, (GRID * 16, 256), lambda i, *_: (0, i % 2)),
        ],
        [
            (act, quarter, pair),
            (act, quarter, pair),
            (like((4, D), F32), (4, 256), lambda i, *_: (0, i)),
        ],
        60,
        1 << 27,
        4 << 20,
        scalars=2,
    )
    whole = (2, 1, TILE, D)
    return (
        mixed.reshape(whole),
        gq.reshape(whole),
        grad_k.reshape(whole),
        grad_v.reshape(whole),
        grad_w,
    )


def solution(mesh):
    block = P("tm", "cam", None, None)
    return jax.shard_map(
        on_device,
        mesh=mesh,
        in_specs=(block, block, block, P(), P(), P(), P(), block),
        out_specs=(block, block, block, block, P(("tm", "cam"), None)),
        check_vma=False,
    )
```

time: 167 us -> 157 us (0.940)
  waiting for transfers between devices: 48.7 us -> 29.6 us
  Pallas kernels: 44.3 us -> 58.1 us
  local copies, waits for them, and re-layouts: 22.4 us -> 8.98 us
  starting transfers between devices: 46.5 us -> 57.6 us
  other arithmetic: 2.93 us -> 0.62 us
    all_to_all x4, waiting for transfers between devices: 31.4 us -> 11 us  [exchange(): lax.all_to_all(block, 'cam', 0, 0, axis_index_groups=plane, tiled=True)]
    pallas_call x7 -> x13, Pallas kernels: 44.3 us -> 58.1 us  [call(): pl.pallas_call(body, grid_spec=pltpu.PrefetchScalarGridSpec(num_scalar_pr...]
    unnamed x52 -> x55, local copies, waits for them, and re-layouts: 18.1 us -> 6.05 us
    ppermute x2 -> x6, waiting for transfers between devices: 0.01 us -> 9.18 us  [the longest x1 7.6 us: on_device(): cot2 = lax.ppermute(cot0, 'tm', [(t, t ^ 2) for t in range(4)])]
    ppermute x1, waiting for transfers between devices: 8.78 us -> 0.01 us  [on_device(): prev = lax.ppermute(last, 'tm', [(i, i + 1) for i in range(3)])]
    ppermute x2 -> x6, starting transfers between devices: 0.01 us -> 4.9 us  [the longest x1 2.42 us: on_device(): cot2 = lax.ppermute(cot0, 'tm', [(t, t ^ 2) for t in range(4)])]
    ppermute x6 -> x9, starting transfers between devices: 18.2 us -> 22.6 us  [along_ring(): return lax.ppermute(block, 'cam', route)]
    convert_element_type x1 -> x0, other arithmetic: 2.04 us -> none  [on_device(): (w_keep[:2].astype(F32) + came[:2].astype(F32)).astype(BF)]
  transfers between devices with their start and end apart: 14 -> 21, of which waited for: 8 -> 10; matrix products, arithmetic and copies ran while one was open for 3% -> 2% of each run, Pallas kernels for 13% -> 24%
where the time goes in v2:
time: 157 us; the launch traced here: 156 us
  Pallas kernels  58.1 us (37%)
  starting transfers between devices  57.6 us (37%)
  waiting for transfers between devices  29.6 us (19%)
  local copies, waits for them, and re-layouts  8.98 us (6%)
    pallas_call x13, Pallas kernels, call(): pl.pallas_call(body, grid_spec=pltpu.PrefetchScalarGridSpec(num_scalar_pr...  58.1 us
    all_to_all x4, starting transfers between devices, exchange(): lax.all_to_all(block, 'cam', 0, 0, axis_index_groups=plane, tiled=True)  25.5 us
    ppermute x9, starting transfers between devices, along_ring(): return lax.ppermute(block, 'cam', route)  22.6 us
    all_to_all x4, waiting for transfers between devices, exchange(): lax.all_to_all(block, 'cam', 0, 0, axis_index_groups=plane, tiled=True)  11 us
    ppermute x9, waiting for transfers between devices, along_ring(): return lax.ppermute(block, 'cam', route)  9.45 us
    ppermute x1, waiting for transfers between devices, on_device(): cot2 = lax.ppermute(cot0, 'tm', [(t, t ^ 2) for t in range(4)])  7.6 us
    unnamed x55, local copies, waits for them, and re-layouts  6.05 us
  transfers between devices with their start and end apart: 21, of which 10 were waited for; matrix products, arithmetic and copies ran while one was open for 2% of the time, Pallas kernels for 24%

profile of v2, /device:TPU:32, one launch (start us, length us, event | category | flops | bytes accessed | tf_op | source)
XLA Modules:
  0.0 155.9 jit_solution(3299743250974142590)
XLA Ops:
  1.2 3.0 %shard_map.120 = (bf16[128,512]{1,0:T(8,128)(2,1)}, bf16[2,128,1024]{2,1,0:T(8,128)(2,1)}) custom-call(s32[2]{0:T(128)} %pad_add_fusion.info, s32[16,64]{1,0:T(8,128)} %bitcast.70, bf16[2,128,1024]{2,1,0:T(8,128)(2,1)} %bitcast.43, bf16[2,128,1024]{2,1,0:T(8,128)(2,1)} %bitcast.46), custom_call_target="tpu_custom_call" | custom-call | flops 134217728 | bytes 2097152 | tf_op jit(solution)/shard_map/pallas_call | solution.py:53
  4.3 1.9 %collective-permute-start.3 = (bf16[2,128,1024]{2,1,0:T(8,128)(2,1)}, bf16[2,128,1024]{2,1,0:T(8,128)(2,1)S(1)}, u32[]{:S(2)}, u32[]{:S(2)}) collective-permute-start(bf16[2,128,1024]{2,1,0:T(8,128)(2,1)} %get-tuple-element.40), channel_id=1, source_target_pairs={{0,64},{64,128},{128,192},{1,65},{65,129},{129,193},{2,66},{66,130... | collective-permute-start | bytes 1572872 | tf_op jit(solution)/shard_map/ppermute | solution.py:356
  6.2 7.1 %all-to-all-start = ((bf16[16,8,512]{2,1,0:T(8,128)(2,1)}), bf16[16,8,512]{2,1,0:T(8,128)(2,1)S(1)}, u32[]{:S(2)}, u32[]{:S(2)}) async-start(bf16[16,8,512]{2,1,0:T(8,128)(2,1)} %bitcast.69), calls=%async_computation | async-start | bytes 262144 | tf_op jit(solution)/shard_map/all_to_all | solution.py:321
  13.3 0.7 reshape.88
  14.0 0.8 reshape.89
  15.3 6.0 %all-to-all-done = bf16[16,8,512]{2,1,0:T(8,128)(2,1)S(1)} async-done(((bf16[16,8,512]{2,1,0:T(8,128)(2,1)}), bf16[16,8,512]{2,1,0:T(8,128)(2,1)S(1)}, u32[]{:S(2)}, u32[]{:S(2)}) %all-to-all-start) | async-done | bytes 131104 | tf_op jit(solution)/shard_map/all_to_all | solution.py:321
  21.3 5.4 %collective-permute-start.2 = (bf16[128,512]{1,0:T(8,128)(2,1)S(1)}, bf16[128,512]{1,0:T(8,128)(2,1)S(1)}, u32[]{:S(2)}, u32[]{:S(2)}) collective-permute-start(bf16[128,512]{1,0:T(8,128)(2,1)S(1)} %bitcast.64), channel_id=1, source_target_pairs={{0,3},{1,0},{2,1},{3,2},{4,7},{5,4},{6,5},{7,6},{8,11},{9,8},{10,9... | collective-permute-start | bytes 393224 | tf_op jit(solution)/shard_map/ppermute | solution.py:329
  26.7 1.4 collective-permute-start.1
  28.1 2.4 %collective-permute-start = (bf16[128,512]{1,0:T(8,128)(2,1)S(1)}, bf16[128,512]{1,0:T(8,128)(2,1)S(1)}, u32[]{:S(2)}, u32[]{:S(2)}) collective-permute-start(bf16[128,512]{1,0:T(8,128)(2,1)S(1)} %bitcast.66), channel_id=1, source_target_pairs={{0,1},{1,2},{2,3},{3,0},{4,5},{5,6},{6,7},{7,4},{8,9},{9,10},{10,1... | collective-permute-start | bytes 393224 | tf_op jit(solution)/shard_map/ppermute | solution.py:329
  30.6 0.8 reshape_reshape.8.rowid
  31.4 0.8 copy-done.5
  32.2 5.7 %shard_map.121 = (f32[8,2,256]{2,1,0:T(2,128)}, f32[8,2,256]{2,1,0:T(2,128)}, f32[8,2,128,128]{3,2,1,0:T(8,128)}) custom-call(s32[2]{0:T(128)} %pad_add_fusion.info, bf16[2,128,1024]{2,1,0:T(8,128)(2,1)} %bitcast.52, bf16[2,128,1024]{2,1,0:T(8,128)(2,1)} %bitcast.44, bf16[2,128,1024]{2,1,0:T(8,128)(2,1)} %bitcast.47, bf16[2,128,1024]{2,1,0:T(8,128)(2,1)} %copy-done.5, ...), custom_call_target="tpu_custom_call" | custom-call | flops 1073741824 | bytes 4194304 | tf_op jit(solution)/shard_map/pallas_call | solution.py:53
  38.0 1.5 collective-permute-done.1.t2
  40.2 3.6 %shard_map.122._ = bf16[512,1024]{1,0:T(8,128)(2,1)} custom-call(s32[2]{0:T(128)} %pad_add_fusion.info, s32[512,1]{1,0:T(8,128)} %reshape_reshape.8.rowid, bf16[128,512]{1,0:T(8,128)(2,1)} %bitcast.68, bf16[128,512]{1,0:T(8,128)(2,1)} %copy-done.26, bf16[128,512]{1,0:T(8,128)(2,1)} %copy-done.24, bf16[128,512]{1,0:T(8,128)(2,1)} %copy-done.22, ...), custom_call_target="tpu_custom_call" | custom-call | flops 536870912 | bytes 2097152 | tf_op jit(solution)/shard_map/pallas_call | solution.py:53
  43.8 4.2 %all-to-all-start.1 = ((bf16[16,32,1024]{2,1,0:T(8,128)(2,1)}), bf16[16,32,1024]{2,1,0:T(8,128)(2,1)S(1)}, u32[]{:S(2)}, u32[]{:S(2)}) async-start(bf16[16,32,1024]{2,1,0:T(8,128)(2,1)} %bitcast.38), calls=%async_computation.1 | async-start | bytes 2097152 | tf_op jit(solution)/shard_map/all_to_all | solution.py:321
  48.0 1.9 %shard_map.123 = bf16[2,128,1024]{2,1,0:T(8,128)(2,1)} custom-call(bf16[2,128,1024]{2,1,0:T(8,128)(2,1)} %bitcast.49, bf16[512,1024]{1,0:T(8,128)(2,1)} %shard_map.122._), custom_call_target="tpu_custom_call" | custom-call | flops 1048576 | bytes 1048576 | tf_op jit(solution)/shard_map/pallas_call | solution.py:53
  49.9 2.4 %collective-permute-start.4 = (bf16[2,128,1024]{2,1,0:T(8,128)(2,1)}, bf16[2,128,1024]{2,1,0:T(8,128)(2,1)S(1)}, u32[]{:S(2)}, u32[]{:S(2)}) collective-permute-start(bf16[2,128,1024]{2,1,0:T(8,128)(2,1)} %shard_map.123), channel_id=1, source_target_pairs={{0,128},{64,192},{128,0},{192,64},{1,129},{65,193},{129,1},{193,65... | collective-permute-start | bytes 1572872 | tf_op jit(solution)/shard_map/ppermute | solution.py:413
  52.3 4.6 %shard_map.119 = (bf16[2,128,1024]{2,1,0:T(8,128)(2,1)}, bf16[1024,256]{1,0:T(8,128)(2,1)}) custom-call(bf16[2,128,1024]{2,1,0:T(8,128)(2,1)} %bitcast.50, bf16[1024,1024]{1,0:T(8,128)(2,1)} %w.3), custom_call_target="tpu_custom_call" | custom-call | flops 1073741824 | bytes 4194304 | tf_op jit(solution)/shard_map/pallas_call | solution.py:53
  57.0 7.6 %collective-permute-done.4._.c2 = bf16[2,128,1024]{2,1,0:T(8,128)(2,1)S(1)} collective-permute-done((bf16[2,128,1024]{2,1,0:T(8,128)(2,1)}, bf16[2,128,1024]{2,1,0:T(8,128)(2,1)S(1)}, u32[]{:S(2)}, u32[]{:S(2)}) %collective-permute-start.4) | collective-permute-done | bytes 524320 | tf_op jit(solution)/shard_map/ppermute | solution.py:413
  64.6 0.8 copy-done.18
  65.7 9.5 %shard_map.124 = (bf16[16,4,8,1024]{3,2,1,0:T(8,128)(2,1)}, f32[8,2,256]{2,1,0:T(2,128)}, f32[8,2,256]{2,1,0:T(2,128)}, f32[8,2,256]{2,1,0:T(2,128)}, f32[8,2,12...) custom-call(s32[2]{0:T(128)} %pad_add_fusion.info, ...), custom_call_target="tpu_custom_call" | custom-call | flops 2147483648 | bytes 10485760 | tf_op jit(solution)/shard_map/pallas_call | solution.py:53
  75.3 7.0 %all-to-all-start.2 = ((bf16[16,32,1024]{2,1,0:T(8,128)(2,1)}), bf16[16,32,1024]{2,1,0:T(8,128)(2,1)S(1)}, u32[]{:S(2)}, u32[]{:S(2)}) async-start(bf16[16,32,1024]{2,1,0:T(8,128)(2,1)} %bitcast.40), calls=%async_computation.2 | async-start | bytes 2097152 | tf_op jit(solution)/shard_map/all_to_all | solution.py:321
  83.0 1.7 %collective-permute-start.11 = (bf16[256,256]{1,0:T(8,128)(2,1)S(1)}, bf16[256,256]{1,0:T(8,128)(2,1)S(1)}, u32[]{:S(2)}, u32[]{:S(2)}) collective-permute-start(bf16[256,256]{1,0:T(8,128)(2,1)S(1)} %copy-done.14), channel_id=1, source_target_pairs={{0,128},{64,192},{128,0},{192,64},{1,129},{65,193},{129,1},{193,65... | collective-permute-start | bytes 393224 | tf_op jit(solution)/shard_map/ppermute | solution.py:456
  84.9 4.6 %shard_map.126 = (bf16[2,128,1024]{2,1,0:T(8,128)(2,1)}, f32[8,128,128]{2,1,0:T(8,128)}) custom-call(s32[2]{0:T(128)} %pad_add_fusion.info, bf16[2,128,1024]{2,1,0:T(8,128)(2,1)} %bitcast.54, bf16[2,128,1024]{2,1,0:T(8,128)(2,1)} %copy-done.5, bf16[2,128,1024]{2,1,0:T(8,128)(2,1)} %get-tuple-element.37.g, f32[8,2,256]{2,1,0:T(2,128)} %get-tuple-element.53.m, ...), custom_call_target="tpu_custom_call" | custom-call | flops 536870912 | bytes 4194304 | tf_op jit(solution)/shard_map/pallas_call | solution.py:53
  89.6 1.6 %collective-permute-done.12.ot3 = bf16[256,256]{1,0:T(8,128)(2,1)S(1)} collective-permute-done((bf16[256,256]{1,0:T(8,128)(2,1)S(1)}, bf16[256,256]{1,0:T(8,128)(2,1)S(1)}, u32[]{:S(2)}, u32[]{:S(2)}) %collective-permute-start.12) | collective-permute-done | bytes 131104 | tf_op jit(solution)/shard_map/ppermute | solution.py:456
  91.8 4.4 %shard_map.127 = (bf16[128,512]{1,0:T(8,128)(2,1)}, bf16[128,512]{1,0:T(8,128)(2,1)}, bf16[128,512]{1,0:T(8,128)(2,1)}, bf16[128,512]{1,0:T(8,128)(2,1)}) custom-call(s32[2]{0:T(128)} %pad_add_fusion.info, bf16[2,128,1024]{2,1,0:T(8,128)(2,1)} %bitcast.51, bf16[2,128,1024]{2,1,0:T(8,128)(2,1)} %copy-done.20, bf16[2,128,1024]{2,1,0:T(8,128)(2,1)} %copy-done.18, ...), custom_call_target="tpu_custom_call" | custom-call | flops 1073741824 | bytes 6291456 | tf_op jit(solution)/shard_map/pallas_call | solution.py:53
  96.2 3.7 %collective-permute-start.13 = (bf16[128,512]{1,0:T(8,128)(2,1)}, bf16[128,512]{1,0:T(8,128)(2,1)S(1)}, u32[]{:S(2)}, u32[]{:S(2)}) collective-permute-start(bf16[128,512]{1,0:T(8,128)(2,1)} %get-tuple-element.59), channel_id=1, source_target_pairs={{0,3},{1,0},{2,1},{3,2},{4,7},{5,4},{6,5},{7,6},{8,11},{9,8},{10,9... | collective-permute-start | bytes 393224 | tf_op jit(solution)/shard_map/ppermute | solution.py:329
  99.9 1.4 collective-permute-start.14
  101.3 1.1 collective-permute-start.15
  102.3 1.4 shard_map.125
  103.8 0.6 copy-done
  104.4 3.1 %collective-permute-start.5 = (bf16[128,512]{1,0:T(8,128)(2,1)S(1)}, bf16[128,512]{1,0:T(8,128)(2,1)S(1)}, u32[]{:S(2)}, u32[]{:S(2)}) collective-permute-start(bf16[128,512]{1,0:T(8,128)(2,1)S(1)} %get-tuple-element.50), channel_id=1, source_target_pairs={{0,3},{1,0},{2,1},{3,2},{4,7},{5,4},{6,5},{7,6},{8,11},{9,8},{10,9... | collective-permute-start | bytes 393224 | tf_op jit(solution)/shard_map/ppermute | solution.py:329
  107.5 2.7 %collective-permute-start.16 = (bf16[2,128,1024]{2,1,0:T(8,128)(2,1)S(1)}, bf16[2,128,1024]{2,1,0:T(8,128)(2,1)S(1)}, u32[]{:S(2)}, u32[]{:S(2)}) collective-permute-start(bf16[2,128,1024]{2,1,0:T(8,128)(2,1)S(1)} %copy-done.17), channel_id=1, source_target_pairs={{64,0},{128,64},{192,128},{65,1},{129,65},{193,129},{66,2},{130,66... | collective-permute-start | bytes 1572872 | tf_op jit(solution)/shard_map/ppermute | solution.py:478
  110.1 1.3 collective-permute-done.13.__
  111.4 3.4 %collective-permute-start.6 = (bf16[128,512]{1,0:T(8,128)(2,1)S(1)}, bf16[128,512]{1,0:T(8,128)(2,1)S(1)}, u32[]{:S(2)}, u32[]{:S(2)}) collective-permute-start(bf16[128,512]{1,0:T(8,128)(2,1)S(1)} %get-tuple-element.51), channel_id=1, source_target_pairs={{0,2},{1,3},{2,0},{3,1},{4,6},{5,7},{6,4},{7,5},{8,10},{9,11},{10,... | collective-permute-start | bytes 393224 | tf_op jit(solution)/shard_map/ppermute | solution.py:329
  114.8 2.6 %collective-permute-done.14.___ = bf16[128,512]{1,0:T(8,128)(2,1)S(1)} collective-permute-done((bf16[128,512]{1,0:T(8,128)(2,1)}, bf16[128,512]{1,0:T(8,128)(2,1)S(1)}, u32[]{:S(2)}, u32[]{:S(2)}) %collective-permute-start.14) | collective-permute-done | bytes 131104 | tf_op jit(solution)/shard_map/ppermute | solution.py:329
  117.5 0.8 collective-permute-start.7
  118.3 1.3 collective-permute-done.5._
  119.6 0.6 copy-done.10
  120.2 8.6 %shard_map.128 = (bf16[2,128,1024]{2,1,0:T(8,128)(2,1)}, f32[2,128,1024]{2,1,0:T(8,128)}, f32[2,128,1024]{2,1,0:T(8,128)}) custom-call(s32[2]{0:T(128)} %pad_add_fusion.info, bf16[2,128,1024]{2,1,0:T(8,128)(2,1)} %bitcast.55, bf16[2,128,1024]{2,1,0:T(8,128)(2,1)} %bitcast.45, bf16[2,128,1024]{2,1,0:T(8,128)(2,1)} %bitcast.48, ...), custom_call_target="tpu_custom_call" | custom-call | flops 2147483648 | bytes 8388608 | tf_op jit(solution)/shard_map/pallas_call | solution.py:53
  128.8 2.6 %collective-permute-done.6 = bf16[128,512]{1,0:T(8,128)(2,1)S(1)} collective-permute-done((bf16[128,512]{1,0:T(8,128)(2,1)S(1)}, bf16[128,512]{1,0:T(8,128)(2,1)S(1)}, u32[]{:S(2)}, u32[]{:S(2)}) %collective-permute-start.6) | collective-permute-done | bytes 131104 | tf_op jit(solution)/shard_map/ppermute | solution.py:329
  131.4 0.6 copy-done.11
  132.1 2.1 %shard_map.129._ = bf16[16,16,512]{2,1,0:T(8,128)(2,1)} custom-call(bf16[16,8,512]{2,1,0:T(8,128)(2,1)} %bitcast.37, bf16[16,8,512]{2,1,0:T(8,128)(2,1)} %bitcast.61, bf16[16,8,512]{2,1,0:T(8,128)(2,1)} %bitcast.62, bf16[16,8,512]{2,1,0:T(8,128)(2,1)} %bitcast.63, bf16[16,8,512]{2,1,0:T(8,128)(2,1)} %bitcast.57, bf16[16,8,512]{2,1,0:T(8,128)(2,1)} %bitcast.58, ...), custom_call_target="tpu_custom_call" | custom-call | flops 1048576 | bytes 1048576 | tf_op jit(solution)/shard_map/pallas_call | solution.py:53
  134.2 7.2 %all-to-all-start.3 = ((bf16[16,16,512]{2,1,0:T(8,128)(2,1)}), bf16[16,16,512]{2,1,0:T(8,128)(2,1)S(1)}, u32[]{:S(2)}, u32[]{:S(2)}) async-start(bf16[16,16,512]{2,1,0:T(8,128)(2,1)} %shard_map.129._), calls=%async_computation.3 | async-start | bytes 524288 | tf_op jit(solution)/shard_map/all_to_all | solution.py:321
  141.5 3.7 %shard_map.130 = bf16[2,128,1024]{2,1,0:T(8,128)(2,1)} custom-call(s32[2]{0:T(128)} %pad_add_fusion.info, bf16[256,256]{1,0:T(8,128)(2,1)} %get-tuple-element.44.ot0, bf16[256,256]{1,0:T(8,128)(2,1)} %get-tuple-element.45.ot1, bf16[256,256]{1,0:T(8,128)(2,1)} %get-tuple-element.46.ot2, bf16[256,256]{1,0:T(8,128)(2,1)} %get-tuple-element.47.ot3, ...), custom_call_target="tpu_custom_call" | custom-call | flops 536870912 | bytes 4194304 | tf_op jit(solution)/shard_map/pallas_call | solution.py:53
  145.2 5.0 %all-to-all-done.3 = bf16[16,16,512]{2,1,0:T(8,128)(2,1)S(1)} async-done(((bf16[16,16,512]{2,1,0:T(8,128)(2,1)}), bf16[16,16,512]{2,1,0:T(8,128)(2,1)S(1)}, u32[]{:S(2)}, u32[]{:S(2)}) %all-to-all-start.3) | async-done | bytes 262176 | tf_op jit(solution)/shard_map/all_to_all | solution.py:321
  150.2 0.7 copy-done.2
  150.8 5.0 %shard_map.131 = (bf16[2,128,1024]{2,1,0:T(8,128)(2,1)}, bf16[2,128,1024]{2,1,0:T(8,128)(2,1)}, f32[4,1024]{1,0:T(4,128)}) custom-call(s32[2]{0:T(128)} %pad_add_fusion.info, s32[16,64]{1,0:T(8,128)} %bitcast.71, f32[2,128,1024]{2,1,0:T(8,128)} %get-tuple-element.64.gk, f32[2,128,1024]{2,1,0:T(8,128)} %get-tuple-element.65.gv, ...), custom_call_target="tpu_custom_call" | custom-call | flops 134217728 | bytes 4194304 | tf_op jit(solution)/shard_map/pallas_call | solution.py:53
  (72 shorter events, 4.0 us)
Async XLA Ops:
  4.3 27.1 %collective-permute-start.3 = (bf16[2,128,1024]{2,1,0:T(8,128)(2,1)}, bf16[2,128,1024]{2,1,0:T(8,128)(2,1)S(1)}, u32[]{:S(2)}, u32[]{:S(2)}) collective-permute-start(bf16[2,128,1024]{2,1,0:T(8,128)(2,1)} %get-tuple-element.40), channel_id=1, source_target_pairs={{0,64},{64,128},{128,192},{1,65},{65,129},{129,193},{2,66},{66,130... | collective-permute-start | bytes 1572872 | tf_op jit(solution)/shard_map/ppermute | solution.py:356
  6.2 15.0 %all-to-all-start = ((bf16[16,8,512]{2,1,0:T(8,128)(2,1)}), bf16[16,8,512]{2,1,0:T(8,128)(2,1)S(1)}, u32[]{:S(2)}, u32[]{:S(2)}) async-start(bf16[16,8,512]{2,1,0:T(8,128)(2,1)} %bitcast.69), calls=%async_computation | async-start | bytes 262144 | tf_op jit(solution)/shard_map/all_to_all | solution.py:321
  21.3 10.2 %copy-start.16 = (bf16[16,8,512]{2,1,0:T(8,128)(2,1)}, bf16[16,8,512]{2,1,0:T(8,128)(2,1)S(1)}, u32[]{:S(2)}) copy-start(bf16[16,8,512]{2,1,0:T(8,128)(2,1)S(1)} %all-to-all-done) | copy-start | bytes 393220
  21.3 16.7 %collective-permute-start.2 = (bf16[128,512]{1,0:T(8,128)(2,1)S(1)}, bf16[128,512]{1,0:T(8,128)(2,1)S(1)}, u32[]{:S(2)}, u32[]{:S(2)}) collective-permute-start(bf16[128,512]{1,0:T(8,128)(2,1)S(1)} %bitcast.64), channel_id=1, source_target_pairs={{0,3},{1,0},{2,1},{3,2},{4,7},{5,4},{6,5},{7,6},{8,11},{9,8},{10,9... | collective-permute-start | bytes 393224 | tf_op jit(solution)/shard_map/ppermute | solution.py:329
  26.7 12.8 %collective-permute-start.1 = (bf16[128,512]{1,0:T(8,128)(2,1)S(1)}, bf16[128,512]{1,0:T(8,128)(2,1)S(1)}, u32[]{:S(2)}, u32[]{:S(2)}) collective-permute-start(bf16[128,512]{1,0:T(8,128)(2,1)S(1)} %bitcast.65), channel_id=1, source_target_pairs={{0,2},{1,3},{2,0},{3,1},{4,6},{5,7},{6,4},{7,5},{8,10},{9,11},{10,... | collective-permute-start | bytes 393224 | tf_op jit(solution)/shard_map/ppermute | solution.py:329
  28.1 11.5 %collective-permute-start = (bf16[128,512]{1,0:T(8,128)(2,1)S(1)}, bf16[128,512]{1,0:T(8,128)(2,1)S(1)}, u32[]{:S(2)}, u32[]{:S(2)}) collective-permute-start(bf16[128,512]{1,0:T(8,128)(2,1)S(1)} %bitcast.66), channel_id=1, source_target_pairs={{0,1},{1,2},{2,3},{3,0},{4,5},{5,6},{6,7},{7,4},{8,9},{9,10},{10,1... | collective-permute-start | bytes 393224 | tf_op jit(solution)/shard_map/ppermute | solution.py:329
  31.4 0.8 copy-start.5
  38.0 1.6 %copy-start.22 = (bf16[128,512]{1,0:T(8,128)(2,1)}, bf16[128,512]{1,0:T(8,128)(2,1)S(1)}, u32[]{:S(2)}) copy-start(bf16[128,512]{1,0:T(8,128)(2,1)S(1)} %collective-permute-done.2.t3) | copy-start | bytes 393220
  39.5 0.7 copy-start.24
  39.6 0.7 copy-start.26
  43.8 20.7 %all-to-all-start.1 = ((bf16[16,32,1024]{2,1,0:T(8,128)(2,1)}), bf16[16,32,1024]{2,1,0:T(8,128)(2,1)S(1)}, u32[]{:S(2)}, u32[]{:S(2)}) async-start(bf16[16,32,1024]{2,1,0:T(8,128)(2,1)} %bitcast.38), calls=%async_computation.1 | async-start | bytes 2097152 | tf_op jit(solution)/shard_map/all_to_all | solution.py:321
  49.9 14.6 %collective-permute-start.4 = (bf16[2,128,1024]{2,1,0:T(8,128)(2,1)}, bf16[2,128,1024]{2,1,0:T(8,128)(2,1)S(1)}, u32[]{:S(2)}, u32[]{:S(2)}) collective-permute-start(bf16[2,128,1024]{2,1,0:T(8,128)(2,1)} %shard_map.123), channel_id=1, source_target_pairs={{0,128},{64,192},{128,0},{192,64},{1,129},{65,193},{129,1},{193,65... | collective-permute-start | bytes 1572872 | tf_op jit(solution)/shard_map/ppermute | solution.py:413
  64.6 0.8 copy-start.18
  64.6 1.2 copy-start.3
  75.2 7.1 %copy-start.6 = (bf16[2,128,1024]{2,1,0:T(8,128)(2,1)S(1)}, bf16[2,128,1024]{2,1,0:T(8,128)(2,1)}, u32[]{:S(2)}) copy-start(bf16[2,128,1024]{2,1,0:T(8,128)(2,1)} %shard_map.123) | copy-start | bytes 1572868
  75.2 7.2 %copy-start.19 = (bf16[2,128,1024]{2,1,0:T(8,128)(2,1)S(1)}, bf16[2,128,1024]{2,1,0:T(8,128)(2,1)}, u32[]{:S(2)}) copy-start(bf16[2,128,1024]{2,1,0:T(8,128)(2,1)} %copy-done.18) | copy-start | bytes 1572868
  75.2 7.7 %copy-start.13 = (bf16[256,256]{1,0:T(8,128)(2,1)S(1)}, bf16[256,256]{1,0:T(8,128)(2,1)}, u32[]{:S(2)}) copy-start(bf16[256,256]{1,0:T(8,128)(2,1)} %get-tuple-element.45.ot1) | copy-start | bytes 393220
  75.2 7.8 %copy-start.14 = (bf16[256,256]{1,0:T(8,128)(2,1)S(1)}, bf16[256,256]{1,0:T(8,128)(2,1)}, u32[]{:S(2)}) copy-start(bf16[256,256]{1,0:T(8,128)(2,1)} %get-tuple-element.46.ot2) | copy-start | bytes 393220
  75.3 9.5 %copy-start.15 = (bf16[256,256]{1,0:T(8,128)(2,1)S(1)}, bf16[256,256]{1,0:T(8,128)(2,1)}, u32[]{:S(2)}) copy-start(bf16[256,256]{1,0:T(8,128)(2,1)} %get-tuple-element.47.ot3) | copy-start | bytes 393220
  75.3 27.1 %all-to-all-start.2 = ((bf16[16,32,1024]{2,1,0:T(8,128)(2,1)}), bf16[16,32,1024]{2,1,0:T(8,128)(2,1)S(1)}, u32[]{:S(2)}, u32[]{:S(2)}) async-start(bf16[16,32,1024]{2,1,0:T(8,128)(2,1)} %bitcast.40), calls=%async_computation.2 | async-start | bytes 2097152 | tf_op jit(solution)/shard_map/all_to_all | solution.py:321
  82.3 7.2 %collective-permute-start.8 = (bf16[2,128,1024]{2,1,0:T(8,128)(2,1)S(1)}, bf16[2,128,1024]{2,1,0:T(8,128)(2,1)S(1)}, u32[]{:S(2)}, u32[]{:S(2)}) collective-permute-start(bf16[2,128,1024]{2,1,0:T(8,128)(2,1)S(1)} %copy-done.6), channel_id=1, source_target_pairs={{0,64},{64,0},{128,192},{192,128},{1,65},{65,1},{129,193},{193,129... | collective-permute-start | bytes 1572872 | tf_op jit(solution)/shard_map/ppermute | solution.py:412
  82.4 7.1 %collective-permute-start.9 = (bf16[2,128,1024]{2,1,0:T(8,128)(2,1)S(1)}, bf16[2,128,1024]{2,1,0:T(8,128)(2,1)}, u32[]{:S(2)}, u32[]{:S(2)}) collective-permute-start(bf16[2,128,1024]{2,1,0:T(8,128)(2,1)S(1)} %copy-done.19), channel_id=1, source_target_pairs={{0,64},{64,0},{128,192},{192,128},{1,65},{65,1},{129,193},{193,129... | collective-permute-start | bytes 1572872 | tf_op jit(solution)/shard_map/ppermute | solution.py:414
  82.9 6.7 %collective-permute-start.10 = (bf16[256,256]{1,0:T(8,128)(2,1)S(1)}, bf16[256,256]{1,0:T(8,128)(2,1)S(1)}, u32[]{:S(2)}, u32[]{:S(2)}) collective-permute-start(bf16[256,256]{1,0:T(8,128)(2,1)S(1)} %copy-done.13), channel_id=1, source_target_pairs={{0,64},{64,0},{128,192},{192,128},{1,65},{65,1},{129,193},{193,129... | collective-permute-start | bytes 393224 | tf_op jit(solution)/shard_map/ppermute | solution.py:456
  83.0 6.6 %collective-permute-start.11 = (bf16[256,256]{1,0:T(8,128)(2,1)S(1)}, bf16[256,256]{1,0:T(8,128)(2,1)S(1)}, u32[]{:S(2)}, u32[]{:S(2)}) collective-permute-start(bf16[256,256]{1,0:T(8,128)(2,1)S(1)} %copy-done.14), channel_id=1, source_target_pairs={{0,128},{64,192},{128,0},{192,64},{1,129},{65,193},{129,1},{193,65... | collective-permute-start | bytes 393224 | tf_op jit(solution)/shard_map/ppermute | solution.py:456
  84.7 6.5 %collective-permute-start.12 = (bf16[256,256]{1,0:T(8,128)(2,1)S(1)}, bf16[256,256]{1,0:T(8,128)(2,1)S(1)}, u32[]{:S(2)}, u32[]{:S(2)}) collective-permute-start(bf16[256,256]{1,0:T(8,128)(2,1)S(1)} %copy-done.15), channel_id=1, source_target_pairs={{0,192},{64,128},{128,64},{192,0},{1,193},{65,129},{129,65},{193,1... | collective-permute-start | bytes 393224 | tf_op jit(solution)/shard_map/ppermute | solution.py:456
  89.5 12.8 %copy-start.1 = (s32[2]{0:T(128)S(1)}, s32[2]{0:T(128)}, u32[]{:S(2)}) copy-start(s32[2]{0:T(128)} %pad_add_fusion.info) | copy-start | bytes 28
  89.5 1.6 %copy-start.20 = (bf16[2,128,1024]{2,1,0:T(8,128)(2,1)}, bf16[2,128,1024]{2,1,0:T(8,128)(2,1)S(1)}, u32[]{:S(2)}) copy-start(bf16[2,128,1024]{2,1,0:T(8,128)(2,1)S(1)} %collective-permute-done.8.c1) | copy-start | bytes 1572868
  89.6 1.6 %copy-start.21 = (bf16[256,256]{1,0:T(8,128)(2,1)}, bf16[256,256]{1,0:T(8,128)(2,1)S(1)}, u32[]{:S(2)}) copy-start(bf16[256,256]{1,0:T(8,128)(2,1)S(1)} %collective-permute-done.10.ot1) | copy-start | bytes 393220
  89.6 1.6 %copy-start.23 = (bf16[256,256]{1,0:T(8,128)(2,1)}, bf16[256,256]{1,0:T(8,128)(2,1)S(1)}, u32[]{:S(2)}) copy-start(bf16[256,256]{1,0:T(8,128)(2,1)S(1)} %collective-permute-done.11.ot2) | copy-start | bytes 393220
  91.2 0.6 copy-start.25
  91.8 15.6 %copy-start.17 = (bf16[2,128,1024]{2,1,0:T(8,128)(2,1)S(1)}, bf16[2,128,1024]{2,1,0:T(8,128)(2,1)}, u32[]{:S(2)}) copy-start(bf16[2,128,1024]{2,1,0:T(8,128)(2,1)} %get-tuple-element.57._) | copy-start | bytes 1572868
  96.2 15.2 %collective-permute-start.13 = (bf16[128,512]{1,0:T(8,128)(2,1)}, bf16[128,512]{1,0:T(8,128)(2,1)S(1)}, u32[]{:S(2)}, u32[]{:S(2)}) collective-permute-start(bf16[128,512]{1,0:T(8,128)(2,1)} %get-tuple-element.59), channel_id=1, source_target_pairs={{0,3},{1,0},{2,1},{3,2},{4,7},{5,4},{6,5},{7,6},{8,11},{9,8},{10,9... | collective-permute-start | bytes 393224 | tf_op jit(solution)/shard_map/ppermute | solution.py:329
  99.9 17.5 %collective-permute-start.14 = (bf16[128,512]{1,0:T(8,128)(2,1)}, bf16[128,512]{1,0:T(8,128)(2,1)S(1)}, u32[]{:S(2)}, u32[]{:S(2)}) collective-permute-start(bf16[128,512]{1,0:T(8,128)(2,1)} %get-tuple-element.60), channel_id=1, source_target_pairs={{0,2},{1,3},{2,0},{3,1},{4,6},{5,7},{6,4},{7,5},{8,10},{9,11},{10,... | collective-permute-start | bytes 393224 | tf_op jit(solution)/shard_map/ppermute | solution.py:329
  101.3 17.0 %collective-permute-start.15 = (bf16[128,512]{1,0:T(8,128)(2,1)}, bf16[128,512]{1,0:T(8,128)(2,1)S(1)}, u32[]{:S(2)}, u32[]{:S(2)}) collective-permute-start(bf16[128,512]{1,0:T(8,128)(2,1)} %get-tuple-element.61), channel_id=1, source_target_pairs={{0,1},{1,2},{2,3},{3,0},{4,5},{5,6},{6,7},{7,4},{8,9},{9,10},{10,1... | collective-permute-start | bytes 393224 | tf_op jit(solution)/shard_map/ppermute | solution.py:329
  103.7 0.7 copy-start
  104.4 15.2 %collective-permute-start.5 = (bf16[128,512]{1,0:T(8,128)(2,1)S(1)}, bf16[128,512]{1,0:T(8,128)(2,1)S(1)}, u32[]{:S(2)}, u32[]{:S(2)}) collective-permute-start(bf16[128,512]{1,0:T(8,128)(2,1)S(1)} %get-tuple-element.50), channel_id=1, source_target_pairs={{0,3},{1,0},{2,1},{3,2},{4,7},{5,4},{6,5},{7,6},{8,11},{9,8},{10,9... | collective-permute-start | bytes 393224 | tf_op jit(solution)/shard_map/ppermute | solution.py:329
  107.5 37.7 %collective-permute-start.16 = (bf16[2,128,1024]{2,1,0:T(8,128)(2,1)S(1)}, bf16[2,128,1024]{2,1,0:T(8,128)(2,1)S(1)}, u32[]{:S(2)}, u32[]{:S(2)}) collective-permute-start(bf16[2,128,1024]{2,1,0:T(8,128)(2,1)S(1)} %copy-done.17), channel_id=1, source_target_pairs={{64,0},{128,64},{192,128},{65,1},{129,65},{193,129},{66,2},{130,66... | collective-permute-start | bytes 1572872 | tf_op jit(solution)/shard_map/ppermute | solution.py:478
  111.4 8.2 %copy-start.7 = (bf16[128,512]{1,0:T(8,128)(2,1)}, bf16[128,512]{1,0:T(8,128)(2,1)S(1)}, u32[]{:S(2)}) copy-start(bf16[128,512]{1,0:T(8,128)(2,1)S(1)} %collective-permute-done.13.__) | copy-start | bytes 393220
  111.4 20.0 %collective-permute-start.6 = (bf16[128,512]{1,0:T(8,128)(2,1)S(1)}, bf16[128,512]{1,0:T(8,128)(2,1)S(1)}, u32[]{:S(2)}, u32[]{:S(2)}) collective-permute-start(bf16[128,512]{1,0:T(8,128)(2,1)S(1)} %get-tuple-element.51), channel_id=1, source_target_pairs={{0,2},{1,3},{2,0},{3,1},{4,6},{5,7},{6,4},{7,5},{8,10},{9,11},{10,... | collective-permute-start | bytes 393224 | tf_op jit(solution)/shard_map/ppermute | solution.py:329
  117.5 2.1 %copy-start.8 = (bf16[128,512]{1,0:T(8,128)(2,1)}, bf16[128,512]{1,0:T(8,128)(2,1)S(1)}, u32[]{:S(2)}) copy-start(bf16[128,512]{1,0:T(8,128)(2,1)S(1)} %collective-permute-done.14.___) | copy-start | bytes 393220
  117.5 14.0 %collective-permute-start.7 = (bf16[128,512]{1,0:T(8,128)(2,1)S(1)}, bf16[128,512]{1,0:T(8,128)(2,1)S(1)}, u32[]{:S(2)}, u32[]{:S(2)}) collective-permute-start(bf16[128,512]{1,0:T(8,128)(2,1)S(1)} %get-tuple-element.52), channel_id=1, source_target_pairs={{0,1},{1,2},{2,3},{3,0},{4,5},{5,6},{6,7},{7,4},{8,9},{9,10},{10,1... | collective-permute-start | bytes 393224 | tf_op jit(solution)/shard_map/ppermute | solution.py:329
  118.3 1.3 copy-start.9
  119.6 0.7 copy-start.10
  131.4 0.7 copy-start.11
  131.4 0.7 copy-start.12
  134.2 15.9 %all-to-all-start.3 = ((bf16[16,16,512]{2,1,0:T(8,128)(2,1)}), bf16[16,16,512]{2,1,0:T(8,128)(2,1)S(1)}, u32[]{:S(2)}, u32[]{:S(2)}) async-start(bf16[16,16,512]{2,1,0:T(8,128)(2,1)} %shard_map.129._), calls=%async_computation.3 | async-start | bytes 524288 | tf_op jit(solution)/shard_map/all_to_all | solution.py:321
  145.2 5.0 %copy-start.4 = (bf16[2,128,1024]{2,1,0:T(8,128)(2,1)}, bf16[2,128,1024]{2,1,0:T(8,128)(2,1)S(1)}, u32[]{:S(2)}) copy-start(bf16[2,128,1024]{2,1,0:T(8,128)(2,1)S(1)} %collective-permute-done.16.ret) | copy-start | bytes 1572868
  150.2 0.7 copy-start.2

commit v3 on v2

--- a/solution.py
+++ b/solution.py
@@ -21,7 +21,7 @@
 TM, CAM = range(2)
 BLOCKS = 4
 WIDE = 2 * TILE
-AFTER = "after"
+AFTER, NEAR, FAR = "after", "near", "far"
 
 
 def nt(a, b):
@@ -41,8 +41,18 @@
 
 
 def call(body, grid, inputs, outputs, limit_mib, flops, nbytes, scalars=1):
+    def space(entry):
+        return pltpu.VMEM if entry[-1] == NEAR else pltpu.HBM
+
+    def place(entry):
+        if not isinstance(entry, tuple):
+            return entry
+        if entry[1:] == (AFTER, None):
+            return entry[0]
+        return pltpu.with_memory_space_constraint(entry[0], space(entry))
+
     def spec(entry):
-        shape, block, index = entry
+        shape, block, index = entry[:3]
         if block == AFTER:
             return pl.BlockSpec(memory_space=pl.ANY)
         if block is None:
@@ -58,10 +68,10 @@
             in_specs=[spec(e) for e in inputs[scalars:]],
             out_specs=[spec(e) for e in outputs],
         ),
-        out_shape=[e[0] for e in outputs],
+        out_shape=[space(e)(e[0].shape, e[0].dtype) for e in outputs],
         compiler_params=pltpu.CompilerParams(vmem_limit_bytes=limit_mib * MIB),
         cost_estimate=pl.CostEstimate(flops=flops, bytes_accessed=nbytes, transcendentals=0),
-    )(*[e[0] if isinstance(e, tuple) else e for e in inputs])
+    )(*[place(e) for e in inputs])
 
 
 def like(shape, dtype=BF):
@@ -121,11 +131,8 @@
     gt_out[...] = nt(w[...], cots).astype(BF)
 
 
-def copy_body(block, _, out):
-    out[...] = block[...]
-
-
-def local_body(info, q, k, v, prev, _, m_out, l_out, o_out):
+def local_body(info, q, k, v, prev, cot, _, m_out, l_out, o_out, cot_out):
+    cot_out[...] = cot[...]
     for n, at, f in units():
         qs = stacked(q[f, :, at] * jnp.asarray(0.125, BF))
         before_k, before_v = (prev[0, :, at], prev[1, :, at]) if f == 0 else (k[0, :, at], v[0, :, at])
@@ -181,7 +188,7 @@
             out[...] = whole
 
 
-def weight_body(info, c0, c1, c2, c3, ot0, ot1, ot2, ot3, _, e0, e1, e2, e3):
+def weight_body(info, c0, c1, c2, c3, ot0, ot1, ot2, ot3, e0, e1, e2, e3):
     total = jnp.zeros((WIDE, D), F32)
     for ot, c in ((ot0, c0), (ot1, c1), (ot2, c2), (ot3, c3)):
         total += nn(ot[...], c[...].reshape(WIDE, D))
@@ -214,40 +221,32 @@
     return nn(ds, qs), nn(p.astype(BF), gs), own_half(tn(kb, ds))
 
 
-def before_body(info, q, prev, g, m, rl, delta, dq, ret_out, dq_out):
-    for n in range(4):
-        at = slice(n * TILE, n * TILE + TILE)
-        qs = stacked(q[0, :, at] * jnp.asarray(0.125, BF))
-        gs = stacked(g[0, :, at])
-        dk, dv, part = block_back(
-            prev[0, :, at], prev[1, :, at], qs, gs, m[n, :1], rl[n, :1], delta[n, :1],
-            info[TM] == 0,
-        )
-        ret_out[0, :, at] = dk.astype(BF)
-        ret_out[1, :, at] = dv.astype(BF)
-        dq_out[n] = dq[n, 0] + part
-
-
 def back_body(
-    info, q, k, v, g, m, rl, delta, dq0, dq, _, __, ___, ____, gq_out, gk_out, gv_out
+    info, q, k, v, prev, g, m, rl, delta, dq, _, gq_out, gk_out, gv_out, ret_out
 ):
+    hidden = (iota((2 * TILE, WIDE), 0) >= TILE) & (info[TM] == 0)
     for n in range(2):
         at = slice(n * TILE, n * TILE + TILE)
         for f in range(2):
             qs = stacked(q[f, :, at] * jnp.asarray(0.125, BF))
             gs = stacked(g[f, :, at])
-            stats = m[n, f : f + 1], rl[n, f : f + 1], delta[n, f : f + 1]
-            dk, dv, part = block_back(k[f, :, at], v[f, :, at], qs, gs, *stats)
+            before_k, before_v = (prev[0], prev[1]) if f == 0 else (k[0], v[0])
+            keys = jnp.concatenate([k[f, :, at], before_k[:, at]], 0)
+            values = jnp.concatenate([v[f, :, at], before_v[:, at]], 0)
+            dk, dv, part = block_back(
+                keys, values, qs, gs, m[n, f : f + 1], rl[n, f : f + 1], delta[n, f : f + 1],
+                hidden if f == 0 else None,
+            )
             if f == 0:
-                total, dk0, dv0 = dq0[n] + part, dk, dv
+                dk0, dv0 = dk[:TILE], dv[:TILE]
+                ret_out[0, :, at] = dk[TILE:].astype(BF)
+                ret_out[1, :, at] = dv[TILE:].astype(BF)
             else:
-                gk_out[1, :, at] = dk
-                gv_out[1, :, at] = dv
-                dk, dv, before = block_back(k[0, :, at], v[0, :, at], qs, gs, *stats)
-                gk_out[0, :, at] = dk0 + dk
-                gv_out[0, :, at] = dv0 + dv
-                total = dq[n, 0] + part + before
-            gq_out[f, :, at] = (total * 0.125).T.astype(BF)
+                gk_out[1, :, at] = dk[:TILE]
+                gv_out[1, :, at] = dv[:TILE]
+                gk_out[0, :, at] = dk0 + dk[TILE:]
+                gv_out[0, :, at] = dv0 + dv[TILE:]
+            gq_out[f, :, at] = ((dq[n, f] + part) * 0.125).T.astype(BF)
 
 
 def select_body(info, rowid, t0, t1, t2, t3, _, out):
@@ -348,7 +347,7 @@
         (1,),
         [info, strip_rows, (k, None, None), (v, None, None)],
         [(like((GRID * 8, 512)), None, None), (act, None, None)],
-        60,
+        6,
         1 << 27,
         2 << 20,
         scalars=2,
@@ -361,13 +360,13 @@
         grad_body,
         (BLOCKS,),
         [(cot, None, None), (w_out, (WIDE, D), row)],
-        [(act, blk, pair), (like((D, WIDE)), (WIDE, WIDE), row)],
-        60,
+        [(act, blk, pair, NEAR), (like((D, WIDE)), (WIDE, WIDE), row)],
+        8,
         1 << 30,
         4 << 20,
         scalars=0,
     )
-    m1, l1, o1 = call(
+    m1, l1, o1, cot0 = call(
         local_body,
         (BLOCKS,),
         [
@@ -376,14 +375,16 @@
             (k, blk, pair),
             (v, blk, pair),
             (prev, blk, pair),
+            (cot, blk, pair),
             (t0, AFTER, None),
         ],
         [
-            (stats, sblk, head),
-            (stats, sblk, head),
-            (heads, hblk, head4),
-        ],
-        60,
+            (stats, sblk, head, NEAR),
+            (stats, sblk, head, NEAR),
+            (heads, hblk, head4, NEAR),
+            (act, blk, pair),
+        ],
+        8,
         1 << 30,
         4 << 20,
     )
@@ -391,23 +392,13 @@
     (sends,) = call(
         select_body,
         (1,),
-        [info, (rowid.reshape(-1, 1), None, None)]
-        + [(t, None, None) for t in (t0, t1, t2, t3)]
+        [info, (rowid.reshape(-1, 1), None, None, NEAR)]
+        + [(t, None, None, NEAR) for t in (t0, t1, t2, t3)]
         + [(m1, AFTER, None)],
         [(like((GRID * 4 * SLOTS, D)), None, None)],
-        60,
+        10,
         1 << 29,
         2 << 20,
-    )
-    (cot0,) = call(
-        copy_body,
-        (1,),
-        [(cot, None, None), (sends, AFTER, None)],
-        [(act, None, None)],
-        60,
-        1 << 20,
-        1 << 20,
-        scalars=0,
     )
     cot1 = lax.ppermute(cot0, "tm", [(t, t ^ 1) for t in range(4)])
     cot2 = lax.ppermute(cot0, "tm", [(t, t ^ 2) for t in range(4)])
@@ -430,13 +421,13 @@
             info,
             rig_count,
             (q, blk, opair),
-            (g, blk, opair),
+            (g, blk, opair, NEAR),
             (gt, (WIDE, WIDE), orow),
-            (strips, gblk, gpair),
-            (m1, sblk, ohead),
-            (l1, sblk, ohead),
-            (o1, hblk, ohead4),
-            (cot2, AFTER, None),
+            (strips, gblk, gpair, NEAR),
+            (m1, sblk, ohead, NEAR),
+            (l1, sblk, ohead, NEAR),
+            (o1, hblk, ohead4, NEAR),
+            (cot3, AFTER, None),
         ],
         [
             (like((GRID, 4, SLOTS, D)), gblk, gpair),
@@ -446,54 +437,33 @@
             (heads, hblk, ohead4),
         ]
         + [(like((WIDE, WIDE)), None, None)] * 4,
-        60,
-        2 << 30,
-        10 << 20,
+        10,
+        1 << 20,
+        1 << 20,
         scalars=2,
     )
     own_ots = ots
     ots = [ots[0]] + [
         lax.ppermute(ots[i], "tm", [(t, t ^ i) for t in range(4)]) for i in (1, 2, 3)
     ]
-    front, wide = (1, TILE, 4 * TILE), (2, TILE, 4 * TILE)
-    wstat = (4, 2, WIDE)
-    ret, dq0 = call(
-        before_body,
-        (2,),
-        [
-            info,
-            (q, front, pair),
-            (prev, wide, pair),
-            (g, front, pair),
-            (m, wstat, head),
-            (rl, wstat, head),
-            (delta, wstat, head),
-            (dq, (4, 1, TILE, TILE), head4),
-        ],
-        [(act, wide, pair), (like((PAIRS, TILE, TILE), F32), (4, TILE, TILE), head)],
-        60,
-        1 << 29,
-        4 << 20,
-    )
-    returned = lax.ppermute(ret, "tm", [(i + 1, i) for i in range(3)])
     b = exchange(back.reshape(GRID, 4 * SLOTS, D)).reshape(GRID * 4 * SLOTS, D)
 
-    piece = (like((GRID * 8, 512)), None, None)
+    piece = (like((GRID * 8, 512)), None, None, NEAR)
     es = call(
         weight_body,
         (1,),
-        [info] + [(o, None, None) for o in (cot, cot1, cot2, cot3, *ots)] + [(ret, AFTER, None)],
+        [info] + [(o, None, None) for o in (cot0, cot1, cot2, cot3, *ots)],
         [piece] * 4,
-        60,
-        1 << 30,
+        12,
+        1 << 34,
         6 << 20,
     )
+
     es = [es[0]] + [along_ring(es[s], -s) for s in (1, 2, 3)]
-
     zs = call(
         sum_body,
         (1,),
-        [info, (rowid.reshape(1, -1), None, None), (b, None, None)],
+        [info, (rowid.reshape(1, -1), None, None, NEAR), (b, None, None, NEAR)],
         [piece] * 4,
         10,
         1 << 29,
@@ -501,7 +471,7 @@
     )
     pieces = [zs[0]] + [along_ring(zs[s], -s) for s in (1, 2, 3)]
 
-    gq, gk, gv = call(
+    gq, gk, gv, ret = call(
         back_body,
         (BLOCKS,),
         [
@@ -509,31 +479,32 @@
             (q, blk, pair),
             (k, blk, pair),
             (v, blk, pair),
+            (prev, blk, pair),
             (g, blk, pair),
             (m, sblk, head),
             (rl, sblk, head),
             (delta, sblk, head),
-            (dq0, (2, TILE, TILE), head),
-            (dq, (2, 1, TILE, TILE), lambda i, *_: (i, 1, 0, 0)),
-            (pieces[1], AFTER, None),
-        ]
-        + [(e, AFTER, None) for e in es[1:]],
+            (dq, hblk, head4),
+            (zs[0], AFTER, None),
+        ],
         [
             (act, blk, pair),
-            (like((2, TILE, D), F32), blk, pair),
-            (like((2, TILE, D), F32), blk, pair),
-        ],
-        60,
-        2 << 30,
+            (like((2, TILE, D), F32), blk, pair, NEAR),
+            (like((2, TILE, D), F32), blk, pair, NEAR),
+            (act, blk, pair),
+        ],
+        14,
+        1 << 30,
         8 << 20,
     )
+    returned = lax.ppermute(ret, "tm", [(i + 1, i) for i in range(3)])
 
     (summed,) = call(
         merge_body,
         (1,),
-        [(x.reshape(GRID, 8, 512), None, None) for x in pieces + es] + [(gq, AFTER, None)],
+        [(x.reshape(GRID, 8, 512), None, None, NEAR) for x in pieces + es] + [(gq, AFTER, FAR)],
         [(like((GRID, 16, 512)), None, None)],
-        60,
+        6,
         1 << 20,
         1 << 20,
         scalars=0,
@@ -546,8 +517,8 @@
         + [(o, None, None) for o in own_ots]
         + [(w_out, (D, 512), lambda i, *_: (0, i)), (summed, AFTER, None)],
         [(act, (2, TILE, 512), pair)],
-        60,
-        1 << 29,
+        8,
+        1 << 34,
         4 << 20,
     )
 
@@ -558,17 +529,17 @@
         [
             info,
             strip_rows,
-            (gk, quarter, pair),
-            (gv, quarter, pair),
-            (returned, quarter, pair),
-            (arrived, (GRID * 16, 256), lambda i, *_: (0, i % 2)),
+            (gk, quarter, pair, NEAR),
+            (gv, quarter, pair, NEAR),
+            (returned, quarter, pair, NEAR),
+            (arrived, (GRID * 16, 256), lambda i, *_: (0, i % 2), NEAR),
         ],
         [
             (act, quarter, pair),
             (act, quarter, pair),
             (like((4, D), F32), (4, 256), lambda i, *_: (0, i)),
         ],
-        60,
+        8,
         1 << 27,
         4 << 20,
         scalars=2,

time: 157 us -> 134 us (0.85)
  Pallas kernels: 58.1 us -> 44 us
  starting transfers between devices: 57.6 us -> 51.2 us
  local copies, waits for them, and re-layouts: 8.98 us -> 5.45 us
    pallas_call x13 -> x11, Pallas kernels: 58.1 us -> 44 us  [call(): pl.pallas_call(body, grid_spec=pltpu.PrefetchScalarGridSpec(num_scalar_pr...]
    all_to_all x4, waiting for transfers between devices: 11 us -> 21 us  [exchange(): lax.all_to_all(block, 'cam', 0, 0, axis_index_groups=plane, tiled=True)]
    ppermute x9, waiting for transfers between devices: 9.45 us -> 1.16 us  [along_ring(): return lax.ppermute(block, 'cam', route)]
    all_to_all x4, starting transfers between devices: 25.5 us -> 18 us  [exchange(): lax.all_to_all(block, 'cam', 0, 0, axis_index_groups=plane, tiled=True)]
    unnamed x55 -> x21, local copies, waits for them, and re-layouts: 6.05 us -> 3.22 us
    ppermute x1, waiting for transfers between devices: 7.6 us -> 5.44 us  [on_device(): cot2 = lax.ppermute(cot0, 'tm', [(t, t ^ 2) for t in range(4)])]
    ppermute x9, starting transfers between devices: 22.6 us -> 24.6 us  [along_ring(): return lax.ppermute(block, 'cam', route)]
  transfers between devices with their start and end apart: 21 -> 21, of which waited for: 10 -> 8; matrix products, arithmetic and copies ran while one was open for 2% -> 2% of each run, Pallas kernels for 24% -> 29%
where the time goes in v3:
time: 134 us; the launch traced here: 132 us
  starting transfers between devices  51.2 us (38%)
  Pallas kernels  44 us (33%)
  waiting for transfers between devices  30.5 us (23%)
  local copies, waits for them, and re-layouts  5.45 us (4%)
    pallas_call x11, Pallas kernels, call(): pl.pallas_call(body, grid_spec=pltpu.PrefetchScalarGridSpec(num_scalar_pr...  44 us
    ppermute x9, starting transfers between devices, along_ring(): return lax.ppermute(block, 'cam', route)  24.6 us
    all_to_all x4, waiting for transfers between devices, exchange(): lax.all_to_all(block, 'cam', 0, 0, axis_index_groups=plane, tiled=True)  21 us
    all_to_all x4, starting transfers between devices, exchange(): lax.all_to_all(block, 'cam', 0, 0, axis_index_groups=plane, tiled=True)  18 us
    ppermute x1, waiting for transfers between devices, on_device(): cot2 = lax.ppermute(cot0, 'tm', [(t, t ^ 2) for t in range(4)])  5.44 us
    unnamed x21, local copies, waits for them, and re-layouts  3.22 us
    ppermute x3, waiting for transfers between devices, on_device(): lax.ppermute(ots[i], 'tm', [(t, t ^ i) for t in range(4)])  2.9 us
    ppermute x1, starting transfers between devices, on_device(): returned = lax.ppermute(ret, 'tm', [(i + 1, i) for i in range(3)])  2.71 us
  transfers between devices with their start and end apart: 21, of which 8 were waited for; matrix products, arithmetic and copies ran while one was open for 2% of the time, Pallas kernels for 29%

profile of v3, /device:TPU:32, one launch (start us, length us, event | category | flops | bytes accessed | tf_op | source)
XLA Modules:
  0.0 132.2 jit_solution(5712110161178474284)
XLA Ops:
  0.7 0.7 copy-done.3
  1.4 2.9 %shard_map.120 = (bf16[128,512]{1,0:T(8,128)(2,1)}, bf16[2,128,1024]{2,1,0:T(8,128)(2,1)}) custom-call(s32[2]{0:T(128)S(1)} %pad_add_fusion.info, s32[16,64]{1,0:T(8,128)S(1)} %bitcast.52, bf16[2,128,1024]{2,1,0:T(8,128)(2,1)} %bitcast.60, bf16[2,128,1024]{2,1,0:T(8,128)(2,1)} %bitcast.63), custom_call_target="tpu_custom_call" | custom-call | flops 134217728 | bytes 2097152 | tf_op jit(solution)/shard_map/pallas_call | solution.py:63
  4.3 1.9 %collective-permute-start.3 = (bf16[2,128,1024]{2,1,0:T(8,128)(2,1)}, bf16[2,128,1024]{2,1,0:T(8,128)(2,1)S(1)}, u32[]{:S(2)}, u32[]{:S(2)}) collective-permute-start(bf16[2,128,1024]{2,1,0:T(8,128)(2,1)} %get-tuple-element.40), channel_id=1, source_target_pairs={{0,64},{64,128},{128,192},{1,65},{65,129},{129,193},{2,66},{66,130... | collective-permute-start | bytes 1572872 | tf_op jit(solution)/shard_map/ppermute | solution.py:355
  6.2 7.0 %all-to-all-start = ((bf16[16,8,512]{2,1,0:T(8,128)(2,1)}), bf16[16,8,512]{2,1,0:T(8,128)(2,1)S(1)}, u32[]{:S(2)}, u32[]{:S(2)}) async-start(bf16[16,8,512]{2,1,0:T(8,128)(2,1)} %bitcast.66), calls=%async_computation | async-start | bytes 262144 | tf_op jit(solution)/shard_map/all_to_all | solution.py:320
  13.3 0.8 reshape.89
  14.1 0.7 reshape.88
  14.8 0.2 dynamic-slice_reduce_fusion.1
  15.0 0.3 dynamic-slice_reduce_fusion
  15.3 6.0 %all-to-all-done = bf16[16,8,512]{2,1,0:T(8,128)(2,1)S(1)} async-done(((bf16[16,8,512]{2,1,0:T(8,128)(2,1)}), bf16[16,8,512]{2,1,0:T(8,128)(2,1)S(1)}, u32[]{:S(2)}, u32[]{:S(2)}) %all-to-all-start) | async-done | bytes 131104 | tf_op jit(solution)/shard_map/all_to_all | solution.py:320
  21.3 3.3 %collective-permute-start = (bf16[128,512]{1,0:T(8,128)(2,1)S(1)}, bf16[128,512]{1,0:T(8,128)(2,1)S(1)}, u32[]{:S(2)}, u32[]{:S(2)}) collective-permute-start(bf16[128,512]{1,0:T(8,128)(2,1)S(1)} %bitcast.47), channel_id=1, source_target_pairs={{0,1},{1,2},{2,3},{3,0},{4,5},{5,6},{6,7},{7,4},{8,9},{9,10},{10,1... | collective-permute-start | bytes 393224 | tf_op jit(solution)/shard_map/ppermute | solution.py:328
  24.6 4.5 %collective-permute-start.1 = (bf16[128,512]{1,0:T(8,128)(2,1)S(1)}, bf16[128,512]{1,0:T(8,128)(2,1)S(1)}, u32[]{:S(2)}, u32[]{:S(2)}) collective-permute-start(bf16[128,512]{1,0:T(8,128)(2,1)S(1)} %bitcast.48), channel_id=1, source_target_pairs={{0,2},{1,3},{2,0},{3,1},{4,6},{5,7},{6,4},{7,5},{8,10},{9,11},{10,... | collective-permute-start | bytes 393224 | tf_op jit(solution)/shard_map/ppermute | solution.py:328
  29.1 2.7 %collective-permute-start.2 = (bf16[128,512]{1,0:T(8,128)(2,1)S(1)}, bf16[128,512]{1,0:T(8,128)(2,1)S(1)}, u32[]{:S(2)}, u32[]{:S(2)}) collective-permute-start(bf16[128,512]{1,0:T(8,128)(2,1)S(1)} %bitcast.49), channel_id=1, source_target_pairs={{0,3},{1,0},{2,1},{3,2},{4,7},{5,4},{6,5},{7,6},{8,11},{9,8},{10,9... | collective-permute-start | bytes 393224 | tf_op jit(solution)/shard_map/ppermute | solution.py:328
  31.7 0.8 copy-done.6
  32.5 5.5 %shard_map.121 = (f32[8,2,256]{2,1,0:T(2,128)S(1)}, f32[8,2,256]{2,1,0:T(2,128)S(1)}, f32[8,2,128,128]{3,2,1,0:T(8,128)S(1)}, bf16[2,128,1024]{2,1,0:T(8,128)(2,1)}) custom-call(s32[2]{0:T(128)S(1)} %pad_add_fusion.info, bf16[2,128,1024]{2,1,0:T(8,128)(2,1)} %bitcast.56, bf16[2,128,1024]{2,1,0:T(8,128)(2,1)} %bitcast.61, bf16[2,128,1024]{2,1,0:T(8,128)(2,1)} %bitcast.64, ...), custom_call_target="tpu_custom_call" | custom-call | flops 1073741824 | bytes 4194304 | tf_op jit(solution)/shard_map/pallas_call | solution.py:63
  38.0 1.5 %collective-permute-start.4 = (bf16[2,128,1024]{2,1,0:T(8,128)(2,1)}, bf16[2,128,1024]{2,1,0:T(8,128)(2,1)}, u32[]{:S(2)}, u32[]{:S(2)}) collective-permute-start(bf16[2,128,1024]{2,1,0:T(8,128)(2,1)} %get-tuple-element.44.c0), channel_id=1, source_target_pairs={{0,128},{64,192},{128,0},{192,64},{1,129},{65,193},{129,1},{193,65... | collective-permute-start | bytes 1572872 | tf_op jit(solution)/shard_map/ppermute | solution.py:404
  39.7 0.1 reshape_reshape.8.rowid
  39.8 2.3 %shard_map.122 = bf16[512,1024]{1,0:T(8,128)(2,1)} custom-call(s32[2]{0:T(128)S(1)} %pad_add_fusion.info, s32[512,1]{1,0:T(8,128)S(1)} %reshape_reshape.8.rowid, bf16[128,512]{1,0:T(8,128)(2,1)S(1)} %bitcast.51, bf16[128,512]{1,0:T(8,128)(2,1)S(1)} %collective-permute-done.t1, bf16[128,512]{1,0:T(8,128)(2,1)S(1)} %collective-permute-done.1.t2, ...), custom_call_target="tpu_custom_call" | custom-call | flops 536870912 | bytes 2097152 | tf_op jit(solution)/shard_map/pallas_call | solution.py:63
  42.1 3.7 %all-to-all-start.1 = ((bf16[16,32,1024]{2,1,0:T(8,128)(2,1)}), bf16[16,32,1024]{2,1,0:T(8,128)(2,1)S(1)}, u32[]{:S(2)}, u32[]{:S(2)}) async-start(bf16[16,32,1024]{2,1,0:T(8,128)(2,1)} %bitcast.55), calls=%async_computation.1 | async-start | bytes 2097152 | tf_op jit(solution)/shard_map/all_to_all | solution.py:320
  45.8 5.4 %collective-permute-done.4.c2 = bf16[2,128,1024]{2,1,0:T(8,128)(2,1)} collective-permute-done((bf16[2,128,1024]{2,1,0:T(8,128)(2,1)}, bf16[2,128,1024]{2,1,0:T(8,128)(2,1)}, u32[]{:S(2)}, u32[]{:S(2)}) %collective-permute-start.4) | collective-permute-done | bytes 524320 | tf_op jit(solution)/shard_map/ppermute | solution.py:404
  51.2 0.5 collective-permute-start.9
  51.7 4.6 %shard_map.119 = (bf16[2,128,1024]{2,1,0:T(8,128)(2,1)S(1)}, bf16[1024,256]{1,0:T(8,128)(2,1)}) custom-call(bf16[2,128,1024]{2,1,0:T(8,128)(2,1)} %bitcast.68, bf16[1024,1024]{1,0:T(8,128)(2,1)} %w.3), custom_call_target="tpu_custom_call" | custom-call | flops 1073741824 | bytes 4194304 | tf_op jit(solution)/shard_map/pallas_call | solution.py:63
  56.3 6.4 %all-to-all-done.1 = bf16[16,32,1024]{2,1,0:T(8,128)(2,1)S(1)} async-done(((bf16[16,32,1024]{2,1,0:T(8,128)(2,1)}), bf16[16,32,1024]{2,1,0:T(8,128)(2,1)S(1)}, u32[]{:S(2)}, u32[]{:S(2)}) %all-to-all-start.1) | async-done | bytes 1048608 | tf_op jit(solution)/shard_map/all_to_all | solution.py:320
  62.7 8.9 %shard_map.123 = (bf16[16,4,8,1024]{3,2,1,0:T(8,128)(2,1)}, f32[8,2,256]{2,1,0:T(2,128)}, f32[8,2,256]{2,1,0:T(2,128)}, f32[8,2,256]{2,1,0:T(2,128)}, f32[8,2,12...) custom-call(s32[2]{0:T(128)S(1)} %pad_add_fusion.info, ...), custom_call_target="tpu_custom_call" | custom-call | flops 1048576 | bytes 1048576 | tf_op jit(solution)/shard_map/pallas_call | solution.py:63
  71.7 1.3 collective-permute-start.11
  73.0 0.6 collective-permute-start.12
  73.6 3.7 %all-to-all-start.2 = ((bf16[16,32,1024]{2,1,0:T(8,128)(2,1)}), bf16[16,32,1024]{2,1,0:T(8,128)(2,1)S(1)}, u32[]{:S(2)}, u32[]{:S(2)}) async-start(bf16[16,32,1024]{2,1,0:T(8,128)(2,1)} %bitcast.54), calls=%async_computation.2 | async-start | bytes 2097152 | tf_op jit(solution)/shard_map/all_to_all | solution.py:320
  77.2 1.0 collective-permute-done.11.ot2
  78.3 1.9 %collective-permute-done.12.ot3 = bf16[256,256]{1,0:T(8,128)(2,1)S(1)} collective-permute-done((bf16[256,256]{1,0:T(8,128)(2,1)}, bf16[256,256]{1,0:T(8,128)(2,1)S(1)}, u32[]{:S(2)}, u32[]{:S(2)}) %collective-permute-start.12) | collective-permute-done | bytes 131104 | tf_op jit(solution)/shard_map/ppermute | solution.py:447
  80.2 0.6 copy-done.9
  80.8 3.4 %shard_map.125 = (bf16[128,512]{1,0:T(8,128)(2,1)S(1)}, bf16[128,512]{1,0:T(8,128)(2,1)S(1)}, bf16[128,512]{1,0:T(8,128)(2,1)S(1)}, bf16[128,512]{1,0:T(8,128)(2,1)S(1)}) custom-call(s32[2]{0:T(128)S(1)} %pad_add_fusion.info, bf16[2,128,1024]{2,1,0:T(8,128)(2,1)} %get-tuple-element.44.c0, bf16[2,128,1024]{2,1,0:T(8,128)(2,1)} %collective-permute-done.9.c1, ...), custom_call_target="tpu_custom_call" | custom-call | flops 17179869184 | bytes 6291456 | tf_op jit(solution)/shard_map/pallas_call | solution.py:63
  84.2 3.3 %collective-permute-start.13 = (bf16[128,512]{1,0:T(8,128)(2,1)S(1)}, bf16[128,512]{1,0:T(8,128)(2,1)S(1)}, u32[]{:S(2)}, u32[]{:S(2)}) collective-permute-start(bf16[128,512]{1,0:T(8,128)(2,1)S(1)} %get-tuple-element.55), channel_id=1, source_target_pairs={{0,3},{1,0},{2,1},{3,2},{4,7},{5,4},{6,5},{7,6},{8,11},{9,8},{10,9... | collective-permute-start | bytes 393224 | tf_op jit(solution)/shard_map/ppermute | solution.py:328
  87.5 0.1 reshape_reshape.7.rowid
  87.6 2.6 %collective-permute-start.14 = (bf16[128,512]{1,0:T(8,128)(2,1)S(1)}, bf16[128,512]{1,0:T(8,128)(2,1)S(1)}, u32[]{:S(2)}, u32[]{:S(2)}) collective-permute-start(bf16[128,512]{1,0:T(8,128)(2,1)S(1)} %get-tuple-element.56), channel_id=1, source_target_pairs={{0,2},{1,3},{2,0},{3,1},{4,6},{5,7},{6,4},{7,5},{8,10},{9,11},{10,... | collective-permute-start | bytes 393224 | tf_op jit(solution)/shard_map/ppermute | solution.py:328
  90.2 1.7 %collective-permute-start.15 = (bf16[128,512]{1,0:T(8,128)(2,1)S(1)}, bf16[128,512]{1,0:T(8,128)(2,1)S(1)}, u32[]{:S(2)}, u32[]{:S(2)}) collective-permute-start(bf16[128,512]{1,0:T(8,128)(2,1)S(1)} %get-tuple-element.57), channel_id=1, source_target_pairs={{0,1},{1,2},{2,3},{3,0},{4,5},{5,6},{6,7},{7,4},{8,9},{9,10},{10,1... | collective-permute-start | bytes 393224 | tf_op jit(solution)/shard_map/ppermute | solution.py:328
  91.9 4.5 %all-to-all-done.2 = bf16[16,32,1024]{2,1,0:T(8,128)(2,1)S(1)} async-done(((bf16[16,32,1024]{2,1,0:T(8,128)(2,1)}), bf16[16,32,1024]{2,1,0:T(8,128)(2,1)S(1)}, u32[]{:S(2)}, u32[]{:S(2)}) %all-to-all-start.2) | async-done | bytes 1048608 | tf_op jit(solution)/shard_map/all_to_all | solution.py:320
  96.4 1.4 %shard_map.124 = (bf16[128,512]{1,0:T(8,128)(2,1)S(1)}, bf16[128,512]{1,0:T(8,128)(2,1)S(1)}, bf16[128,512]{1,0:T(8,128)(2,1)S(1)}, bf16[128,512]{1,0:T(8,128)(2,1)S(1)}) custom-call(s32[2]{0:T(128)S(1)} %pad_add_fusion.info, s32[1,512]{1,0:T(1,128)S(1)} %reshape_reshape.7.rowid, bf16[512,1024]{1,0:T(8,128)(2,1)S(1)} %bitcast.38), custom_call_target="tpu_custom_call" | custom-call | flops 536870912 | bytes 2097152 | tf_op jit(solution)/shard_map/pallas_call | solution.py:63
  97.8 2.4 %collective-permute-start.6 = (bf16[128,512]{1,0:T(8,128)(2,1)S(1)}, bf16[128,512]{1,0:T(8,128)(2,1)S(1)}, u32[]{:S(2)}, u32[]{:S(2)}) collective-permute-start(bf16[128,512]{1,0:T(8,128)(2,1)S(1)} %get-tuple-element.51), channel_id=1, source_target_pairs={{0,3},{1,0},{2,1},{3,2},{4,7},{5,4},{6,5},{7,6},{8,11},{9,8},{10,9... | collective-permute-start | bytes 393224 | tf_op jit(solution)/shard_map/ppermute | solution.py:328
  100.2 2.5 %collective-permute-start.7 = (bf16[128,512]{1,0:T(8,128)(2,1)S(1)}, bf16[128,512]{1,0:T(8,128)(2,1)S(1)}, u32[]{:S(2)}, u32[]{:S(2)}) collective-permute-start(bf16[128,512]{1,0:T(8,128)(2,1)S(1)} %get-tuple-element.52), channel_id=1, source_target_pairs={{0,2},{1,3},{2,0},{3,1},{4,6},{5,7},{6,4},{7,5},{8,10},{9,11},{10,... | collective-permute-start | bytes 393224 | tf_op jit(solution)/shard_map/ppermute | solution.py:328
  102.7 1.7 %collective-permute-start.8 = (bf16[128,512]{1,0:T(8,128)(2,1)S(1)}, bf16[128,512]{1,0:T(8,128)(2,1)S(1)}, u32[]{:S(2)}, u32[]{:S(2)}) collective-permute-start(bf16[128,512]{1,0:T(8,128)(2,1)S(1)} %get-tuple-element.53), channel_id=1, source_target_pairs={{0,1},{1,2},{2,3},{3,0},{4,5},{5,6},{6,7},{7,4},{8,9},{9,10},{10,1... | collective-permute-start | bytes 393224 | tf_op jit(solution)/shard_map/ppermute | solution.py:328
  104.4 7.5 %shard_map.126 = (bf16[2,128,1024]{2,1,0:T(8,128)(2,1)}, f32[2,128,1024]{2,1,0:T(8,128)S(1)}, f32[2,128,1024]{2,1,0:T(8,128)S(1)}, bf16[2,128,1024]{2,1,0:T(8,128)(2,1)}) custom-call(s32[2]{0:T(128)S(1)} %pad_add_fusion.info, bf16[2,128,1024]{2,1,0:T(8,128)(2,1)} %bitcast.58, bf16[2,128,1024]{2,1,0:T(8,128)(2,1)} %bitcast.62, ...), custom_call_target="tpu_custom_call" | custom-call | flops 1073741824 | bytes 8388608 | tf_op jit(solution)/shard_map/pallas_call | solution.py:63
  111.9 2.7 %collective-permute-start.16 = (bf16[2,128,1024]{2,1,0:T(8,128)(2,1)}, bf16[2,128,1024]{2,1,0:T(8,128)(2,1)S(1)}, u32[]{:S(2)}, u32[]{:S(2)}) collective-permute-start(bf16[2,128,1024]{2,1,0:T(8,128)(2,1)} %get-tuple-element.65), channel_id=1, source_target_pairs={{64,0},{128,64},{192,128},{65,1},{129,65},{193,129},{66,2},{130,66... | collective-permute-start | bytes 1572872 | tf_op jit(solution)/shard_map/ppermute | solution.py:500
  114.7 1.1 collective-permute-done.8
  115.8 0.8 shard_map.127._
  116.7 3.6 %all-to-all-start.3 = ((bf16[16,16,512]{2,1,0:T(8,128)(2,1)}), bf16[16,16,512]{2,1,0:T(8,128)(2,1)S(1)}, u32[]{:S(2)}, u32[]{:S(2)}) async-start(bf16[16,16,512]{2,1,0:T(8,128)(2,1)} %shard_map.127._), calls=%async_computation.3 | async-start | bytes 524288 | tf_op jit(solution)/shard_map/all_to_all | solution.py:320
  120.3 1.0 copy-done
  121.3 3.6 %shard_map.128 = bf16[2,128,1024]{2,1,0:T(8,128)(2,1)} custom-call(s32[2]{0:T(128)S(1)} %pad_add_fusion.info, bf16[256,256]{1,0:T(8,128)(2,1)} %get-tuple-element.45.ot0, bf16[256,256]{1,0:T(8,128)(2,1)} %get-tuple-element.46.ot1, bf16[256,256]{1,0:T(8,128)(2,1)} %get-tuple-element.47.ot2, bf16[256,256]{1,0:T(8,128)(2,1)} %get-tuple-element.48.ot3, ...), custom_call_target="tpu_custom_call" | custom-call | flops 17179869184 | bytes 4194304 | tf_op jit(solution)/shard_map/pallas_call | solution.py:63
  124.8 4.1 %all-to-all-done.3 = bf16[16,16,512]{2,1,0:T(8,128)(2,1)S(1)} async-done(((bf16[16,16,512]{2,1,0:T(8,128)(2,1)}), bf16[16,16,512]{2,1,0:T(8,128)(2,1)S(1)}, u32[]{:S(2)}, u32[]{:S(2)}) %all-to-all-start.3) | async-done | bytes 262176 | tf_op jit(solution)/shard_map/all_to_all | solution.py:320
  129.0 3.2 %shard_map.129 = (bf16[2,128,1024]{2,1,0:T(8,128)(2,1)}, bf16[2,128,1024]{2,1,0:T(8,128)(2,1)}, f32[4,1024]{1,0:T(4,128)}) custom-call(s32[2]{0:T(128)S(1)} %pad_add_fusion.info, s32[16,64]{1,0:T(8,128)S(1)} %bitcast.53, f32[2,128,1024]{2,1,0:T(8,128)S(1)} %get-tuple-element.63.gk, f32[2,128,1024]{2,1,0:T(8,128)S(1)} %get-tuple-element.64.gv, ...), custom_call_target="tpu_custom_call" | custom-call | flops 134217728 | bytes 4194304 | tf_op jit(solution)/shard_map/pallas_call | solution.py:63
  (36 shorter events, 0.3 us)
Async XLA Ops:
  0.7 0.7 copy-start.3
  4.3 27.4 %collective-permute-start.3 = (bf16[2,128,1024]{2,1,0:T(8,128)(2,1)}, bf16[2,128,1024]{2,1,0:T(8,128)(2,1)S(1)}, u32[]{:S(2)}, u32[]{:S(2)}) collective-permute-start(bf16[2,128,1024]{2,1,0:T(8,128)(2,1)} %get-tuple-element.40), channel_id=1, source_target_pairs={{0,64},{64,128},{128,192},{1,65},{65,129},{129,193},{2,66},{66,130... | collective-permute-start | bytes 1572872 | tf_op jit(solution)/shard_map/ppermute | solution.py:355
  6.2 15.0 %all-to-all-start = ((bf16[16,8,512]{2,1,0:T(8,128)(2,1)}), bf16[16,8,512]{2,1,0:T(8,128)(2,1)S(1)}, u32[]{:S(2)}, u32[]{:S(2)}) async-start(bf16[16,8,512]{2,1,0:T(8,128)(2,1)} %bitcast.66), calls=%async_computation | async-start | bytes 262144 | tf_op jit(solution)/shard_map/all_to_all | solution.py:320
  21.3 18.5 %collective-permute-start = (bf16[128,512]{1,0:T(8,128)(2,1)S(1)}, bf16[128,512]{1,0:T(8,128)(2,1)S(1)}, u32[]{:S(2)}, u32[]{:S(2)}) collective-permute-start(bf16[128,512]{1,0:T(8,128)(2,1)S(1)} %bitcast.47), channel_id=1, source_target_pairs={{0,1},{1,2},{2,3},{3,0},{4,5},{5,6},{6,7},{7,4},{8,9},{9,10},{10,1... | collective-permute-start | bytes 393224 | tf_op jit(solution)/shard_map/ppermute | solution.py:328
  24.6 15.3 %collective-permute-start.1 = (bf16[128,512]{1,0:T(8,128)(2,1)S(1)}, bf16[128,512]{1,0:T(8,128)(2,1)S(1)}, u32[]{:S(2)}, u32[]{:S(2)}) collective-permute-start(bf16[128,512]{1,0:T(8,128)(2,1)S(1)} %bitcast.48), channel_id=1, source_target_pairs={{0,2},{1,3},{2,0},{3,1},{4,6},{5,7},{6,4},{7,5},{8,10},{9,11},{10,... | collective-permute-start | bytes 393224 | tf_op jit(solution)/shard_map/ppermute | solution.py:328
  29.1 10.8 %collective-permute-start.2 = (bf16[128,512]{1,0:T(8,128)(2,1)S(1)}, bf16[128,512]{1,0:T(8,128)(2,1)S(1)}, u32[]{:S(2)}, u32[]{:S(2)}) collective-permute-start(bf16[128,512]{1,0:T(8,128)(2,1)S(1)} %bitcast.49), channel_id=1, source_target_pairs={{0,3},{1,0},{2,1},{3,2},{4,7},{5,4},{6,5},{7,6},{8,11},{9,8},{10,9... | collective-permute-start | bytes 393224 | tf_op jit(solution)/shard_map/ppermute | solution.py:328
  31.7 0.8 copy-start.6
  38.0 13.2 %collective-permute-start.4 = (bf16[2,128,1024]{2,1,0:T(8,128)(2,1)}, bf16[2,128,1024]{2,1,0:T(8,128)(2,1)}, u32[]{:S(2)}, u32[]{:S(2)}) collective-permute-start(bf16[2,128,1024]{2,1,0:T(8,128)(2,1)} %get-tuple-element.44.c0), channel_id=1, source_target_pairs={{0,128},{64,192},{128,0},{192,64},{1,129},{65,193},{129,1},{193,65... | collective-permute-start | bytes 1572872 | tf_op jit(solution)/shard_map/ppermute | solution.py:404
  42.1 20.5 %all-to-all-start.1 = ((bf16[16,32,1024]{2,1,0:T(8,128)(2,1)}), bf16[16,32,1024]{2,1,0:T(8,128)(2,1)S(1)}, u32[]{:S(2)}, u32[]{:S(2)}) async-start(bf16[16,32,1024]{2,1,0:T(8,128)(2,1)} %bitcast.55), calls=%async_computation.1 | async-start | bytes 2097152 | tf_op jit(solution)/shard_map/all_to_all | solution.py:320
  45.8 16.9 %copy-start.5 = (s32[64]{0:T(128)S(1)}, s32[64]{0:T(128)}, u32[]{:S(2)}) copy-start(s32[64]{0:T(128)} %rig_count.1) | copy-start | bytes 772
  51.2 11.4 %collective-permute-start.5 = (bf16[2,128,1024]{2,1,0:T(8,128)(2,1)}, bf16[2,128,1024]{2,1,0:T(8,128)(2,1)S(1)}, u32[]{:S(2)}, u32[]{:S(2)}) collective-permute-start(bf16[2,128,1024]{2,1,0:T(8,128)(2,1)} %collective-permute-done.4.c2), channel_id=1, source_target_pairs={{0,64},{64,0},{128,192},{192,128},{1,65},{65,1},{129,193},{193,129... | collective-permute-start | bytes 1572872 | tf_op jit(solution)/shard_map/ppermute | solution.py:405
  51.2 26.0 %collective-permute-start.9 = (bf16[2,128,1024]{2,1,0:T(8,128)(2,1)}, bf16[2,128,1024]{2,1,0:T(8,128)(2,1)}, u32[]{:S(2)}, u32[]{:S(2)}) collective-permute-start(bf16[2,128,1024]{2,1,0:T(8,128)(2,1)} %get-tuple-element.44.c0), channel_id=1, source_target_pairs={{0,64},{64,0},{128,192},{192,128},{1,65},{65,1},{129,193},{193,129... | collective-permute-start | bytes 1572872 | tf_op jit(solution)/shard_map/ppermute | solution.py:403
  56.3 15.3 %copy-start.1 = (bf16[2,128,1024]{2,1,0:T(8,128)(2,1)}, bf16[2,128,1024]{2,1,0:T(8,128)(2,1)S(1)}, u32[]{:S(2)}) copy-start(bf16[2,128,1024]{2,1,0:T(8,128)(2,1)S(1)} %get-tuple-element.37.g) | copy-start | bytes 1572868
  62.7 8.9 %copy-start.2 = (bf16[2,128,1024]{2,1,0:T(8,128)(2,1)}, bf16[2,128,1024]{2,1,0:T(8,128)(2,1)S(1)}, u32[]{:S(2)}) copy-start(bf16[2,128,1024]{2,1,0:T(8,128)(2,1)S(1)} %collective-permute-done.5._.c3) | copy-start | bytes 1572868
  71.6 5.6 %collective-permute-start.10 = (bf16[256,256]{1,0:T(8,128)(2,1)}, bf16[256,256]{1,0:T(8,128)(2,1)S(1)}, u32[]{:S(2)}, u32[]{:S(2)}) collective-permute-start(bf16[256,256]{1,0:T(8,128)(2,1)} %get-tuple-element.46.ot1), channel_id=1, source_target_pairs={{0,64},{64,0},{128,192},{192,128},{1,65},{65,1},{129,193},{193,129... | collective-permute-start | bytes 393224 | tf_op jit(solution)/shard_map/ppermute | solution.py:447
  71.7 6.6 %collective-permute-start.11 = (bf16[256,256]{1,0:T(8,128)(2,1)}, bf16[256,256]{1,0:T(8,128)(2,1)S(1)}, u32[]{:S(2)}, u32[]{:S(2)}) collective-permute-start(bf16[256,256]{1,0:T(8,128)(2,1)} %get-tuple-element.47.ot2), channel_id=1, source_target_pairs={{0,128},{64,192},{128,0},{192,64},{1,129},{65,193},{129,1},{193,65... | collective-permute-start | bytes 393224 | tf_op jit(solution)/shard_map/ppermute | solution.py:447
  73.0 7.2 %collective-permute-start.12 = (bf16[256,256]{1,0:T(8,128)(2,1)}, bf16[256,256]{1,0:T(8,128)(2,1)S(1)}, u32[]{:S(2)}, u32[]{:S(2)}) collective-permute-start(bf16[256,256]{1,0:T(8,128)(2,1)} %get-tuple-element.48.ot3), channel_id=1, source_target_pairs={{0,192},{64,128},{128,64},{192,0},{1,193},{65,129},{129,65},{193,1... | collective-permute-start | bytes 393224 | tf_op jit(solution)/shard_map/ppermute | solution.py:447
  73.6 22.9 %all-to-all-start.2 = ((bf16[16,32,1024]{2,1,0:T(8,128)(2,1)}), bf16[16,32,1024]{2,1,0:T(8,128)(2,1)S(1)}, u32[]{:S(2)}, u32[]{:S(2)}) async-start(bf16[16,32,1024]{2,1,0:T(8,128)(2,1)} %bitcast.54), calls=%async_computation.2 | async-start | bytes 2097152 | tf_op jit(solution)/shard_map/all_to_all | solution.py:320
  77.2 2.9 %copy-start.7 = (bf16[256,256]{1,0:T(8,128)(2,1)}, bf16[256,256]{1,0:T(8,128)(2,1)S(1)}, u32[]{:S(2)}) copy-start(bf16[256,256]{1,0:T(8,128)(2,1)S(1)} %collective-permute-done.10.ot1) | copy-start | bytes 393220
  78.3 1.9 %copy-start.8 = (bf16[256,256]{1,0:T(8,128)(2,1)}, bf16[256,256]{1,0:T(8,128)(2,1)S(1)}, u32[]{:S(2)}) copy-start(bf16[256,256]{1,0:T(8,128)(2,1)S(1)} %collective-permute-done.11.ot2) | copy-start | bytes 393220
  80.1 0.7 copy-start.9
  84.2 18.5 %collective-permute-start.13 = (bf16[128,512]{1,0:T(8,128)(2,1)S(1)}, bf16[128,512]{1,0:T(8,128)(2,1)S(1)}, u32[]{:S(2)}, u32[]{:S(2)}) collective-permute-start(bf16[128,512]{1,0:T(8,128)(2,1)S(1)} %get-tuple-element.55), channel_id=1, source_target_pairs={{0,3},{1,0},{2,1},{3,2},{4,7},{5,4},{6,5},{7,6},{8,11},{9,8},{10,9... | collective-permute-start | bytes 393224 | tf_op jit(solution)/shard_map/ppermute | solution.py:328
  87.6 24.3 %collective-permute-start.14 = (bf16[128,512]{1,0:T(8,128)(2,1)S(1)}, bf16[128,512]{1,0:T(8,128)(2,1)S(1)}, u32[]{:S(2)}, u32[]{:S(2)}) collective-permute-start(bf16[128,512]{1,0:T(8,128)(2,1)S(1)} %get-tuple-element.56), channel_id=1, source_target_pairs={{0,2},{1,3},{2,0},{3,1},{4,6},{5,7},{6,4},{7,5},{8,10},{9,11},{10,... | collective-permute-start | bytes 393224 | tf_op jit(solution)/shard_map/ppermute | solution.py:328
  90.2 24.5 %collective-permute-start.15 = (bf16[128,512]{1,0:T(8,128)(2,1)S(1)}, bf16[128,512]{1,0:T(8,128)(2,1)S(1)}, u32[]{:S(2)}, u32[]{:S(2)}) collective-permute-start(bf16[128,512]{1,0:T(8,128)(2,1)S(1)} %get-tuple-element.57), channel_id=1, source_target_pairs={{0,1},{1,2},{2,3},{3,0},{4,5},{5,6},{6,7},{7,4},{8,9},{9,10},{10,1... | collective-permute-start | bytes 393224 | tf_op jit(solution)/shard_map/ppermute | solution.py:328
  97.8 16.9 %collective-permute-start.6 = (bf16[128,512]{1,0:T(8,128)(2,1)S(1)}, bf16[128,512]{1,0:T(8,128)(2,1)S(1)}, u32[]{:S(2)}, u32[]{:S(2)}) collective-permute-start(bf16[128,512]{1,0:T(8,128)(2,1)S(1)} %get-tuple-element.51), channel_id=1, source_target_pairs={{0,3},{1,0},{2,1},{3,2},{4,7},{5,4},{6,5},{7,6},{8,11},{9,8},{10,9... | collective-permute-start | bytes 393224 | tf_op jit(solution)/shard_map/ppermute | solution.py:328
  100.2 14.5 %collective-permute-start.7 = (bf16[128,512]{1,0:T(8,128)(2,1)S(1)}, bf16[128,512]{1,0:T(8,128)(2,1)S(1)}, u32[]{:S(2)}, u32[]{:S(2)}) collective-permute-start(bf16[128,512]{1,0:T(8,128)(2,1)S(1)} %get-tuple-element.52), channel_id=1, source_target_pairs={{0,2},{1,3},{2,0},{3,1},{4,6},{5,7},{6,4},{7,5},{8,10},{9,11},{10,... | collective-permute-start | bytes 393224 | tf_op jit(solution)/shard_map/ppermute | solution.py:328
  102.7 13.1 %collective-permute-start.8 = (bf16[128,512]{1,0:T(8,128)(2,1)S(1)}, bf16[128,512]{1,0:T(8,128)(2,1)S(1)}, u32[]{:S(2)}, u32[]{:S(2)}) collective-permute-start(bf16[128,512]{1,0:T(8,128)(2,1)S(1)} %get-tuple-element.53), channel_id=1, source_target_pairs={{0,1},{1,2},{2,3},{3,0},{4,5},{5,6},{6,7},{7,4},{8,9},{9,10},{10,1... | collective-permute-start | bytes 393224 | tf_op jit(solution)/shard_map/ppermute | solution.py:328
  111.9 17.1 %collective-permute-start.16 = (bf16[2,128,1024]{2,1,0:T(8,128)(2,1)}, bf16[2,128,1024]{2,1,0:T(8,128)(2,1)S(1)}, u32[]{:S(2)}, u32[]{:S(2)}) collective-permute-start(bf16[2,128,1024]{2,1,0:T(8,128)(2,1)} %get-tuple-element.65), channel_id=1, source_target_pairs={{64,0},{128,64},{192,128},{65,1},{129,65},{193,129},{66,2},{130,66... | collective-permute-start | bytes 1572872 | tf_op jit(solution)/shard_map/ppermute | solution.py:500
  116.7 12.3 %all-to-all-start.3 = ((bf16[16,16,512]{2,1,0:T(8,128)(2,1)}), bf16[16,16,512]{2,1,0:T(8,128)(2,1)S(1)}, u32[]{:S(2)}, u32[]{:S(2)}) async-start(bf16[16,16,512]{2,1,0:T(8,128)(2,1)} %shard_map.127._), calls=%async_computation.3 | async-start | bytes 524288 | tf_op jit(solution)/shard_map/all_to_all | solution.py:320
  120.3 1.0 copy-start
  121.3 7.7 %copy-start.4 = (s32[64,16]{0,1:T(8,128)S(1)}, s32[64,16]{0,1:T(8,128)}, u32[]{:S(2)}) copy-start(s32[64,16]{0,1:T(8,128)} %param.14) | copy-start | bytes 12292

commit v4 on v3

--- a/solution.py
+++ b/solution.py
@@ -121,8 +121,8 @@
     )
 
 
-def units():
-    return [(n, slice(n * TILE, n * TILE + TILE), f) for n in range(2) for f in range(2)]
+def units(pairs=2):
+    return [(n, slice(n * TILE, n * TILE + TILE), f) for n in range(pairs) for f in range(2)]
 
 
 def grad_body(cot, w, g_out, gt_out):
@@ -133,7 +133,7 @@
 
 def local_body(info, q, k, v, prev, cot, _, m_out, l_out, o_out, cot_out):
     cot_out[...] = cot[...]
-    for n, at, f in units():
+    for n, at, f in units(4):
         qs = stacked(q[f, :, at] * jnp.asarray(0.125, BF))
         before_k, before_v = (prev[0, :, at], prev[1, :, at]) if f == 0 else (k[0, :, at], v[0, :, at])
         s1 = nt(k[f, :, at], qs)
@@ -154,7 +154,7 @@
 ):
     seen = iota((TILE, WIDE), 0) % SLOTS < rig_count[info[CAM]]
     ots = {}
-    for n, at, f in units():
+    for n, at, f in units(4):
         qs = stacked(q[f, :, at] * jnp.asarray(0.125, BF))
         gs = stacked(g[f, :, at])
         ks = strips[:, 2 * f, :, at].astype(F32).reshape(TILE, TILE).astype(BF)
@@ -180,12 +180,18 @@
         rl_out[n, f] = rl[0]
         delta_out[n, f] = delta[0]
         ots[n, f] = ot
-    whole = jnp.concatenate([jnp.concatenate([ots[n, 0], ots[n, 1]], 1) for n in range(2)], 0)
+    sides = [
+        jnp.concatenate([jnp.concatenate([ots[n, 0], ots[n, 1]], 1) for n in (i, i + 1)], 0)
+        for i in (0, 2)
+    ]
+    even = info[TM] % 2 == 0
+    mine = jnp.where(even, sides[0], sides[1])
+    other = jnp.where(even, sides[1], sides[0])
     for i, out in enumerate(ot_out):
 
-        @pl.when(pl.program_id(0) == i)
+        @pl.when(pl.program_id(0) == i // 2)
         def _():
-            out[...] = whole
+            out[...] = other if i % 2 else mine
 
 
 def weight_body(info, c0, c1, c2, c3, ot0, ot1, ot2, ot3, e0, e1, e2, e3):
@@ -225,7 +231,7 @@
     info, q, k, v, prev, g, m, rl, delta, dq, _, gq_out, gk_out, gv_out, ret_out
 ):
     hidden = (iota((2 * TILE, WIDE), 0) >= TILE) & (info[TM] == 0)
-    for n in range(2):
+    for n in range(4):
         at = slice(n * TILE, n * TILE + TILE)
         for f in range(2):
             qs = stacked(q[f, :, at] * jnp.asarray(0.125, BF))
@@ -283,7 +289,7 @@
 
 
 def final_body(info, strip_rows, gk, gv, ret, r_in, gk_out, gv_out, w_out):
-    half = pl.program_id(0) // 2
+    half = pl.program_id(0)
     shape = (GRID * 16, TILE)
     r, t = iota(shape, 0), iota(shape, 1)
     hit = strip_target(info, strip_rows, shape, 16) == t
@@ -307,7 +313,8 @@
     tm = lax.axis_index("tm")
     ring = cam % RING
     info = jnp.stack([tm, cam]).astype(jnp.int32)
-    strip_rows = strip_rows.T
+    strip_rows = pltpu.with_memory_space_constraint(strip_rows.T, pltpu.HBM)
+    counts_of = pltpu.with_memory_space_constraint(rig_count, pltpu.HBM)
 
     q = queries.reshape(2, TILE, D)
     k = key_vectors.reshape(2, TILE, D)
@@ -338,8 +345,9 @@
     head = lambda i, *_: (i, 0, 0)
     head4 = lambda i, *_: (i, 0, 0, 0)
     blk = (2, TILE, WIDE)
+    wide = (2, TILE, 4 * TILE)
     stats, sblk = like((PAIRS, 2, WIDE), F32), (2, 2, WIDE)
-    heads, hblk = like((PAIRS, 2, TILE, TILE), F32), (2, 2, TILE, TILE)
+    heads = like((PAIRS, 2, TILE, TILE), F32)
     act = like((2, TILE, D))
 
     mine, last = call(
@@ -368,23 +376,23 @@
     )
     m1, l1, o1, cot0 = call(
         local_body,
-        (BLOCKS,),
+        (2,),
         [
             info,
-            (q, blk, pair),
-            (k, blk, pair),
-            (v, blk, pair),
-            (prev, blk, pair),
-            (cot, blk, pair),
+            (q, wide, pair),
+            (k, wide, pair),
+            (v, wide, pair),
+            (prev, wide, pair, NEAR),
+            (cot, wide, pair),
             (t0, AFTER, None),
         ],
         [
-            (stats, sblk, head, NEAR),
-            (stats, sblk, head, NEAR),
-            (heads, hblk, head4, NEAR),
-            (act, blk, pair),
-        ],
-        8,
+            (stats, (4, 2, WIDE), head, NEAR),
+            (stats, (4, 2, WIDE), head, NEAR),
+            (heads, (4, 2, TILE, TILE), head4, NEAR),
+            (act, wide, pair),
+        ],
+        16,
         1 << 30,
         4 << 20,
     )
@@ -406,38 +414,38 @@
     strips = exchange(sends.reshape(GRID, 4 * SLOTS, D)).reshape(GRID, 4, SLOTS, D)
 
     def block_of(i, info):
-        return info[TM] ^ i
+        return (info[TM] // 2) ^ i
 
     opair = lambda i, info, _: (0, 0, block_of(i, info))
     orow = lambda i, info, _: (block_of(i, info), 0)
     ohead = lambda i, info, _: (block_of(i, info), 0, 0)
     ohead4 = lambda i, info, _: (block_of(i, info), 0, 0, 0)
-    gblk = (GRID, 4, SLOTS, WIDE)
+    gblk = (GRID, 4, SLOTS, 4 * TILE)
     gpair = lambda i, info, _: (0, 0, 0, block_of(i, info))
     back, m, rl, delta, dq, *ots = call(
         strip_body,
-        (BLOCKS,),
+        (2,),
         [
             info,
-            rig_count,
-            (q, blk, opair),
-            (g, blk, opair, NEAR),
-            (gt, (WIDE, WIDE), orow),
+            counts_of,
+            (q, wide, opair),
+            (g, wide, opair, NEAR),
+            (gt, (4 * TILE, WIDE), orow),
             (strips, gblk, gpair, NEAR),
-            (m1, sblk, ohead, NEAR),
-            (l1, sblk, ohead, NEAR),
-            (o1, hblk, ohead4, NEAR),
+            (m1, (4, 2, WIDE), ohead, NEAR),
+            (l1, (4, 2, WIDE), ohead, NEAR),
+            (o1, (4, 2, TILE, TILE), ohead4, NEAR),
             (cot3, AFTER, None),
         ],
         [
             (like((GRID, 4, SLOTS, D)), gblk, gpair),
-            (stats, sblk, ohead),
-            (stats, sblk, ohead),
-            (stats, sblk, ohead),
-            (heads, hblk, ohead4),
+            (stats, (4, 2, WIDE), ohead),
+            (stats, (4, 2, WIDE), ohead),
+            (stats, (4, 2, WIDE), ohead),
+            (heads, (4, 2, TILE, TILE), ohead4),
         ]
         + [(like((WIDE, WIDE)), None, None)] * 4,
-        10,
+        20,
         1 << 20,
         1 << 20,
         scalars=2,
@@ -473,27 +481,27 @@
 
     gq, gk, gv, ret = call(
         back_body,
-        (BLOCKS,),
+        (2,),
         [
             info,
-            (q, blk, pair),
-            (k, blk, pair),
-            (v, blk, pair),
-            (prev, blk, pair),
-            (g, blk, pair),
-            (m, sblk, head),
-            (rl, sblk, head),
-            (delta, sblk, head),
-            (dq, hblk, head4),
+            (q, wide, pair),
+            (k, wide, pair),
+            (v, wide, pair),
+            (prev, wide, pair),
+            (g, wide, pair),
+            (m, (4, 2, WIDE), head),
+            (rl, (4, 2, WIDE), head),
+            (delta, (4, 2, WIDE), head),
+            (dq, (4, 2, TILE, TILE), head4),
             (zs[0], AFTER, None),
         ],
         [
-            (act, blk, pair),
-            (like((2, TILE, D), F32), blk, pair, NEAR),
-            (like((2, TILE, D), F32), blk, pair, NEAR),
-            (act, blk, pair),
-        ],
-        14,
+            (act, wide, pair),
+            (like((2, TILE, D), F32), wide, pair, NEAR),
+            (like((2, TILE, D), F32), wide, pair, NEAR),
+            (act, wide, pair),
+        ],
+        24,
         1 << 30,
         8 << 20,
     )
@@ -522,24 +530,23 @@
         4 << 20,
     )
 
-    quarter = (2, TILE, 256)
     grad_k, grad_v, grad_w = call(
         final_body,
-        (4,),
+        (2,),
         [
             info,
             strip_rows,
-            (gk, quarter, pair, NEAR),
-            (gv, quarter, pair, NEAR),
-            (returned, quarter, pair, NEAR),
-            (arrived, (GRID * 16, 256), lambda i, *_: (0, i % 2), NEAR),
-        ],
-        [
-            (act, quarter, pair),
-            (act, quarter, pair),
-            (like((4, D), F32), (4, 256), lambda i, *_: (0, i)),
-        ],
-        8,
+            (gk, wide, pair, NEAR),
+            (gv, wide, pair, NEAR),
+            (returned, wide, pair, NEAR),
+            (arrived, None, None, NEAR),
+        ],
+        [
+            (act, wide, pair),
+            (act, wide, pair),
+            (like((4, D), F32), (4, 512), lambda i, *_: (0, i)),
+        ],
+        14,
         1 << 27,
         4 << 20,
         scalars=2,

time: 134 us -> 132 us (0.985)
  starting transfers between devices: 51.2 us -> 54.4 us
  Pallas kernels: 44 us -> 41 us
  local copies, waits for them, and re-layouts: 5.45 us -> 3.95 us
    all_to_all x4, waiting for transfers between devices: 21 us -> 17.9 us  [exchange(): lax.all_to_all(block, 'cam', 0, 0, axis_index_groups=plane, tiled=True)]
    pallas_call x11, Pallas kernels: 44 us -> 41 us  [call(): pl.pallas_call(body, grid_spec=pltpu.PrefetchScalarGridSpec(num_scalar_pr...]
    ppermute x9, starting transfers between devices: 24.6 us -> 26.4 us  [along_ring(): return lax.ppermute(block, 'cam', route)]
    ppermute x1, waiting for transfers between devices: 5.44 us -> 7.02 us  [on_device(): cot2 = lax.ppermute(cot0, 'tm', [(t, t ^ 2) for t in range(4)])]
    ppermute x9, waiting for transfers between devices: 1.16 us -> 2.7 us  [along_ring(): return lax.ppermute(block, 'cam', route)]
    unnamed x21 -> x15, local copies, waits for them, and re-layouts: 3.22 us -> 1.73 us
    ppermute x3, starting transfers between devices: 1.96 us -> 3.37 us  [on_device(): lax.ppermute(ots[i], 'tm', [(t, t ^ i) for t in range(4)])]
  transfers between devices with their start and end apart: 21 -> 21, of which waited for: 8 -> 8; matrix products, arithmetic and copies ran while one was open for 2% -> 2% of each run, Pallas kernels for 29% -> 27%
where the time goes in v4:
time: 132 us; the launch traced here: 131 us
  starting transfers between devices  54.4 us (41%)
  Pallas kernels  41 us (31%)
  waiting for transfers between devices  30.7 us (23%)
  local copies, waits for them, and re-layouts  3.95 us (3%)
    pallas_call x11, Pallas kernels, call(): pl.pallas_call(body, grid_spec=pltpu.PrefetchScalarGridSpec(num_scalar_pr...  41 us
    ppermute x9, starting transfers between devices, along_ring(): return lax.ppermute(block, 'cam', route)  26.4 us
    all_to_all x4, waiting for transfers between devices, exchange(): lax.all_to_all(block, 'cam', 0, 0, axis_index_groups=plane, tiled=True)  17.9 us
    all_to_all x4, starting transfers between devices, exchange(): lax.all_to_all(block, 'cam', 0, 0, axis_index_groups=plane, tiled=True)  17.9 us
    ppermute x1, waiting for transfers between devices, on_device(): cot2 = lax.ppermute(cot0, 'tm', [(t, t ^ 2) for t in range(4)])  7.02 us
    ppermute x3, starting transfers between devices, on_device(): lax.ppermute(ots[i], 'tm', [(t, t ^ i) for t in range(4)])  3.37 us
    ppermute x3, waiting for transfers between devices, on_device(): lax.ppermute(ots[i], 'tm', [(t, t ^ i) for t in range(4)])  3.06 us
    ppermute x1, starting transfers between devices, on_device(): returned = lax.ppermute(ret, 'tm', [(i + 1, i) for i in range(3)])  2.71 us
  transfers between devices with their start and end apart: 21, of which 8 were waited for; matrix products, arithmetic and copies ran while one was open for 2% of the time, Pallas kernels for 27%

profile of v4, /device:TPU:32, one launch (start us, length us, event | category | flops | bytes accessed | tf_op | source)
XLA Modules:
  0.0 131.0 jit_solution(10457435380260516672)
XLA Ops:
  0.6 0.1 pad_add_fusion.info
  0.7 3.1 %shard_map.120 = (bf16[128,512]{1,0:T(8,128)(2,1)}, bf16[2,128,1024]{2,1,0:T(8,128)(2,1)}) custom-call(s32[2]{0:T(128)S(1)} %pad_add_fusion.info, s32[16,64]{1,0:T(8,128)} %bitcast.65, bf16[2,128,1024]{2,1,0:T(8,128)(2,1)} %bitcast.58, bf16[2,128,1024]{2,1,0:T(8,128)(2,1)} %bitcast.61), custom_call_target="tpu_custom_call" | custom-call | flops 134217728 | bytes 2097152 | tf_op jit(solution)/shard_map/pallas_call | solution.py:63
  3.8 1.9 %collective-permute-start.3 = (bf16[2,128,1024]{2,1,0:T(8,128)(2,1)}, bf16[2,128,1024]{2,1,0:T(8,128)(2,1)S(1)}, u32[]{:S(2)}, u32[]{:S(2)}) collective-permute-start(bf16[2,128,1024]{2,1,0:T(8,128)(2,1)} %get-tuple-element.40), channel_id=1, source_target_pairs={{0,64},{64,128},{128,192},{1,65},{65,129},{129,193},{2,66},{66,130... | collective-permute-start | bytes 1572872 | tf_op jit(solution)/shard_map/ppermute | solution.py:363
  5.7 7.1 %all-to-all-start = ((bf16[16,8,512]{2,1,0:T(8,128)(2,1)}), bf16[16,8,512]{2,1,0:T(8,128)(2,1)S(1)}, u32[]{:S(2)}, u32[]{:S(2)}) async-start(bf16[16,8,512]{2,1,0:T(8,128)(2,1)} %bitcast.64), calls=%async_computation | async-start | bytes 262144 | tf_op jit(solution)/shard_map/all_to_all | solution.py:327
  12.8 0.8 reshape.89
  13.5 0.7 reshape.88
  14.3 0.2 dynamic-slice_reduce_fusion.1
  14.5 0.3 dynamic-slice_reduce_fusion
  14.8 6.0 %all-to-all-done = bf16[16,8,512]{2,1,0:T(8,128)(2,1)S(1)} async-done(((bf16[16,8,512]{2,1,0:T(8,128)(2,1)}), bf16[16,8,512]{2,1,0:T(8,128)(2,1)S(1)}, u32[]{:S(2)}, u32[]{:S(2)}) %all-to-all-start) | async-done | bytes 131104 | tf_op jit(solution)/shard_map/all_to_all | solution.py:327
  20.7 3.3 %collective-permute-start = (bf16[128,512]{1,0:T(8,128)(2,1)S(1)}, bf16[128,512]{1,0:T(8,128)(2,1)S(1)}, u32[]{:S(2)}, u32[]{:S(2)}) collective-permute-start(bf16[128,512]{1,0:T(8,128)(2,1)S(1)} %bitcast.47), channel_id=1, source_target_pairs={{0,1},{1,2},{2,3},{3,0},{4,5},{5,6},{6,7},{7,4},{8,9},{9,10},{10,1... | collective-permute-start | bytes 393224 | tf_op jit(solution)/shard_map/ppermute | solution.py:335
  24.0 4.5 %collective-permute-start.1 = (bf16[128,512]{1,0:T(8,128)(2,1)S(1)}, bf16[128,512]{1,0:T(8,128)(2,1)S(1)}, u32[]{:S(2)}, u32[]{:S(2)}) collective-permute-start(bf16[128,512]{1,0:T(8,128)(2,1)S(1)} %bitcast.48), channel_id=1, source_target_pairs={{0,2},{1,3},{2,0},{3,1},{4,6},{5,7},{6,4},{7,5},{8,10},{9,11},{10,... | collective-permute-start | bytes 393224 | tf_op jit(solution)/shard_map/ppermute | solution.py:335
  28.5 2.7 %collective-permute-start.2 = (bf16[128,512]{1,0:T(8,128)(2,1)S(1)}, bf16[128,512]{1,0:T(8,128)(2,1)S(1)}, u32[]{:S(2)}, u32[]{:S(2)}) collective-permute-start(bf16[128,512]{1,0:T(8,128)(2,1)S(1)} %bitcast.49), channel_id=1, source_target_pairs={{0,3},{1,0},{2,1},{3,2},{4,7},{5,4},{6,5},{7,6},{8,11},{9,8},{10,9... | collective-permute-start | bytes 393224 | tf_op jit(solution)/shard_map/ppermute | solution.py:335
  31.2 4.3 %shard_map.121 = (f32[8,2,256]{2,1,0:T(2,128)S(1)}, f32[8,2,256]{2,1,0:T(2,128)S(1)}, f32[8,2,128,128]{3,2,1,0:T(8,128)S(1)}, bf16[2,128,1024]{2,1,0:T(8,128)(2,1)}) custom-call(s32[2]{0:T(128)S(1)} %pad_add_fusion.info, bf16[2,128,1024]{2,1,0:T(8,128)(2,1)} %bitcast.54, bf16[2,128,1024]{2,1,0:T(8,128)(2,1)} %bitcast.59, bf16[2,128,1024]{2,1,0:T(8,128)(2,1)} %bitcast.62, ...), custom_call_target="tpu_custom_call" | custom-call | flops 1073741824 | bytes 4194304 | tf_op jit(solution)/shard_map/pallas_call | solution.py:63
  35.5 1.5 %collective-permute-start.4 = (bf16[2,128,1024]{2,1,0:T(8,128)(2,1)}, bf16[2,128,1024]{2,1,0:T(8,128)(2,1)}, u32[]{:S(2)}, u32[]{:S(2)}) collective-permute-start(bf16[2,128,1024]{2,1,0:T(8,128)(2,1)} %get-tuple-element.44.c0), channel_id=1, source_target_pairs={{0,128},{64,192},{128,0},{192,64},{1,129},{65,193},{129,1},{193,65... | collective-permute-start | bytes 1572872 | tf_op jit(solution)/shard_map/ppermute | solution.py:412
  37.0 0.1 copy.30
  37.2 0.1 reshape_reshape.8.rowid
  37.3 2.3 %shard_map.122 = bf16[512,1024]{1,0:T(8,128)(2,1)} custom-call(s32[2]{0:T(128)S(1)} %pad_add_fusion.info, s32[512,1]{1,0:T(8,128)S(1)} %reshape_reshape.8.rowid, bf16[128,512]{1,0:T(8,128)(2,1)S(1)} %bitcast.51, bf16[128,512]{1,0:T(8,128)(2,1)S(1)} %collective-permute-done.t1, bf16[128,512]{1,0:T(8,128)(2,1)S(1)} %collective-permute-done.1.t2, ...), custom_call_target="tpu_custom_call" | custom-call | flops 536870912 | bytes 2097152 | tf_op jit(solution)/shard_map/pallas_call | solution.py:63
  39.6 3.7 %all-to-all-start.1 = ((bf16[16,32,1024]{2,1,0:T(8,128)(2,1)}), bf16[16,32,1024]{2,1,0:T(8,128)(2,1)S(1)}, u32[]{:S(2)}, u32[]{:S(2)}) async-start(bf16[16,32,1024]{2,1,0:T(8,128)(2,1)} %bitcast.53), calls=%async_computation.1 | async-start | bytes 2097152 | tf_op jit(solution)/shard_map/all_to_all | solution.py:327
  43.3 7.0 %collective-permute-done.4.c2 = bf16[2,128,1024]{2,1,0:T(8,128)(2,1)} collective-permute-done((bf16[2,128,1024]{2,1,0:T(8,128)(2,1)}, bf16[2,128,1024]{2,1,0:T(8,128)(2,1)}, u32[]{:S(2)}, u32[]{:S(2)}) %collective-permute-start.4) | collective-permute-done | bytes 524320 | tf_op jit(solution)/shard_map/ppermute | solution.py:412
  50.3 0.5 collective-permute-start.9
  50.8 4.6 %shard_map.119 = (bf16[2,128,1024]{2,1,0:T(8,128)(2,1)S(1)}, bf16[1024,256]{1,0:T(8,128)(2,1)}) custom-call(bf16[2,128,1024]{2,1,0:T(8,128)(2,1)} %bitcast.68, bf16[1024,1024]{1,0:T(8,128)(2,1)} %w.3), custom_call_target="tpu_custom_call" | custom-call | flops 1073741824 | bytes 4194304 | tf_op jit(solution)/shard_map/pallas_call | solution.py:63
  55.4 4.8 %all-to-all-done.1 = bf16[16,32,1024]{2,1,0:T(8,128)(2,1)S(1)} async-done(((bf16[16,32,1024]{2,1,0:T(8,128)(2,1)}), bf16[16,32,1024]{2,1,0:T(8,128)(2,1)S(1)}, u32[]{:S(2)}, u32[]{:S(2)}) %all-to-all-start.1) | async-done | bytes 1048608 | tf_op jit(solution)/shard_map/all_to_all | solution.py:327
  60.2 8.0 %shard_map.123 = (bf16[16,4,8,1024]{3,2,1,0:T(8,128)(2,1)}, f32[8,2,256]{2,1,0:T(2,128)}, f32[8,2,256]{2,1,0:T(2,128)}, f32[8,2,256]{2,1,0:T(2,128)}, f32[8,2,12...) custom-call(s32[2]{0:T(128)S(1)} %pad_add_fusion.info, ...), custom_call_target="tpu_custom_call" | custom-call | flops 1048576 | bytes 1048576 | tf_op jit(solution)/shard_map/pallas_call | solution.py:63
  68.2 0.1 collective-permute-start.10
  68.3 3.2 %collective-permute-start.11 = (bf16[256,256]{1,0:T(8,128)(2,1)}, bf16[256,256]{1,0:T(8,128)(2,1)S(1)}, u32[]{:S(2)}, u32[]{:S(2)}) collective-permute-start(bf16[256,256]{1,0:T(8,128)(2,1)} %get-tuple-element.47.ot2), channel_id=1, source_target_pairs={{0,128},{64,192},{128,0},{192,64},{1,129},{65,193},{129,1},{193,65... | collective-permute-start | bytes 393224 | tf_op jit(solution)/shard_map/ppermute | solution.py:455
  71.6 3.7 %all-to-all-start.2 = ((bf16[16,32,1024]{2,1,0:T(8,128)(2,1)}), bf16[16,32,1024]{2,1,0:T(8,128)(2,1)S(1)}, u32[]{:S(2)}, u32[]{:S(2)}) async-start(bf16[16,32,1024]{2,1,0:T(8,128)(2,1)} %bitcast.52), calls=%async_computation.2 | async-start | bytes 2097152 | tf_op jit(solution)/shard_map/all_to_all | solution.py:327
  75.3 0.8 collective-permute-done.11.ot2
  76.1 2.2 %collective-permute-done.12.ot3 = bf16[256,256]{1,0:T(8,128)(2,1)S(1)} collective-permute-done((bf16[256,256]{1,0:T(8,128)(2,1)}, bf16[256,256]{1,0:T(8,128)(2,1)S(1)}, u32[]{:S(2)}, u32[]{:S(2)}) %collective-permute-start.12) | collective-permute-done | bytes 131104 | tf_op jit(solution)/shard_map/ppermute | solution.py:455
  78.3 0.6 copy-done.6
  79.0 3.4 %shard_map.125 = (bf16[128,512]{1,0:T(8,128)(2,1)S(1)}, bf16[128,512]{1,0:T(8,128)(2,1)S(1)}, bf16[128,512]{1,0:T(8,128)(2,1)S(1)}, bf16[128,512]{1,0:T(8,128)(2,1)S(1)}) custom-call(s32[2]{0:T(128)S(1)} %pad_add_fusion.info, bf16[2,128,1024]{2,1,0:T(8,128)(2,1)} %get-tuple-element.44.c0, bf16[2,128,1024]{2,1,0:T(8,128)(2,1)} %collective-permute-done.9.c1, ...), custom_call_target="tpu_custom_call" | custom-call | flops 17179869184 | bytes 6291456 | tf_op jit(solution)/shard_map/pallas_call | solution.py:63
  82.4 3.9 %collective-permute-start.13 = (bf16[128,512]{1,0:T(8,128)(2,1)S(1)}, bf16[128,512]{1,0:T(8,128)(2,1)S(1)}, u32[]{:S(2)}, u32[]{:S(2)}) collective-permute-start(bf16[128,512]{1,0:T(8,128)(2,1)S(1)} %get-tuple-element.55), channel_id=1, source_target_pairs={{0,3},{1,0},{2,1},{3,2},{4,7},{5,4},{6,5},{7,6},{8,11},{9,8},{10,9... | collective-permute-start | bytes 393224 | tf_op jit(solution)/shard_map/ppermute | solution.py:335
  86.3 0.1 reshape_reshape.7.rowid
  86.4 2.7 %collective-permute-start.14 = (bf16[128,512]{1,0:T(8,128)(2,1)S(1)}, bf16[128,512]{1,0:T(8,128)(2,1)S(1)}, u32[]{:S(2)}, u32[]{:S(2)}) collective-permute-start(bf16[128,512]{1,0:T(8,128)(2,1)S(1)} %get-tuple-element.56), channel_id=1, source_target_pairs={{0,2},{1,3},{2,0},{3,1},{4,6},{5,7},{6,4},{7,5},{8,10},{9,11},{10,... | collective-permute-start | bytes 393224 | tf_op jit(solution)/shard_map/ppermute | solution.py:335
  89.1 1.5 %collective-permute-start.15 = (bf16[128,512]{1,0:T(8,128)(2,1)S(1)}, bf16[128,512]{1,0:T(8,128)(2,1)S(1)}, u32[]{:S(2)}, u32[]{:S(2)}) collective-permute-start(bf16[128,512]{1,0:T(8,128)(2,1)S(1)} %get-tuple-element.57), channel_id=1, source_target_pairs={{0,1},{1,2},{2,3},{3,0},{4,5},{5,6},{6,7},{7,4},{8,9},{9,10},{10,1... | collective-permute-start | bytes 393224 | tf_op jit(solution)/shard_map/ppermute | solution.py:335
  90.6 3.1 %all-to-all-done.2 = bf16[16,32,1024]{2,1,0:T(8,128)(2,1)S(1)} async-done(((bf16[16,32,1024]{2,1,0:T(8,128)(2,1)}), bf16[16,32,1024]{2,1,0:T(8,128)(2,1)S(1)}, u32[]{:S(2)}, u32[]{:S(2)}) %all-to-all-start.2) | async-done | bytes 1048608 | tf_op jit(solution)/shard_map/all_to_all | solution.py:327
  93.7 1.4 %shard_map.124 = (bf16[128,512]{1,0:T(8,128)(2,1)S(1)}, bf16[128,512]{1,0:T(8,128)(2,1)S(1)}, bf16[128,512]{1,0:T(8,128)(2,1)S(1)}, bf16[128,512]{1,0:T(8,128)(2,1)S(1)}) custom-call(s32[2]{0:T(128)S(1)} %pad_add_fusion.info, s32[1,512]{1,0:T(1,128)S(1)} %reshape_reshape.7.rowid, bf16[512,1024]{1,0:T(8,128)(2,1)S(1)} %bitcast.38), custom_call_target="tpu_custom_call" | custom-call | flops 536870912 | bytes 2097152 | tf_op jit(solution)/shard_map/pallas_call | solution.py:63
  95.1 3.7 %collective-permute-start.6 = (bf16[128,512]{1,0:T(8,128)(2,1)S(1)}, bf16[128,512]{1,0:T(8,128)(2,1)S(1)}, u32[]{:S(2)}, u32[]{:S(2)}) collective-permute-start(bf16[128,512]{1,0:T(8,128)(2,1)S(1)} %get-tuple-element.51), channel_id=1, source_target_pairs={{0,3},{1,0},{2,1},{3,2},{4,7},{5,4},{6,5},{7,6},{8,11},{9,8},{10,9... | collective-permute-start | bytes 393224 | tf_op jit(solution)/shard_map/ppermute | solution.py:335
  98.8 2.6 %collective-permute-start.7 = (bf16[128,512]{1,0:T(8,128)(2,1)S(1)}, bf16[128,512]{1,0:T(8,128)(2,1)S(1)}, u32[]{:S(2)}, u32[]{:S(2)}) collective-permute-start(bf16[128,512]{1,0:T(8,128)(2,1)S(1)} %get-tuple-element.52), channel_id=1, source_target_pairs={{0,2},{1,3},{2,0},{3,1},{4,6},{5,7},{6,4},{7,5},{8,10},{9,11},{10,... | collective-permute-start | bytes 393224 | tf_op jit(solution)/shard_map/ppermute | solution.py:335
  101.4 1.5 %collective-permute-start.8 = (bf16[128,512]{1,0:T(8,128)(2,1)S(1)}, bf16[128,512]{1,0:T(8,128)(2,1)S(1)}, u32[]{:S(2)}, u32[]{:S(2)}) collective-permute-start(bf16[128,512]{1,0:T(8,128)(2,1)S(1)} %get-tuple-element.53), channel_id=1, source_target_pairs={{0,1},{1,2},{2,3},{3,0},{4,5},{5,6},{6,7},{7,4},{8,9},{9,10},{10,1... | collective-permute-start | bytes 393224 | tf_op jit(solution)/shard_map/ppermute | solution.py:335
  102.9 7.1 %shard_map.126 = (bf16[2,128,1024]{2,1,0:T(8,128)(2,1)}, f32[2,128,1024]{2,1,0:T(8,128)S(1)}, f32[2,128,1024]{2,1,0:T(8,128)S(1)}, bf16[2,128,1024]{2,1,0:T(8,128)(2,1)}) custom-call(s32[2]{0:T(128)S(1)} %pad_add_fusion.info, bf16[2,128,1024]{2,1,0:T(8,128)(2,1)} %bitcast.56, bf16[2,128,1024]{2,1,0:T(8,128)(2,1)} %bitcast.60, ...), custom_call_target="tpu_custom_call" | custom-call | flops 1073741824 | bytes 8388608 | tf_op jit(solution)/shard_map/pallas_call | solution.py:63
  110.0 2.7 %collective-permute-start.16 = (bf16[2,128,1024]{2,1,0:T(8,128)(2,1)}, bf16[2,128,1024]{2,1,0:T(8,128)(2,1)S(1)}, u32[]{:S(2)}, u32[]{:S(2)}) collective-permute-start(bf16[2,128,1024]{2,1,0:T(8,128)(2,1)} %get-tuple-element.65), channel_id=1, source_target_pairs={{64,0},{128,64},{192,128},{65,1},{129,65},{193,129},{66,2},{130,66... | collective-permute-start | bytes 1572872 | tf_op jit(solution)/shard_map/ppermute | solution.py:508
  112.8 2.7 %collective-permute-done.8 = bf16[128,512]{1,0:T(8,128)(2,1)S(1)} collective-permute-done((bf16[128,512]{1,0:T(8,128)(2,1)S(1)}, bf16[128,512]{1,0:T(8,128)(2,1)S(1)}, u32[]{:S(2)}, u32[]{:S(2)}) %collective-permute-start.8) | collective-permute-done | bytes 131104 | tf_op jit(solution)/shard_map/ppermute | solution.py:335
  115.4 0.8 shard_map.127._
  116.3 3.5 %all-to-all-start.3 = ((bf16[16,16,512]{2,1,0:T(8,128)(2,1)}), bf16[16,16,512]{2,1,0:T(8,128)(2,1)S(1)}, u32[]{:S(2)}, u32[]{:S(2)}) async-start(bf16[16,16,512]{2,1,0:T(8,128)(2,1)} %shard_map.127._), calls=%async_computation.3 | async-start | bytes 524288 | tf_op jit(solution)/shard_map/all_to_all | solution.py:327
  119.8 1.0 copy-done
  120.8 3.6 %shard_map.128 = bf16[2,128,1024]{2,1,0:T(8,128)(2,1)} custom-call(s32[2]{0:T(128)S(1)} %pad_add_fusion.info, bf16[256,256]{1,0:T(8,128)(2,1)} %get-tuple-element.45.ot0, bf16[256,256]{1,0:T(8,128)(2,1)} %get-tuple-element.46.ot1, bf16[256,256]{1,0:T(8,128)(2,1)} %get-tuple-element.47.ot2, bf16[256,256]{1,0:T(8,128)(2,1)} %get-tuple-element.48.ot3, ...), custom_call_target="tpu_custom_call" | custom-call | flops 17179869184 | bytes 4194304 | tf_op jit(solution)/shard_map/pallas_call | solution.py:63
  124.4 4.1 %all-to-all-done.3 = bf16[16,16,512]{2,1,0:T(8,128)(2,1)S(1)} async-done(((bf16[16,16,512]{2,1,0:T(8,128)(2,1)}), bf16[16,16,512]{2,1,0:T(8,128)(2,1)S(1)}, u32[]{:S(2)}, u32[]{:S(2)}) %all-to-all-start.3) | async-done | bytes 262176 | tf_op jit(solution)/shard_map/all_to_all | solution.py:327
  128.5 2.5 %shard_map.129 = (bf16[2,128,1024]{2,1,0:T(8,128)(2,1)}, bf16[2,128,1024]{2,1,0:T(8,128)(2,1)}, f32[4,1024]{1,0:T(4,128)}) custom-call(s32[2]{0:T(128)S(1)} %pad_add_fusion.info, s32[16,64]{1,0:T(8,128)} %bitcast.66, f32[2,128,1024]{2,1,0:T(8,128)S(1)} %get-tuple-element.63.gk, f32[2,128,1024]{2,1,0:T(8,128)S(1)} %get-tuple-element.64.gv, ...), custom_call_target="tpu_custom_call" | custom-call | flops 134217728 | bytes 4194304 | tf_op jit(solution)/shard_map/pallas_call | solution.py:63
  (30 shorter events, 0.1 us)
Async XLA Ops:
  3.8 27.4 %collective-permute-start.3 = (bf16[2,128,1024]{2,1,0:T(8,128)(2,1)}, bf16[2,128,1024]{2,1,0:T(8,128)(2,1)S(1)}, u32[]{:S(2)}, u32[]{:S(2)}) collective-permute-start(bf16[2,128,1024]{2,1,0:T(8,128)(2,1)} %get-tuple-element.40), channel_id=1, source_target_pairs={{0,64},{64,128},{128,192},{1,65},{65,129},{129,193},{2,66},{66,130... | collective-permute-start | bytes 1572872 | tf_op jit(solution)/shard_map/ppermute | solution.py:363
  5.7 15.0 %all-to-all-start = ((bf16[16,8,512]{2,1,0:T(8,128)(2,1)}), bf16[16,8,512]{2,1,0:T(8,128)(2,1)S(1)}, u32[]{:S(2)}, u32[]{:S(2)}) async-start(bf16[16,8,512]{2,1,0:T(8,128)(2,1)} %bitcast.64), calls=%async_computation | async-start | bytes 262144 | tf_op jit(solution)/shard_map/all_to_all | solution.py:327
  20.7 16.6 %collective-permute-start = (bf16[128,512]{1,0:T(8,128)(2,1)S(1)}, bf16[128,512]{1,0:T(8,128)(2,1)S(1)}, u32[]{:S(2)}, u32[]{:S(2)}) collective-permute-start(bf16[128,512]{1,0:T(8,128)(2,1)S(1)} %bitcast.47), channel_id=1, source_target_pairs={{0,1},{1,2},{2,3},{3,0},{4,5},{5,6},{6,7},{7,4},{8,9},{9,10},{10,1... | collective-permute-start | bytes 393224 | tf_op jit(solution)/shard_map/ppermute | solution.py:335
  24.0 13.3 %collective-permute-start.1 = (bf16[128,512]{1,0:T(8,128)(2,1)S(1)}, bf16[128,512]{1,0:T(8,128)(2,1)S(1)}, u32[]{:S(2)}, u32[]{:S(2)}) collective-permute-start(bf16[128,512]{1,0:T(8,128)(2,1)S(1)} %bitcast.48), channel_id=1, source_target_pairs={{0,2},{1,3},{2,0},{3,1},{4,6},{5,7},{6,4},{7,5},{8,10},{9,11},{10,... | collective-permute-start | bytes 393224 | tf_op jit(solution)/shard_map/ppermute | solution.py:335
  28.5 8.8 %collective-permute-start.2 = (bf16[128,512]{1,0:T(8,128)(2,1)S(1)}, bf16[128,512]{1,0:T(8,128)(2,1)S(1)}, u32[]{:S(2)}, u32[]{:S(2)}) collective-permute-start(bf16[128,512]{1,0:T(8,128)(2,1)S(1)} %bitcast.49), channel_id=1, source_target_pairs={{0,3},{1,0},{2,1},{3,2},{4,7},{5,4},{6,5},{7,6},{8,11},{9,8},{10,9... | collective-permute-start | bytes 393224 | tf_op jit(solution)/shard_map/ppermute | solution.py:335
  31.2 6.1 %copy-start.3 = (bf16[2,128,1024]{2,1,0:T(8,128)(2,1)}, bf16[2,128,1024]{2,1,0:T(8,128)(2,1)S(1)}, u32[]{:S(2)}) copy-start(bf16[2,128,1024]{2,1,0:T(8,128)(2,1)S(1)} %collective-permute-done.3.prev) | copy-start | bytes 1572868
  35.5 14.8 %collective-permute-start.4 = (bf16[2,128,1024]{2,1,0:T(8,128)(2,1)}, bf16[2,128,1024]{2,1,0:T(8,128)(2,1)}, u32[]{:S(2)}, u32[]{:S(2)}) collective-permute-start(bf16[2,128,1024]{2,1,0:T(8,128)(2,1)} %get-tuple-element.44.c0), channel_id=1, source_target_pairs={{0,128},{64,192},{128,0},{192,64},{1,129},{65,193},{129,1},{193,65... | collective-permute-start | bytes 1572872 | tf_op jit(solution)/shard_map/ppermute | solution.py:412
  39.6 20.5 %all-to-all-start.1 = ((bf16[16,32,1024]{2,1,0:T(8,128)(2,1)}), bf16[16,32,1024]{2,1,0:T(8,128)(2,1)S(1)}, u32[]{:S(2)}, u32[]{:S(2)}) async-start(bf16[16,32,1024]{2,1,0:T(8,128)(2,1)} %bitcast.53), calls=%async_computation.1 | async-start | bytes 2097152 | tf_op jit(solution)/shard_map/all_to_all | solution.py:327
  50.3 9.9 %collective-permute-start.5 = (bf16[2,128,1024]{2,1,0:T(8,128)(2,1)}, bf16[2,128,1024]{2,1,0:T(8,128)(2,1)S(1)}, u32[]{:S(2)}, u32[]{:S(2)}) collective-permute-start(bf16[2,128,1024]{2,1,0:T(8,128)(2,1)} %collective-permute-done.4.c2), channel_id=1, source_target_pairs={{0,64},{64,0},{128,192},{192,128},{1,65},{65,1},{129,193},{193,129... | collective-permute-start | bytes 1572872 | tf_op jit(solution)/shard_map/ppermute | solution.py:413
  50.3 24.9 %collective-permute-start.9 = (bf16[2,128,1024]{2,1,0:T(8,128)(2,1)}, bf16[2,128,1024]{2,1,0:T(8,128)(2,1)}, u32[]{:S(2)}, u32[]{:S(2)}) collective-permute-start(bf16[2,128,1024]{2,1,0:T(8,128)(2,1)} %get-tuple-element.44.c0), channel_id=1, source_target_pairs={{0,64},{64,0},{128,192},{192,128},{1,65},{65,1},{129,193},{193,129... | collective-permute-start | bytes 1572872 | tf_op jit(solution)/shard_map/ppermute | solution.py:411
  55.4 12.8 %copy-start.1 = (bf16[2,128,1024]{2,1,0:T(8,128)(2,1)}, bf16[2,128,1024]{2,1,0:T(8,128)(2,1)S(1)}, u32[]{:S(2)}) copy-start(bf16[2,128,1024]{2,1,0:T(8,128)(2,1)S(1)} %get-tuple-element.37.g) | copy-start | bytes 1572868
  60.2 8.0 %copy-start.2 = (bf16[2,128,1024]{2,1,0:T(8,128)(2,1)}, bf16[2,128,1024]{2,1,0:T(8,128)(2,1)S(1)}, u32[]{:S(2)}) copy-start(bf16[2,128,1024]{2,1,0:T(8,128)(2,1)S(1)} %collective-permute-done.5._.c3) | copy-start | bytes 1572868
  68.2 7.0 %collective-permute-start.10 = (bf16[256,256]{1,0:T(8,128)(2,1)}, bf16[256,256]{1,0:T(8,128)(2,1)S(1)}, u32[]{:S(2)}, u32[]{:S(2)}) collective-permute-start(bf16[256,256]{1,0:T(8,128)(2,1)} %get-tuple-element.46.ot1), channel_id=1, source_target_pairs={{0,64},{64,0},{128,192},{192,128},{1,65},{65,1},{129,193},{193,129... | collective-permute-start | bytes 393224 | tf_op jit(solution)/shard_map/ppermute | solution.py:455
  68.3 7.8 %collective-permute-start.11 = (bf16[256,256]{1,0:T(8,128)(2,1)}, bf16[256,256]{1,0:T(8,128)(2,1)S(1)}, u32[]{:S(2)}, u32[]{:S(2)}) collective-permute-start(bf16[256,256]{1,0:T(8,128)(2,1)} %get-tuple-element.47.ot2), channel_id=1, source_target_pairs={{0,128},{64,192},{128,0},{192,64},{1,129},{65,193},{129,1},{193,65... | collective-permute-start | bytes 393224 | tf_op jit(solution)/shard_map/ppermute | solution.py:455
  71.5 6.8 %collective-permute-start.12 = (bf16[256,256]{1,0:T(8,128)(2,1)}, bf16[256,256]{1,0:T(8,128)(2,1)S(1)}, u32[]{:S(2)}, u32[]{:S(2)}) collective-permute-start(bf16[256,256]{1,0:T(8,128)(2,1)} %get-tuple-element.48.ot3), channel_id=1, source_target_pairs={{0,192},{64,128},{128,64},{192,0},{1,193},{65,129},{129,65},{193,1... | collective-permute-start | bytes 393224 | tf_op jit(solution)/shard_map/ppermute | solution.py:455
  71.6 22.1 %all-to-all-start.2 = ((bf16[16,32,1024]{2,1,0:T(8,128)(2,1)}), bf16[16,32,1024]{2,1,0:T(8,128)(2,1)S(1)}, u32[]{:S(2)}, u32[]{:S(2)}) async-start(bf16[16,32,1024]{2,1,0:T(8,128)(2,1)} %bitcast.52), calls=%async_computation.2 | async-start | bytes 2097152 | tf_op jit(solution)/shard_map/all_to_all | solution.py:327
  75.3 3.1 %copy-start.4 = (bf16[256,256]{1,0:T(8,128)(2,1)}, bf16[256,256]{1,0:T(8,128)(2,1)S(1)}, u32[]{:S(2)}) copy-start(bf16[256,256]{1,0:T(8,128)(2,1)S(1)} %collective-permute-done.10.ot1) | copy-start | bytes 393220
  76.1 2.3 %copy-start.5 = (bf16[256,256]{1,0:T(8,128)(2,1)}, bf16[256,256]{1,0:T(8,128)(2,1)S(1)}, u32[]{:S(2)}) copy-start(bf16[256,256]{1,0:T(8,128)(2,1)S(1)} %collective-permute-done.11.ot2) | copy-start | bytes 393220
  78.3 0.7 copy-start.6
  82.4 19.0 %collective-permute-start.13 = (bf16[128,512]{1,0:T(8,128)(2,1)S(1)}, bf16[128,512]{1,0:T(8,128)(2,1)S(1)}, u32[]{:S(2)}, u32[]{:S(2)}) collective-permute-start(bf16[128,512]{1,0:T(8,128)(2,1)S(1)} %get-tuple-element.55), channel_id=1, source_target_pairs={{0,3},{1,0},{2,1},{3,2},{4,7},{5,4},{6,5},{7,6},{8,11},{9,8},{10,9... | collective-permute-start | bytes 393224 | tf_op jit(solution)/shard_map/ppermute | solution.py:335
  86.4 23.7 %collective-permute-start.14 = (bf16[128,512]{1,0:T(8,128)(2,1)S(1)}, bf16[128,512]{1,0:T(8,128)(2,1)S(1)}, u32[]{:S(2)}, u32[]{:S(2)}) collective-permute-start(bf16[128,512]{1,0:T(8,128)(2,1)S(1)} %get-tuple-element.56), channel_id=1, source_target_pairs={{0,2},{1,3},{2,0},{3,1},{4,6},{5,7},{6,4},{7,5},{8,10},{9,11},{10,... | collective-permute-start | bytes 393224 | tf_op jit(solution)/shard_map/ppermute | solution.py:335
  89.1 23.7 %collective-permute-start.15 = (bf16[128,512]{1,0:T(8,128)(2,1)S(1)}, bf16[128,512]{1,0:T(8,128)(2,1)S(1)}, u32[]{:S(2)}, u32[]{:S(2)}) collective-permute-start(bf16[128,512]{1,0:T(8,128)(2,1)S(1)} %get-tuple-element.57), channel_id=1, source_target_pairs={{0,1},{1,2},{2,3},{3,0},{4,5},{5,6},{6,7},{7,4},{8,9},{9,10},{10,1... | collective-permute-start | bytes 393224 | tf_op jit(solution)/shard_map/ppermute | solution.py:335
  95.1 17.7 %collective-permute-start.6 = (bf16[128,512]{1,0:T(8,128)(2,1)S(1)}, bf16[128,512]{1,0:T(8,128)(2,1)S(1)}, u32[]{:S(2)}, u32[]{:S(2)}) collective-permute-start(bf16[128,512]{1,0:T(8,128)(2,1)S(1)} %get-tuple-element.51), channel_id=1, source_target_pairs={{0,3},{1,0},{2,1},{3,2},{4,7},{5,4},{6,5},{7,6},{8,11},{9,8},{10,9... | collective-permute-start | bytes 393224 | tf_op jit(solution)/shard_map/ppermute | solution.py:335
  98.8 14.0 %collective-permute-start.7 = (bf16[128,512]{1,0:T(8,128)(2,1)S(1)}, bf16[128,512]{1,0:T(8,128)(2,1)S(1)}, u32[]{:S(2)}, u32[]{:S(2)}) collective-permute-start(bf16[128,512]{1,0:T(8,128)(2,1)S(1)} %get-tuple-element.52), channel_id=1, source_target_pairs={{0,2},{1,3},{2,0},{3,1},{4,6},{5,7},{6,4},{7,5},{8,10},{9,11},{10,... | collective-permute-start | bytes 393224 | tf_op jit(solution)/shard_map/ppermute | solution.py:335
  101.4 14.0 %collective-permute-start.8 = (bf16[128,512]{1,0:T(8,128)(2,1)S(1)}, bf16[128,512]{1,0:T(8,128)(2,1)S(1)}, u32[]{:S(2)}, u32[]{:S(2)}) collective-permute-start(bf16[128,512]{1,0:T(8,128)(2,1)S(1)} %get-tuple-element.53), channel_id=1, source_target_pairs={{0,1},{1,2},{2,3},{3,0},{4,5},{5,6},{6,7},{7,4},{8,9},{9,10},{10,1... | collective-permute-start | bytes 393224 | tf_op jit(solution)/shard_map/ppermute | solution.py:335
  110.0 18.5 %collective-permute-start.16 = (bf16[2,128,1024]{2,1,0:T(8,128)(2,1)}, bf16[2,128,1024]{2,1,0:T(8,128)(2,1)S(1)}, u32[]{:S(2)}, u32[]{:S(2)}) collective-permute-start(bf16[2,128,1024]{2,1,0:T(8,128)(2,1)} %get-tuple-element.65), channel_id=1, source_target_pairs={{64,0},{128,64},{192,128},{65,1},{129,65},{193,129},{66,2},{130,66... | collective-permute-start | bytes 1572872 | tf_op jit(solution)/shard_map/ppermute | solution.py:508
  116.3 12.2 %all-to-all-start.3 = ((bf16[16,16,512]{2,1,0:T(8,128)(2,1)}), bf16[16,16,512]{2,1,0:T(8,128)(2,1)S(1)}, u32[]{:S(2)}, u32[]{:S(2)}) async-start(bf16[16,16,512]{2,1,0:T(8,128)(2,1)} %shard_map.127._), calls=%async_computation.3 | async-start | bytes 524288 | tf_op jit(solution)/shard_map/all_to_all | solution.py:327
  119.8 1.0 copy-start

commit v5 on v4

--- a/solution.py
+++ b/solution.py
@@ -149,7 +149,7 @@
 
 
 def strip_body(
-    info, rig_count, q, g, gt, strips, m1, l1, o1, _,
+    info, rig_count, q, g, gt, strips, m1, l1, o1, _, __,
     back, m_out, rl_out, delta_out, dq_out, *ot_out,
 ):
     seen = iota((TILE, WIDE), 0) % SLOTS < rig_count[info[CAM]]
@@ -436,6 +436,7 @@
             (l1, (4, 2, WIDE), ohead, NEAR),
             (o1, (4, 2, TILE, TILE), ohead4, NEAR),
             (cot3, AFTER, None),
+            (cot1, AFTER, None),
         ],
         [
             (like((GRID, 4, SLOTS, D)), gblk, gpair),

time: 132 us -> 135 us (1.023)
  the two profiles are of different devices: /device:TPU:32 before, /device:TPU:1 now
where the time goes in v5:
time: 135 us; the launch traced here: 134 us
  starting transfers between devices  52.2 us (39%)
  Pallas kernels  41 us (30%)
  waiting for transfers between devices  36.4 us (27%)
  local copies, waits for them, and re-layouts  3.96 us (3%)
    pallas_call x11, Pallas kernels, call(): pl.pallas_call(body, grid_spec=pltpu.PrefetchScalarGridSpec(num_scalar_pr...  41 us
    all_to_all x4, waiting for transfers between devices, exchange(): lax.all_to_all(block, 'cam', 0, 0, axis_index_groups=plane, tiled=True)  21.6 us
    ppermute x9, starting transfers between devices, along_ring(): return lax.ppermute(block, 'cam', route)  21.2 us
    all_to_all x4, starting transfers between devices, exchange(): lax.all_to_all(block, 'cam', 0, 0, axis_index_groups=plane, tiled=True)  17.6 us
    ppermute x9, waiting for transfers between devices, along_ring(): return lax.ppermute(block, 'cam', route)  9.08 us
    ppermute x1, starting transfers between devices, on_device(): prev = lax.ppermute(last, 'tm', [(i, i + 1) for i in range(3)])  4.92 us
    ppermute x3, starting transfers between devices, on_device(): lax.ppermute(ots[i], 'tm', [(t, t ^ i) for t in range(4)])  3.83 us
    ppermute x1, starting transfers between devices, on_device(): returned = lax.ppermute(ret, 'tm', [(i + 1, i) for i in range(3)])  3.43 us
  transfers between devices with their start and end apart: 21, of which 9 were waited for; matrix products, arithmetic and copies ran while one was open for 2% of the time, Pallas kernels for 20%

profile of v5, /device:TPU:1, one launch (start us, length us, event | category | flops | bytes accessed | tf_op | source)
XLA Modules:
  0.0 134.4 jit_solution(6952742838888102425)
XLA Ops:
  0.7 3.1 %shard_map.120 = (bf16[128,512]{1,0:T(8,128)(2,1)}, bf16[2,128,1024]{2,1,0:T(8,128)(2,1)}) custom-call(s32[2]{0:T(128)S(1)} %pad_add_fusion.info, s32[16,64]{1,0:T(8,128)} %bitcast.65, bf16[2,128,1024]{2,1,0:T(8,128)(2,1)} %bitcast.55, bf16[2,128,1024]{2,1,0:T(8,128)(2,1)} %bitcast.58), custom_call_target="tpu_custom_call" | custom-call | flops 134217728 | bytes 2097152 | tf_op jit(solution)/shard_map/pallas_call | solution.py:63
  3.8 4.9 %collective-permute-start.3 = (bf16[2,128,1024]{2,1,0:T(8,128)(2,1)}, bf16[2,128,1024]{2,1,0:T(8,128)(2,1)S(1)}, u32[]{:S(2)}, u32[]{:S(2)}) collective-permute-start(bf16[2,128,1024]{2,1,0:T(8,128)(2,1)} %get-tuple-element.40), channel_id=1, source_target_pairs={{0,64},{64,128},{128,192},{1,65},{65,129},{129,193},{2,66},{66,130... | collective-permute-start | bytes 1572872 | tf_op jit(solution)/shard_map/ppermute | solution.py:363
  8.7 6.8 %all-to-all-start = ((bf16[16,8,512]{2,1,0:T(8,128)(2,1)}), bf16[16,8,512]{2,1,0:T(8,128)(2,1)S(1)}, u32[]{:S(2)}, u32[]{:S(2)}) async-start(bf16[16,8,512]{2,1,0:T(8,128)(2,1)} %bitcast.64), calls=%async_computation | async-start | bytes 262144 | tf_op jit(solution)/shard_map/all_to_all | solution.py:327
  15.5 0.7 reshape.88
  16.2 0.8 reshape.89
  17.0 0.2 dynamic-slice_reduce_fusion.1
  17.2 0.3 dynamic-slice_reduce_fusion
  17.5 4.8 %all-to-all-done = bf16[16,8,512]{2,1,0:T(8,128)(2,1)S(1)} async-done(((bf16[16,8,512]{2,1,0:T(8,128)(2,1)}), bf16[16,8,512]{2,1,0:T(8,128)(2,1)S(1)}, u32[]{:S(2)}, u32[]{:S(2)}) %all-to-all-start) | async-done | bytes 131104 | tf_op jit(solution)/shard_map/all_to_all | solution.py:327
  22.3 6.1 %collective-permute-start.2 = (bf16[128,512]{1,0:T(8,128)(2,1)S(1)}, bf16[128,512]{1,0:T(8,128)(2,1)S(1)}, u32[]{:S(2)}, u32[]{:S(2)}) collective-permute-start(bf16[128,512]{1,0:T(8,128)(2,1)S(1)} %bitcast.47), channel_id=1, source_target_pairs={{0,3},{1,0},{2,1},{3,2},{4,7},{5,4},{6,5},{7,6},{8,11},{9,8},{10,9... | collective-permute-start | bytes 393224 | tf_op jit(solution)/shard_map/ppermute | solution.py:335
  28.4 0.9 collective-permute-start.1
  29.3 2.4 %collective-permute-start = (bf16[128,512]{1,0:T(8,128)(2,1)S(1)}, bf16[128,512]{1,0:T(8,128)(2,1)S(1)}, u32[]{:S(2)}, u32[]{:S(2)}) collective-permute-start(bf16[128,512]{1,0:T(8,128)(2,1)S(1)} %bitcast.49), channel_id=1, source_target_pairs={{0,1},{1,2},{2,3},{3,0},{4,5},{5,6},{6,7},{7,4},{8,9},{9,10},{10,1... | collective-permute-start | bytes 393224 | tf_op jit(solution)/shard_map/ppermute | solution.py:335
  31.6 4.3 %shard_map.121 = (f32[8,2,256]{2,1,0:T(2,128)S(1)}, f32[8,2,256]{2,1,0:T(2,128)S(1)}, f32[8,2,128,128]{3,2,1,0:T(8,128)S(1)}, bf16[2,128,1024]{2,1,0:T(8,128)(2,1)}) custom-call(s32[2]{0:T(128)S(1)} %pad_add_fusion.info, bf16[2,128,1024]{2,1,0:T(8,128)(2,1)} %bitcast.61, bf16[2,128,1024]{2,1,0:T(8,128)(2,1)} %bitcast.56, bf16[2,128,1024]{2,1,0:T(8,128)(2,1)} %bitcast.59, ...), custom_call_target="tpu_custom_call" | custom-call | flops 1073741824 | bytes 4194304 | tf_op jit(solution)/shard_map/pallas_call | solution.py:63
  36.0 0.1 copy.30
  36.1 0.1 reshape_reshape.8.rowid
  36.3 1.4 %collective-permute-done.2.t3 = bf16[128,512]{1,0:T(8,128)(2,1)S(1)} collective-permute-done((bf16[128,512]{1,0:T(8,128)(2,1)S(1)}, bf16[128,512]{1,0:T(8,128)(2,1)S(1)}, u32[]{:S(2)}, u32[]{:S(2)}) %collective-permute-start.2) | collective-permute-done | bytes 131104 | tf_op jit(solution)/shard_map/ppermute | solution.py:335
  37.7 5.1 %collective-permute-done.1.t2 = bf16[128,512]{1,0:T(8,128)(2,1)S(1)} collective-permute-done((bf16[128,512]{1,0:T(8,128)(2,1)S(1)}, bf16[128,512]{1,0:T(8,128)(2,1)S(1)}, u32[]{:S(2)}, u32[]{:S(2)}) %collective-permute-start.1) | collective-permute-done | bytes 131104 | tf_op jit(solution)/shard_map/ppermute | solution.py:335
  42.8 2.3 %shard_map.122 = bf16[512,1024]{1,0:T(8,128)(2,1)} custom-call(s32[2]{0:T(128)S(1)} %pad_add_fusion.info, s32[512,1]{1,0:T(8,128)S(1)} %reshape_reshape.8.rowid, bf16[128,512]{1,0:T(8,128)(2,1)S(1)} %bitcast.51, bf16[128,512]{1,0:T(8,128)(2,1)S(1)} %collective-permute-done.t1, bf16[128,512]{1,0:T(8,128)(2,1)S(1)} %collective-permute-done.1.t2, ...), custom_call_target="tpu_custom_call" | custom-call | flops 536870912 | bytes 2097152 | tf_op jit(solution)/shard_map/pallas_call | solution.py:63
  45.1 3.7 %all-to-all-start.1 = ((bf16[16,32,1024]{2,1,0:T(8,128)(2,1)}), bf16[16,32,1024]{2,1,0:T(8,128)(2,1)S(1)}, u32[]{:S(2)}, u32[]{:S(2)}) async-start(bf16[16,32,1024]{2,1,0:T(8,128)(2,1)} %bitcast.53), calls=%async_computation.1 | async-start | bytes 2097152 | tf_op jit(solution)/shard_map/all_to_all | solution.py:327
  48.8 0.7 collective-permute-start.6
  49.4 2.8 %collective-permute-done.4.c2 = bf16[2,128,1024]{2,1,0:T(8,128)(2,1)} collective-permute-done((bf16[2,128,1024]{2,1,0:T(8,128)(2,1)}, bf16[2,128,1024]{2,1,0:T(8,128)(2,1)}, u32[]{:S(2)}, u32[]{:S(2)}) %collective-permute-start.4) | collective-permute-done | bytes 524320 | tf_op jit(solution)/shard_map/ppermute | solution.py:412
  52.3 0.5 collective-permute-start.5
  52.8 4.6 %shard_map.119 = (bf16[2,128,1024]{2,1,0:T(8,128)(2,1)S(1)}, bf16[1024,256]{1,0:T(8,128)(2,1)}) custom-call(bf16[2,128,1024]{2,1,0:T(8,128)(2,1)} %bitcast.68, bf16[1024,1024]{1,0:T(8,128)(2,1)} %w.3), custom_call_target="tpu_custom_call" | custom-call | flops 1073741824 | bytes 4194304 | tf_op jit(solution)/shard_map/pallas_call | solution.py:63
  57.3 7.8 %all-to-all-done.1 = bf16[16,32,1024]{2,1,0:T(8,128)(2,1)S(1)} async-done(((bf16[16,32,1024]{2,1,0:T(8,128)(2,1)}), bf16[16,32,1024]{2,1,0:T(8,128)(2,1)S(1)}, u32[]{:S(2)}, u32[]{:S(2)}) %all-to-all-start.1) | async-done | bytes 1048608 | tf_op jit(solution)/shard_map/all_to_all | solution.py:327
  65.1 8.0 %shard_map.123 = (bf16[16,4,8,1024]{3,2,1,0:T(8,128)(2,1)}, f32[8,2,256]{2,1,0:T(2,128)}, f32[8,2,256]{2,1,0:T(2,128)}, f32[8,2,256]{2,1,0:T(2,128)}, f32[8,2,12...) custom-call(s32[2]{0:T(128)S(1)} %pad_add_fusion.info, ...), custom_call_target="tpu_custom_call" | custom-call | flops 1048576 | bytes 1048576 | tf_op jit(solution)/shard_map/pallas_call | solution.py:63
  73.2 2.1 %collective-permute-start.10 = (bf16[256,256]{1,0:T(8,128)(2,1)}, bf16[256,256]{1,0:T(8,128)(2,1)S(1)}, u32[]{:S(2)}, u32[]{:S(2)}) collective-permute-start(bf16[256,256]{1,0:T(8,128)(2,1)} %get-tuple-element.46.ot1), channel_id=1, source_target_pairs={{0,64},{64,0},{128,192},{192,128},{1,65},{65,1},{129,193},{193,129... | collective-permute-start | bytes 393224 | tf_op jit(solution)/shard_map/ppermute | solution.py:456
  75.3 1.7 %collective-permute-start.12 = (bf16[256,256]{1,0:T(8,128)(2,1)}, bf16[256,256]{1,0:T(8,128)(2,1)S(1)}, u32[]{:S(2)}, u32[]{:S(2)}) collective-permute-start(bf16[256,256]{1,0:T(8,128)(2,1)} %get-tuple-element.48.ot3), channel_id=1, source_target_pairs={{0,192},{64,128},{128,64},{192,0},{1,193},{65,129},{129,65},{193,1... | collective-permute-start | bytes 393224 | tf_op jit(solution)/shard_map/ppermute | solution.py:456
  77.0 3.7 %all-to-all-start.2 = ((bf16[16,32,1024]{2,1,0:T(8,128)(2,1)}), bf16[16,32,1024]{2,1,0:T(8,128)(2,1)S(1)}, u32[]{:S(2)}, u32[]{:S(2)}) async-start(bf16[16,32,1024]{2,1,0:T(8,128)(2,1)} %bitcast.52), calls=%async_computation.2 | async-start | bytes 2097152 | tf_op jit(solution)/shard_map/all_to_all | solution.py:327
  80.7 2.8 %collective-permute-done.12.ot3 = bf16[256,256]{1,0:T(8,128)(2,1)S(1)} collective-permute-done((bf16[256,256]{1,0:T(8,128)(2,1)}, bf16[256,256]{1,0:T(8,128)(2,1)S(1)}, u32[]{:S(2)}, u32[]{:S(2)}) %collective-permute-start.12) | collective-permute-done | bytes 131104 | tf_op jit(solution)/shard_map/ppermute | solution.py:456
  83.5 0.6 copy-done.6
  84.2 3.4 %shard_map.125 = (bf16[128,512]{1,0:T(8,128)(2,1)S(1)}, bf16[128,512]{1,0:T(8,128)(2,1)S(1)}, bf16[128,512]{1,0:T(8,128)(2,1)S(1)}, bf16[128,512]{1,0:T(8,128)(2,1)S(1)}) custom-call(s32[2]{0:T(128)S(1)} %pad_add_fusion.info, bf16[2,128,1024]{2,1,0:T(8,128)(2,1)} %get-tuple-element.44.c0, bf16[2,128,1024]{2,1,0:T(8,128)(2,1)} %copy-done.2, ...), custom_call_target="tpu_custom_call" | custom-call | flops 17179869184 | bytes 6291456 | tf_op jit(solution)/shard_map/pallas_call | solution.py:63
  87.6 3.9 %collective-permute-start.13 = (bf16[128,512]{1,0:T(8,128)(2,1)S(1)}, bf16[128,512]{1,0:T(8,128)(2,1)S(1)}, u32[]{:S(2)}, u32[]{:S(2)}) collective-permute-start(bf16[128,512]{1,0:T(8,128)(2,1)S(1)} %get-tuple-element.55), channel_id=1, source_target_pairs={{0,3},{1,0},{2,1},{3,2},{4,7},{5,4},{6,5},{7,6},{8,11},{9,8},{10,9... | collective-permute-start | bytes 393224 | tf_op jit(solution)/shard_map/ppermute | solution.py:335
  91.4 0.1 reshape_reshape.7.rowid
  91.5 1.0 collective-permute-start.14
  92.5 1.2 collective-permute-start.15
  93.7 5.3 %all-to-all-done.2 = bf16[16,32,1024]{2,1,0:T(8,128)(2,1)S(1)} async-done(((bf16[16,32,1024]{2,1,0:T(8,128)(2,1)}), bf16[16,32,1024]{2,1,0:T(8,128)(2,1)S(1)}, u32[]{:S(2)}, u32[]{:S(2)}) %all-to-all-start.2) | async-done | bytes 1048608 | tf_op jit(solution)/shard_map/all_to_all | solution.py:327
  99.1 1.4 %shard_map.124 = (bf16[128,512]{1,0:T(8,128)(2,1)S(1)}, bf16[128,512]{1,0:T(8,128)(2,1)S(1)}, bf16[128,512]{1,0:T(8,128)(2,1)S(1)}, bf16[128,512]{1,0:T(8,128)(2,1)S(1)}) custom-call(s32[2]{0:T(128)S(1)} %pad_add_fusion.info, s32[1,512]{1,0:T(1,128)S(1)} %reshape_reshape.7.rowid, bf16[512,1024]{1,0:T(8,128)(2,1)S(1)} %bitcast.38), custom_call_target="tpu_custom_call" | custom-call | flops 536870912 | bytes 2097152 | tf_op jit(solution)/shard_map/pallas_call | solution.py:63
  100.4 3.7 %collective-permute-start.7 = (bf16[128,512]{1,0:T(8,128)(2,1)S(1)}, bf16[128,512]{1,0:T(8,128)(2,1)S(1)}, u32[]{:S(2)}, u32[]{:S(2)}) collective-permute-start(bf16[128,512]{1,0:T(8,128)(2,1)S(1)} %get-tuple-element.51), channel_id=1, source_target_pairs={{0,3},{1,0},{2,1},{3,2},{4,7},{5,4},{6,5},{7,6},{8,11},{9,8},{10,9... | collective-permute-start | bytes 393224 | tf_op jit(solution)/shard_map/ppermute | solution.py:335
  104.1 0.9 collective-permute-start.8
  105.0 1.3 collective-permute-start.9
  106.3 7.1 %shard_map.126 = (bf16[2,128,1024]{2,1,0:T(8,128)(2,1)}, f32[2,128,1024]{2,1,0:T(8,128)S(1)}, f32[2,128,1024]{2,1,0:T(8,128)S(1)}, bf16[2,128,1024]{2,1,0:T(8,128)(2,1)}) custom-call(s32[2]{0:T(128)S(1)} %pad_add_fusion.info, bf16[2,128,1024]{2,1,0:T(8,128)(2,1)} %bitcast.63, bf16[2,128,1024]{2,1,0:T(8,128)(2,1)} %bitcast.57, ...), custom_call_target="tpu_custom_call" | custom-call | flops 1073741824 | bytes 8388608 | tf_op jit(solution)/shard_map/pallas_call | solution.py:63
  113.4 3.4 %collective-permute-start.16 = (bf16[2,128,1024]{2,1,0:T(8,128)(2,1)}, bf16[2,128,1024]{2,1,0:T(8,128)(2,1)S(1)}, u32[]{:S(2)}, u32[]{:S(2)}) collective-permute-start(bf16[2,128,1024]{2,1,0:T(8,128)(2,1)} %get-tuple-element.65), channel_id=1, source_target_pairs={{64,0},{128,64},{192,128},{65,1},{129,65},{193,129},{66,2},{130,66... | collective-permute-start | bytes 1572872 | tf_op jit(solution)/shard_map/ppermute | solution.py:509
  116.9 2.5 %collective-permute-done.9 = bf16[128,512]{1,0:T(8,128)(2,1)S(1)} collective-permute-done((bf16[128,512]{1,0:T(8,128)(2,1)S(1)}, bf16[128,512]{1,0:T(8,128)(2,1)S(1)}, u32[]{:S(2)}, u32[]{:S(2)}) %collective-permute-start.9) | collective-permute-done | bytes 131104 | tf_op jit(solution)/shard_map/ppermute | solution.py:335
  119.4 0.8 shard_map.127._
  120.2 3.5 %all-to-all-start.3 = ((bf16[16,16,512]{2,1,0:T(8,128)(2,1)}), bf16[16,16,512]{2,1,0:T(8,128)(2,1)S(1)}, u32[]{:S(2)}, u32[]{:S(2)}) async-start(bf16[16,16,512]{2,1,0:T(8,128)(2,1)} %shard_map.127._), calls=%async_computation.3 | async-start | bytes 524288 | tf_op jit(solution)/shard_map/all_to_all | solution.py:327
  123.8 1.0 copy-done
  124.7 3.6 %shard_map.128 = bf16[2,128,1024]{2,1,0:T(8,128)(2,1)} custom-call(s32[2]{0:T(128)S(1)} %pad_add_fusion.info, bf16[256,256]{1,0:T(8,128)(2,1)} %get-tuple-element.45.ot0, bf16[256,256]{1,0:T(8,128)(2,1)} %get-tuple-element.46.ot1, bf16[256,256]{1,0:T(8,128)(2,1)} %get-tuple-element.47.ot2, bf16[256,256]{1,0:T(8,128)(2,1)} %get-tuple-element.48.ot3, ...), custom_call_target="tpu_custom_call" | custom-call | flops 17179869184 | bytes 4194304 | tf_op jit(solution)/shard_map/pallas_call | solution.py:63
  128.3 3.7 %all-to-all-done.3 = bf16[16,16,512]{2,1,0:T(8,128)(2,1)S(1)} async-done(((bf16[16,16,512]{2,1,0:T(8,128)(2,1)}), bf16[16,16,512]{2,1,0:T(8,128)(2,1)S(1)}, u32[]{:S(2)}, u32[]{:S(2)}) %all-to-all-start.3) | async-done | bytes 262176 | tf_op jit(solution)/shard_map/all_to_all | solution.py:327
  132.0 2.5 %shard_map.129 = (bf16[2,128,1024]{2,1,0:T(8,128)(2,1)}, bf16[2,128,1024]{2,1,0:T(8,128)(2,1)}, f32[4,1024]{1,0:T(4,128)}) custom-call(s32[2]{0:T(128)S(1)} %pad_add_fusion.info, s32[16,64]{1,0:T(8,128)} %bitcast.66, f32[2,128,1024]{2,1,0:T(8,128)S(1)} %get-tuple-element.63.gk, f32[2,128,1024]{2,1,0:T(8,128)S(1)} %get-tuple-element.64.gv, ...), custom_call_target="tpu_custom_call" | custom-call | flops 134217728 | bytes 4194304 | tf_op jit(solution)/shard_map/pallas_call | solution.py:63
  (30 shorter events, 0.2 us)
Async XLA Ops:
  3.8 27.9 %collective-permute-start.3 = (bf16[2,128,1024]{2,1,0:T(8,128)(2,1)}, bf16[2,128,1024]{2,1,0:T(8,128)(2,1)S(1)}, u32[]{:S(2)}, u32[]{:S(2)}) collective-permute-start(bf16[2,128,1024]{2,1,0:T(8,128)(2,1)} %get-tuple-element.40), channel_id=1, source_target_pairs={{0,64},{64,128},{128,192},{1,65},{65,129},{129,193},{2,66},{66,130... | collective-permute-start | bytes 1572872 | tf_op jit(solution)/shard_map/ppermute | solution.py:363
  8.7 13.6 %all-to-all-start = ((bf16[16,8,512]{2,1,0:T(8,128)(2,1)}), bf16[16,8,512]{2,1,0:T(8,128)(2,1)S(1)}, u32[]{:S(2)}, u32[]{:S(2)}) async-start(bf16[16,8,512]{2,1,0:T(8,128)(2,1)} %bitcast.64), calls=%async_computation | async-start | bytes 262144 | tf_op jit(solution)/shard_map/all_to_all | solution.py:327
  22.3 15.4 %collective-permute-start.2 = (bf16[128,512]{1,0:T(8,128)(2,1)S(1)}, bf16[128,512]{1,0:T(8,128)(2,1)S(1)}, u32[]{:S(2)}, u32[]{:S(2)}) collective-permute-start(bf16[128,512]{1,0:T(8,128)(2,1)S(1)} %bitcast.47), channel_id=1, source_target_pairs={{0,3},{1,0},{2,1},{3,2},{4,7},{5,4},{6,5},{7,6},{8,11},{9,8},{10,9... | collective-permute-start | bytes 393224 | tf_op jit(solution)/shard_map/ppermute | solution.py:335
  28.4 14.4 %collective-permute-start.1 = (bf16[128,512]{1,0:T(8,128)(2,1)S(1)}, bf16[128,512]{1,0:T(8,128)(2,1)S(1)}, u32[]{:S(2)}, u32[]{:S(2)}) collective-permute-start(bf16[128,512]{1,0:T(8,128)(2,1)S(1)} %bitcast.48), channel_id=1, source_target_pairs={{0,2},{1,3},{2,0},{3,1},{4,6},{5,7},{6,4},{7,5},{8,10},{9,11},{10,... | collective-permute-start | bytes 393224 | tf_op jit(solution)/shard_map/ppermute | solution.py:335
  29.3 13.5 %collective-permute-start = (bf16[128,512]{1,0:T(8,128)(2,1)S(1)}, bf16[128,512]{1,0:T(8,128)(2,1)S(1)}, u32[]{:S(2)}, u32[]{:S(2)}) collective-permute-start(bf16[128,512]{1,0:T(8,128)(2,1)S(1)} %bitcast.49), channel_id=1, source_target_pairs={{0,1},{1,2},{2,3},{3,0},{4,5},{5,6},{6,7},{7,4},{8,9},{9,10},{10,1... | collective-permute-start | bytes 393224 | tf_op jit(solution)/shard_map/ppermute | solution.py:335
  31.6 4.6 %copy-start.3 = (bf16[2,128,1024]{2,1,0:T(8,128)(2,1)}, bf16[2,128,1024]{2,1,0:T(8,128)(2,1)S(1)}, u32[]{:S(2)}) copy-start(bf16[2,128,1024]{2,1,0:T(8,128)(2,1)S(1)} %collective-permute-done.3.prev) | copy-start | bytes 1572868
  36.0 16.3 %collective-permute-start.4 = (bf16[2,128,1024]{2,1,0:T(8,128)(2,1)}, bf16[2,128,1024]{2,1,0:T(8,128)(2,1)}, u32[]{:S(2)}, u32[]{:S(2)}) collective-permute-start(bf16[2,128,1024]{2,1,0:T(8,128)(2,1)} %get-tuple-element.44.c0), channel_id=1, source_target_pairs={{0,128},{64,192},{128,0},{192,64},{1,129},{65,193},{129,1},{193,65... | collective-permute-start | bytes 1572872 | tf_op jit(solution)/shard_map/ppermute | solution.py:412
  45.1 20.0 %all-to-all-start.1 = ((bf16[16,32,1024]{2,1,0:T(8,128)(2,1)}), bf16[16,32,1024]{2,1,0:T(8,128)(2,1)S(1)}, u32[]{:S(2)}, u32[]{:S(2)}) async-start(bf16[16,32,1024]{2,1,0:T(8,128)(2,1)} %bitcast.53), calls=%async_computation.1 | async-start | bytes 2097152 | tf_op jit(solution)/shard_map/all_to_all | solution.py:327
  48.8 8.6 %collective-permute-start.6 = (bf16[2,128,1024]{2,1,0:T(8,128)(2,1)}, bf16[2,128,1024]{2,1,0:T(8,128)(2,1)S(1)}, u32[]{:S(2)}, u32[]{:S(2)}) collective-permute-start(bf16[2,128,1024]{2,1,0:T(8,128)(2,1)} %get-tuple-element.44.c0), channel_id=1, source_target_pairs={{0,64},{64,0},{128,192},{192,128},{1,65},{65,1},{129,193},{193,129... | collective-permute-start | bytes 1572872 | tf_op jit(solution)/shard_map/ppermute | solution.py:411
  52.3 12.9 %collective-permute-start.5 = (bf16[2,128,1024]{2,1,0:T(8,128)(2,1)}, bf16[2,128,1024]{2,1,0:T(8,128)(2,1)}, u32[]{:S(2)}, u32[]{:S(2)}) collective-permute-start(bf16[2,128,1024]{2,1,0:T(8,128)(2,1)} %collective-permute-done.4.c2), channel_id=1, source_target_pairs={{0,64},{64,0},{128,192},{192,128},{1,65},{65,1},{129,193},{193,129... | collective-permute-start | bytes 1572872 | tf_op jit(solution)/shard_map/ppermute | solution.py:413
  57.3 15.8 %copy-start.1 = (bf16[2,128,1024]{2,1,0:T(8,128)(2,1)}, bf16[2,128,1024]{2,1,0:T(8,128)(2,1)S(1)}, u32[]{:S(2)}) copy-start(bf16[2,128,1024]{2,1,0:T(8,128)(2,1)S(1)} %get-tuple-element.37.g) | copy-start | bytes 1572868
  57.3 15.8 %copy-start.2 = (bf16[2,128,1024]{2,1,0:T(8,128)(2,1)}, bf16[2,128,1024]{2,1,0:T(8,128)(2,1)S(1)}, u32[]{:S(2)}) copy-start(bf16[2,128,1024]{2,1,0:T(8,128)(2,1)S(1)} %collective-permute-done.6.__.c1) | copy-start | bytes 1572868
  73.2 7.5 %collective-permute-start.10 = (bf16[256,256]{1,0:T(8,128)(2,1)}, bf16[256,256]{1,0:T(8,128)(2,1)S(1)}, u32[]{:S(2)}, u32[]{:S(2)}) collective-permute-start(bf16[256,256]{1,0:T(8,128)(2,1)} %get-tuple-element.46.ot1), channel_id=1, source_target_pairs={{0,64},{64,0},{128,192},{192,128},{1,65},{65,1},{129,193},{193,129... | collective-permute-start | bytes 393224 | tf_op jit(solution)/shard_map/ppermute | solution.py:456
  75.3 5.4 %collective-permute-start.11 = (bf16[256,256]{1,0:T(8,128)(2,1)}, bf16[256,256]{1,0:T(8,128)(2,1)S(1)}, u32[]{:S(2)}, u32[]{:S(2)}) collective-permute-start(bf16[256,256]{1,0:T(8,128)(2,1)} %get-tuple-element.47.ot2), channel_id=1, source_target_pairs={{0,128},{64,192},{128,0},{192,64},{1,129},{65,193},{129,1},{193,65... | collective-permute-start | bytes 393224 | tf_op jit(solution)/shard_map/ppermute | solution.py:456
  75.3 8.3 %collective-permute-start.12 = (bf16[256,256]{1,0:T(8,128)(2,1)}, bf16[256,256]{1,0:T(8,128)(2,1)S(1)}, u32[]{:S(2)}, u32[]{:S(2)}) collective-permute-start(bf16[256,256]{1,0:T(8,128)(2,1)} %get-tuple-element.48.ot3), channel_id=1, source_target_pairs={{0,192},{64,128},{128,64},{192,0},{1,193},{65,129},{129,65},{193,1... | collective-permute-start | bytes 393224 | tf_op jit(solution)/shard_map/ppermute | solution.py:456
  77.0 22.1 %all-to-all-start.2 = ((bf16[16,32,1024]{2,1,0:T(8,128)(2,1)}), bf16[16,32,1024]{2,1,0:T(8,128)(2,1)S(1)}, u32[]{:S(2)}, u32[]{:S(2)}) async-start(bf16[16,32,1024]{2,1,0:T(8,128)(2,1)} %bitcast.52), calls=%async_computation.2 | async-start | bytes 2097152 | tf_op jit(solution)/shard_map/all_to_all | solution.py:327
  80.7 2.9 %copy-start.4 = (bf16[256,256]{1,0:T(8,128)(2,1)}, bf16[256,256]{1,0:T(8,128)(2,1)S(1)}, u32[]{:S(2)}) copy-start(bf16[256,256]{1,0:T(8,128)(2,1)S(1)} %collective-permute-done.10.ot1) | copy-start | bytes 393220
  80.7 2.8 %copy-start.5 = (bf16[256,256]{1,0:T(8,128)(2,1)}, bf16[256,256]{1,0:T(8,128)(2,1)S(1)}, u32[]{:S(2)}) copy-start(bf16[256,256]{1,0:T(8,128)(2,1)S(1)} %collective-permute-done.11.ot2) | copy-start | bytes 393220
  83.5 0.7 copy-start.6
  87.6 17.4 %collective-permute-start.13 = (bf16[128,512]{1,0:T(8,128)(2,1)S(1)}, bf16[128,512]{1,0:T(8,128)(2,1)S(1)}, u32[]{:S(2)}, u32[]{:S(2)}) collective-permute-start(bf16[128,512]{1,0:T(8,128)(2,1)S(1)} %get-tuple-element.55), channel_id=1, source_target_pairs={{0,3},{1,0},{2,1},{3,2},{4,7},{5,4},{6,5},{7,6},{8,11},{9,8},{10,9... | collective-permute-start | bytes 393224 | tf_op jit(solution)/shard_map/ppermute | solution.py:335
  91.5 21.8 %collective-permute-start.14 = (bf16[128,512]{1,0:T(8,128)(2,1)S(1)}, bf16[128,512]{1,0:T(8,128)(2,1)S(1)}, u32[]{:S(2)}, u32[]{:S(2)}) collective-permute-start(bf16[128,512]{1,0:T(8,128)(2,1)S(1)} %get-tuple-element.56), channel_id=1, source_target_pairs={{0,2},{1,3},{2,0},{3,1},{4,6},{5,7},{6,4},{7,5},{8,10},{9,11},{10,... | collective-permute-start | bytes 393224 | tf_op jit(solution)/shard_map/ppermute | solution.py:335
  92.5 24.3 %collective-permute-start.15 = (bf16[128,512]{1,0:T(8,128)(2,1)S(1)}, bf16[128,512]{1,0:T(8,128)(2,1)S(1)}, u32[]{:S(2)}, u32[]{:S(2)}) collective-permute-start(bf16[128,512]{1,0:T(8,128)(2,1)S(1)} %get-tuple-element.57), channel_id=1, source_target_pairs={{0,1},{1,2},{2,3},{3,0},{4,5},{5,6},{6,7},{7,4},{8,9},{9,10},{10,1... | collective-permute-start | bytes 393224 | tf_op jit(solution)/shard_map/ppermute | solution.py:335
  100.4 16.4 %collective-permute-start.7 = (bf16[128,512]{1,0:T(8,128)(2,1)S(1)}, bf16[128,512]{1,0:T(8,128)(2,1)S(1)}, u32[]{:S(2)}, u32[]{:S(2)}) collective-permute-start(bf16[128,512]{1,0:T(8,128)(2,1)S(1)} %get-tuple-element.51), channel_id=1, source_target_pairs={{0,3},{1,0},{2,1},{3,2},{4,7},{5,4},{6,5},{7,6},{8,11},{9,8},{10,9... | collective-permute-start | bytes 393224 | tf_op jit(solution)/shard_map/ppermute | solution.py:335
  104.1 12.7 %collective-permute-start.8 = (bf16[128,512]{1,0:T(8,128)(2,1)S(1)}, bf16[128,512]{1,0:T(8,128)(2,1)S(1)}, u32[]{:S(2)}, u32[]{:S(2)}) collective-permute-start(bf16[128,512]{1,0:T(8,128)(2,1)S(1)} %get-tuple-element.52), channel_id=1, source_target_pairs={{0,2},{1,3},{2,0},{3,1},{4,6},{5,7},{6,4},{7,5},{8,10},{9,11},{10,... | collective-permute-start | bytes 393224 | tf_op jit(solution)/shard_map/ppermute | solution.py:335
  105.0 14.3 %collective-permute-start.9 = (bf16[128,512]{1,0:T(8,128)(2,1)S(1)}, bf16[128,512]{1,0:T(8,128)(2,1)S(1)}, u32[]{:S(2)}, u32[]{:S(2)}) collective-permute-start(bf16[128,512]{1,0:T(8,128)(2,1)S(1)} %get-tuple-element.53), channel_id=1, source_target_pairs={{0,1},{1,2},{2,3},{3,0},{4,5},{5,6},{6,7},{7,4},{8,9},{9,10},{10,1... | collective-permute-start | bytes 393224 | tf_op jit(solution)/shard_map/ppermute | solution.py:335
  113.4 18.6 %collective-permute-start.16 = (bf16[2,128,1024]{2,1,0:T(8,128)(2,1)}, bf16[2,128,1024]{2,1,0:T(8,128)(2,1)S(1)}, u32[]{:S(2)}, u32[]{:S(2)}) collective-permute-start(bf16[2,128,1024]{2,1,0:T(8,128)(2,1)} %get-tuple-element.65), channel_id=1, source_target_pairs={{64,0},{128,64},{192,128},{65,1},{129,65},{193,129},{66,2},{130,66... | collective-permute-start | bytes 1572872 | tf_op jit(solution)/shard_map/ppermute | solution.py:509
  120.2 11.7 %all-to-all-start.3 = ((bf16[16,16,512]{2,1,0:T(8,128)(2,1)}), bf16[16,16,512]{2,1,0:T(8,128)(2,1)S(1)}, u32[]{:S(2)}, u32[]{:S(2)}) async-start(bf16[16,16,512]{2,1,0:T(8,128)(2,1)} %shard_map.127._), calls=%async_computation.3 | async-start | bytes 524288 | tf_op jit(solution)/shard_map/all_to_all | solution.py:327
  123.7 1.0 copy-start
